TPU v7x, 32 devices: a whole 2x2x4 slice. The times are simulated.
32 devices in a mesh: head: 4 (over x, core), seq: 8 (over z, y).
Axes of the slice: x: 2, y: 2, z: 4, core: 2. Of those that a mesh axis runs over, the one named last changes fastest.
Arguments:
- frames: bfloat16 [8, 2048, 1024], P('seq', 'head'), may hold values from -6 to 6
- time_embed: bfloat16 [8, 2, 1024], P('seq'), may hold values from -6 to 6
- segment_ids: int32 [8, 2048], P('seq', 'head'), may hold values from 0 to 1, as said below
- frame_mask: int32 [8, 2048], P('seq', 'head'), may hold values from 0 to 1, as said below
- positions: int32 [8, 2048], P('seq', 'head'), may hold values from 0 to 3582, as said below
- w_ada: bfloat16 [1024, 6144], P(('head', 'seq')), may hold values from -0.1875 to 0.1875
- b_ada: bfloat16 [6144], P(('head', 'seq')), may hold values from -3 to 3
- w_qkv: bfloat16 [1024, 3072], P(('head', 'seq')), may hold values from -0.1875 to 0.1875
- b_qkv: bfloat16 [3072], P(('head', 'seq')), may hold values from -2 to 2
- w_out: bfloat16 [1024, 1024], P(('head', 'seq')), may hold values from -2 to 2
- b_out: bfloat16 [1024], P(('head', 'seq')), may hold values from -2 to 2
- w_up: bfloat16 [1024, 2048], P(('head', 'seq')), may hold values from -0.1875 to 0.1875
- b_up: bfloat16 [2048], P(('head', 'seq')), may hold values from -2 to 2
- w_down: bfloat16 [2048, 1024], P(('head', 'seq')), may hold values from -0.25 to 0.25
- b_down: bfloat16 [1024], P(('head', 'seq')), may hold values from -2 to 2
- cotangent: bfloat16 [8, 2048, 1024], P('seq', 'head'), may hold values from -6 to 6
Outputs:
- out_frames: bfloat16 [8, 2048, 1024], P('seq', 'head')
- grad_frames: float32 [8, 2048, 1024], P('seq', 'head')
- grad_time: float32 [8, 2, 1024], P('seq')
- grad_w_ada: float32 [1024, 6144], P(('head', 'seq'))
- grad_b_ada: float32 [6144], P(('head', 'seq'))
- grad_w_qkv: float32 [1024, 3072], P(('head', 'seq'))
- grad_b_qkv: float32 [3072], P(('head', 'seq'))
- grad_w_out: float32 [1024, 1024], P(('head', 'seq'))
- grad_b_out: float32 [1024], P(('head', 'seq'))
- grad_w_up: float32 [1024, 2048], P(('head', 'seq'))
- grad_b_up: float32 [2048], P(('head', 'seq'))
- grad_w_down: float32 [2048, 1024], P(('head', 'seq'))
- grad_b_down: float32 [1024], P(('head', 'seq'))
Inputs may be any that keep to these rules, and one draw needn't show every extreme that they name: `segment_ids`: every row holds two utterances, segment 0 in one run of frames and then segment 1 to the row's end; the longer one has 1024 frames or more; padding frames lie at the end of the row, inside segment 1. `frame_mask`: in every row 1 for the frames before a run of 1 to 256 padding frames at its end, 0 on that run; each utterance keeps real frames. `positions`: 0 at the first frame of each utterance, then rising by 1 or 2 from one frame to the next within it.
All inputs are finite; a program needn't handle non-finite values.
Results may differ from a plain program's by a relative error of at most 0.017.
The roundings to bfloat16 on the way count: a program that leaves them out, or rounds other values in their place, can miss the bound.
Values may be sent and summed in bfloat16 or wider, within the bound.
A program may use at most 256 MiB of HBM per device.

v0:
```python
import jax
import jax.numpy as jnp
from jax import lax
from jax.sharding import PartitionSpec as P

HEAD_DIM = 64


norm_eps = 1e-06
masked_score = -1e30


def normalize(inputs):
    centre = jnp.mean(inputs, -1, keepdims=True)
    centred = inputs - centre
    spread = jnp.mean(centred * centred, -1, keepdims=True)
    return centred * lax.rsqrt(spread + norm_eps)


def modulate(inputs, shift_in, scale_in):
    return normalize(inputs) * (1.0 + scale_in) + shift_in


def rotary_angles(positions, model_width, head_size):
    column = lax.iota(jnp.int32, model_width)
    pair_index = (column % head_size // 2).astype(jnp.float32)
    inverse = 10000.0 ** (-(2.0 * pair_index) / head_size)
    return positions.astype(jnp.float32)[..., None] * inverse


def rotate(inputs, angles):
    column = lax.iota(jnp.int32, inputs.shape[-1])
    following = jnp.roll(inputs, -1, axis=-1)
    preceding = jnp.roll(inputs, 1, axis=-1)
    partner = jnp.where(column % 2 == 0, -following, preceding)
    return inputs * jnp.cos(angles) + partner * jnp.sin(angles)


def gelu_tanh(inputs):
    return jax.nn.gelu(inputs, approximate=True)


def block_scores(query_block, key_all, seg_query, seg_all, mask_all, first_row, head_size):
    block_rows = query_block.shape[0]
    total_frames = key_all.shape[0]
    head_count = query_block.shape[1] // head_size
    scores = jnp.einsum(
        "qhd,khd->hqk",
        query_block.reshape(block_rows, head_count, head_size),
        key_all.reshape(total_frames, head_count, head_size),
        preferred_element_type=jnp.float32,
    ) * head_size ** (-0.5)
    row_place = first_row + lax.iota(jnp.int32, block_rows)
    col_place = lax.iota(jnp.int32, total_frames)
    allowed = (seg_query[:, None] == seg_all[None, :]) & (mask_all[None, :] == 1) | (
        row_place[:, None] == col_place[None, :]
    )
    return (jnp.where(allowed[None], scores, masked_score), allowed)


def body(
    frames,
    time_embed,
    segment_ids,
    frame_mask,
    positions,
    w_ada,
    b_ada,
    w_qkv,
    b_qkv,
    w_out,
    b_out,
    w_up,
    b_up,
    w_down,
    b_down,
    cotangent,
):
    row_count, frame_count, model_width = frames.shape
    head_size = HEAD_DIM
    score_scale = head_size ** (-0.5)
    (
        full_ada,
        full_bada,
        full_qkv,
        full_bqkv,
        full_out,
        full_bout,
        full_up,
        full_bup,
        full_down,
        full_bdown,
    ) = (
        lax.all_gather(w_ada, ("head", "seq"), axis=0, tiled=True),
        lax.all_gather(b_ada, ("head", "seq"), axis=0, tiled=True),
        lax.all_gather(w_qkv, ("head", "seq"), axis=0, tiled=True),
        lax.all_gather(b_qkv, ("head", "seq"), axis=0, tiled=True),
        lax.all_gather(w_out, ("head", "seq"), axis=0, tiled=True),
        lax.all_gather(b_out, ("head", "seq"), axis=0, tiled=True),
        lax.all_gather(w_up, ("head", "seq"), axis=0, tiled=True),
        lax.all_gather(b_up, ("head", "seq"), axis=0, tiled=True),
        lax.all_gather(w_down, ("head", "seq"), axis=0, tiled=True),
        lax.all_gather(b_down, ("head", "seq"), axis=0, tiled=True),
    )
    time_value = time_embed.astype(jnp.float32)
    time_act, time_pull = jax.vjp(jax.nn.silu, time_value)
    time_low = time_act.astype(jnp.bfloat16)
    embedding = jnp.einsum(
        "rsd,de->rse", time_low, full_ada, preferred_element_type=jnp.float32
    ) + full_bada.astype(jnp.float32)
    seg_index = lax.iota(jnp.int32, time_embed.shape[1])
    member = (segment_ids[:, :, None] == seg_index[None, None, :]).astype(jnp.float32)
    modulation = jnp.einsum("rfs,rse->rfe", member, embedding, precision=lax.Precision.HIGHEST)
    shift_one, scale_one, gate_one, shift_two, scale_two, gate_two = jnp.split(
        modulation, 6, axis=2
    )
    source = frames.astype(jnp.float32)
    normed_one, norm_one_pull = jax.vjp(modulate, source, shift_one, scale_one)
    normed_one_low = normed_one.astype(jnp.bfloat16)
    projected = jnp.einsum(
        "rfd,de->rfe", normed_one_low, full_qkv, preferred_element_type=jnp.float32
    ) + full_bqkv.astype(jnp.float32)
    angles = rotary_angles(positions, model_width, head_size)
    query_rot, rotate_pull = jax.vjp(
        lambda inputs: rotate(inputs, angles), projected[:, :, :model_width]
    )
    key_rot = rotate(projected[:, :, model_width : 2 * model_width], angles)
    packed = jnp.stack((query_rot, key_rot, projected[:, :, 2 * model_width :]), axis=2).astype(
        jnp.bfloat16
    )
    head_side = lax.all_to_all(packed, "head", split_axis=3, concat_axis=1, tiled=True)
    seg_all, mask_all = (
        lax.all_gather(segment_ids, "head", axis=1, tiled=True),
        lax.all_gather(frame_mask, "head", axis=1, tiled=True),
    )
    total_frames = head_side.shape[1]
    local_width = head_side.shape[3]
    head_count = local_width // head_size
    block_rows = min(512, total_frames)
    starts = lax.iota(jnp.int32, total_frames // block_rows) * block_rows

    def attend_row(row_items):
        qkv_row, seg_row, mask_row = row_items
        query_all = qkv_row[:, 0]
        key_all = qkv_row[:, 1]
        value_heads = qkv_row[:, 2].reshape(total_frames, head_count, head_size)

        def one_block(first_row):
            query_block = lax.dynamic_slice_in_dim(query_all, first_row, block_rows, 0)
            seg_query = lax.dynamic_slice_in_dim(seg_row, first_row, block_rows, 0)
            scores, allowed = block_scores(
                query_block, key_all, seg_query, seg_row, mask_row, first_row, head_size
            )
            row_max = jnp.max(scores, axis=2, keepdims=True)
            exp_sum = jnp.sum(
                jnp.where(allowed[None], jnp.exp(scores - row_max), 0.0), axis=2, keepdims=True
            )
            log_total = row_max + jnp.log(exp_sum)
            probability = jnp.where(allowed[None], jnp.exp(scores - log_total), 0.0).astype(
                jnp.bfloat16
            )
            mixed_heads = jnp.einsum(
                "hqk,khd->qhd", probability, value_heads, preferred_element_type=jnp.float32
            )
            return (
                mixed_heads.reshape(block_rows, local_width).astype(jnp.bfloat16),
                log_total[:, :, 0],
            )

        mixed_blocks, total_blocks = lax.map(one_block, starts)
        return (mixed_blocks.reshape(total_frames, local_width), total_blocks)

    mixed_rows, log_totals = lax.map(attend_row, (head_side, seg_all, mask_all))
    attended = lax.all_to_all(mixed_rows, "head", split_axis=1, concat_axis=2, tiled=True)
    mask_local = frame_mask.astype(jnp.float32)[:, :, None]
    branch = (
        jnp.einsum("rfd,de->rfe", attended, full_out, preferred_element_type=jnp.float32)
        + full_bout.astype(jnp.float32)
    ) * mask_local
    middle = source + gate_one * branch
    normed_two, norm_two_pull = jax.vjp(modulate, middle, shift_two, scale_two)
    normed_two_low = normed_two.astype(jnp.bfloat16)
    hidden = jnp.einsum(
        "rfd,dh->rfh", normed_two_low, full_up, preferred_element_type=jnp.float32
    ) + full_bup.astype(jnp.float32)
    activated, gelu_pull = jax.vjp(gelu_tanh, hidden)
    activated_low = activated.astype(jnp.bfloat16)
    feed_out = jnp.einsum(
        "rfh,hd->rfd", activated_low, full_down, preferred_element_type=jnp.float32
    ) + full_bdown.astype(jnp.float32)
    out_frames = (middle + gate_two * feed_out).astype(jnp.bfloat16)
    back_ada, back_qkv, back_out, back_up, back_down = (
        lax.all_gather(w_ada, ("head", "seq"), axis=0, tiled=True),
        lax.all_gather(w_qkv, ("head", "seq"), axis=0, tiled=True),
        lax.all_gather(w_out, ("head", "seq"), axis=0, tiled=True),
        lax.all_gather(w_up, ("head", "seq"), axis=0, tiled=True),
        lax.all_gather(w_down, ("head", "seq"), axis=0, tiled=True),
    )
    upstream = cotangent.astype(jnp.float32)
    d_feed = (upstream * gate_two).astype(jnp.bfloat16)
    d_gate_two = upstream * feed_out
    grad_down = jnp.einsum("rfh,rfd->hd", activated_low, d_feed, preferred_element_type=jnp.float32)
    grad_bdown = jnp.sum(d_feed.astype(jnp.float32), axis=(0, 1))
    d_activated = jnp.einsum("rfd,hd->rfh", d_feed, back_down, preferred_element_type=jnp.float32)
    (d_hidden,) = gelu_pull(d_activated)
    d_hidden_low = d_hidden.astype(jnp.bfloat16)
    grad_up = jnp.einsum(
        "rfd,rfh->dh", normed_two_low, d_hidden_low, preferred_element_type=jnp.float32
    )
    grad_bup = jnp.sum(d_hidden_low.astype(jnp.float32), axis=(0, 1))
    d_normed_two = jnp.einsum(
        "rfh,dh->rfd", d_hidden_low, back_up, preferred_element_type=jnp.float32
    )
    d_middle_norm, d_shift_two, d_scale_two = norm_two_pull(d_normed_two)
    d_middle = upstream + d_middle_norm
    d_gate_one = d_middle * branch
    d_proj = (d_middle * gate_one * mask_local).astype(jnp.bfloat16)
    grad_out = jnp.einsum("rfd,rfe->de", attended, d_proj, preferred_element_type=jnp.float32)
    grad_bout = jnp.sum(d_proj.astype(jnp.float32), axis=(0, 1))
    d_attended = jnp.einsum(
        "rfe,de->rfd", d_proj, back_out, preferred_element_type=jnp.float32
    ).astype(jnp.bfloat16)
    grad_heads = lax.all_to_all(d_attended, "head", split_axis=2, concat_axis=1, tiled=True)

    def attend_back(row_items):
        qkv_row, grad_row, total_row, seg_row, mask_row = row_items
        query_all = qkv_row[:, 0]
        key_all = qkv_row[:, 1]
        key_heads = key_all.reshape(total_frames, head_count, head_size)
        value_heads = qkv_row[:, 2].reshape(total_frames, head_count, head_size)

        def one_block(running, block_items):
            key_grad, value_grad = running
            first_row, log_total = block_items
            query_block = lax.dynamic_slice_in_dim(query_all, first_row, block_rows, 0)
            seg_query = lax.dynamic_slice_in_dim(seg_row, first_row, block_rows, 0)
            scores, allowed = block_scores(
                query_block, key_all, seg_query, seg_row, mask_row, first_row, head_size
            )
            probability = jnp.where(allowed[None], jnp.exp(scores - log_total[:, :, None]), 0.0)
            grad_block = lax.dynamic_slice_in_dim(grad_row, first_row, block_rows, 0).reshape(
                block_rows, head_count, head_size
            )
            prob_grad = jnp.einsum(
                "qhd,khd->hqk", grad_block, value_heads, preferred_element_type=jnp.float32
            )
            row_dot = jnp.sum(probability * prob_grad, axis=2, keepdims=True)
            score_grad = (probability * (prob_grad - row_dot)).astype(jnp.bfloat16)
            query_grad = (
                jnp.einsum(
                    "hqk,khd->qhd", score_grad, key_heads, preferred_element_type=jnp.float32
                )
                * score_scale
            )
            query_heads = query_block.reshape(block_rows, head_count, head_size)
            key_grad = (
                key_grad
                + jnp.einsum(
                    "hqk,qhd->khd", score_grad, query_heads, preferred_element_type=jnp.float32
                )
                * score_scale
            )
            value_grad = value_grad + jnp.einsum(
                "hqk,qhd->khd",
                probability.astype(jnp.bfloat16),
                grad_block,
                preferred_element_type=jnp.float32,
            )
            return ((key_grad, value_grad), query_grad.reshape(block_rows, local_width))

        zero_heads = jnp.zeros((total_frames, head_count, head_size), jnp.float32)
        (key_grad, value_grad), query_blocks = lax.scan(
            one_block, (zero_heads, zero_heads), (starts, total_row)
        )
        stacked = jnp.stack(
            (
                query_blocks.reshape(total_frames, local_width),
                key_grad.reshape(total_frames, local_width),
                value_grad.reshape(total_frames, local_width),
            ),
            axis=1,
        )
        return stacked.astype(jnp.bfloat16)

    qkv_grads = lax.map(attend_back, (head_side, grad_heads, log_totals, seg_all, mask_all))
    frame_grads = lax.all_to_all(qkv_grads, "head", split_axis=1, concat_axis=3, tiled=True)
    (query_raw_grad,) = rotate_pull(frame_grads[:, :, 0].astype(jnp.float32))
    (key_raw_grad,) = rotate_pull(frame_grads[:, :, 1].astype(jnp.float32))
    d_projected = jnp.concatenate(
        (query_raw_grad, key_raw_grad, frame_grads[:, :, 2].astype(jnp.float32)), axis=2
    ).astype(jnp.bfloat16)
    grad_qkv = jnp.einsum(
        "rfd,rfe->de", normed_one_low, d_projected, preferred_element_type=jnp.float32
    )
    grad_bqkv = jnp.sum(d_projected.astype(jnp.float32), axis=(0, 1))
    d_normed_one = jnp.einsum(
        "rfe,de->rfd", d_projected, back_qkv, preferred_element_type=jnp.float32
    )
    d_source_norm, d_shift_one, d_scale_one = norm_one_pull(d_normed_one)
    grad_frames = d_middle + d_source_norm
    d_modulation = jnp.concatenate(
        (d_shift_one, d_scale_one, d_gate_one, d_shift_two, d_scale_two, d_gate_two), axis=2
    )
    emb_part = jnp.einsum("rfs,rfe->rse", member, d_modulation, precision=lax.Precision.HIGHEST)
    emb_share = lax.psum_scatter(
        emb_part.astype(jnp.bfloat16), "head", scatter_dimension=2, tiled=True
    )
    emb_grad_low = lax.all_gather(emb_share, "head", axis=2, tiled=True)
    d_time_act = jnp.einsum(
        "rse,de->rsd", emb_grad_low, back_ada, preferred_element_type=jnp.float32
    )
    (grad_time,) = time_pull(d_time_act)
    leader = (lax.axis_index("head") == 0).astype(jnp.float32)
    grad_ada = (
        jnp.einsum("rsd,rse->de", time_low, emb_grad_low, preferred_element_type=jnp.float32)
        * leader
    )
    grad_bada = jnp.sum(emb_grad_low.astype(jnp.float32), axis=(0, 1)) * leader
    (
        shard_ada,
        shard_bada,
        shard_qkv,
        shard_bqkv,
        shard_out,
        shard_bout,
        shard_up,
        shard_bup,
        shard_down,
        shard_bdown,
    ) = (
        lax.psum_scatter(grad_ada, ("head", "seq"), scatter_dimension=0, tiled=True),
        lax.psum_scatter(grad_bada, ("head", "seq"), scatter_dimension=0, tiled=True),
        lax.psum_scatter(grad_qkv, ("head", "seq"), scatter_dimension=0, tiled=True),
        lax.psum_scatter(grad_bqkv, ("head", "seq"), scatter_dimension=0, tiled=True),
        lax.psum_scatter(grad_out, ("head", "seq"), scatter_dimension=0, tiled=True),
        lax.psum_scatter(grad_bout, ("head", "seq"), scatter_dimension=0, tiled=True),
        lax.psum_scatter(grad_up, ("head", "seq"), scatter_dimension=0, tiled=True),
        lax.psum_scatter(grad_bup, ("head", "seq"), scatter_dimension=0, tiled=True),
        lax.psum_scatter(grad_down, ("head", "seq"), scatter_dimension=0, tiled=True),
        lax.psum_scatter(grad_bdown, ("head", "seq"), scatter_dimension=0, tiled=True),
    )
    return (
        out_frames,
        grad_frames,
        grad_time,
        shard_ada,
        shard_bada,
        shard_qkv,
        shard_bqkv,
        shard_out,
        shard_bout,
        shard_up,
        shard_bup,
        shard_down,
        shard_bdown,
    )


def solution(mesh):
    in_specs = (
        P("seq", "head", None),
        P("seq", None, None),
        P("seq", "head"),
        P("seq", "head"),
        P("seq", "head"),
        P(("head", "seq"), None),
        P(("head", "seq")),
        P(("head", "seq"), None),
        P(("head", "seq")),
        P(("head", "seq"), None),
        P(("head", "seq")),
        P(("head", "seq"), None),
        P(("head", "seq")),
        P(("head", "seq"), None),
        P(("head", "seq")),
        P("seq", "head", None),
    )
    out_specs = (
        P("seq", "head", None),
        P("seq", "head", None),
        P("seq", None, None),
        P(("head", "seq"), None),
        P(("head", "seq")),
        P(("head", "seq"), None),
        P(("head", "seq")),
        P(("head", "seq"), None),
        P(("head", "seq")),
        P(("head", "seq"), None),
        P(("head", "seq")),
        P(("head", "seq"), None),
        P(("head", "seq")),
    )
    return jax.shard_map(body, mesh=mesh, in_specs=in_specs, out_specs=out_specs, check_vma=False)
```

profile of v0, /device:TPU:0, one launch (start us, length us, event | category | flops | bytes accessed | tf_op | source)
XLA Modules:
  0.0 1869.1 jit_solution(877220399513312636)
XLA Ops:
  14.2 43.8 %all-reduce.19 = (bf16[6144]{0:T(1024)(128)(2,1)S(1)}, bf16[3072]{0:T(1024)(128)(2,1)S(1)}, bf16[1024]{0:T(1024)(128)(2,1)}, bf16[2048]{0:T(1024)(128)(2,1)}, bf16[1024]{0:T(1024)(128)(2,1)}) all-reduce(bf16[6144]{0:T(1024)(128)(2,1)S(1)} %dynamic-update-slice, ...), channel_id=1, replica_groups=mesh['head'=4,'seq'=8] {'head','seq'}, use_global_device_ids=true, to_apply=%add.8 | all-reduce | flops 13312 | bytes 53248
  60.8 49.8 %all-gather.6.cloned.1.call-done = bf16[1024,6144]{1,0:T(8,128)(2,1)} async-done(((bf16[32,6144]{1,0:T(8,128)(2,1)}), bf16[1024,6144]{1,0:T(8,128)(2,1)}) %all-gather.6.cloned.1.call-update) | async-done | bytes 12582928 | tf_op jit(solution)/shard_map/all_gather | solution.py:94
  127.1 54.1 %all-gather.8.cloned.1.call-done = bf16[1024,3072]{1,0:T(8,128)(2,1)} async-done(((bf16[32,3072]{1,0:T(8,128)(2,1)}), bf16[1024,3072]{1,0:T(8,128)(2,1)}) %all-gather.8.cloned.1.call-update) | async-done | bytes 6291472 | tf_op jit(solution)/shard_map/all_gather | solution.py:96
  188.8 9.6 fusion.94
  210.3 53.1 %all_gather.46 = s32[1,2048]{1,0:T(1,128)S(1)} all-gather(s32[1,512]{1,0:T(1,128)S(1)} %copy-done.38), channel_id=1, replica_groups=mesh['head'=4,'seq'=8] {'head'}, dimensions={1}, use_global_device_ids=true | all-gather | bytes 10240 | tf_op jit(solution)/shard_map/all_gather | solution.py:133
  282.3 86.2 %while.45 = (s32[]{:T(128)}, bf16[4,512,256]{2,1,0:T(8,128)(2,1)S(1)}, f32[4,4,512]{2,1,0:T(4,128)}, s32[4]{0:T(128)}, s32[2048]{0:T(1024)S(1)}, /*index=5*/s32[...) while((s32[]{:T(128)}, ...), condition=%wide.region_5.6_spmd, body=%wide.region_2.5_spmd.sunk | while | flops 1132593664 | bytes 58817204 | solution.py:170
  373.2 11.6 reduce.10
  392.8 14.4 all-to-all-done.1
  433.2 9.3 convert_reduce_fusion.1
  482.6 14.4 all-to-all-done.2
  503.3 279.0 %while.46 = (s32[]{:T(128)}, f32[2048,4,64]{0,2,1:T(8,128)}, f32[2048,4,64]{0,2,1:T(8,128)}, bf16[4,512,256]{2,1,0:T(8,128)(2,1)}, s32[4]{0:T(128)}, /*index=5*/...) while((s32[]{:T(128)}, f32[2048,4,64]{0,2,1:T(8,128)}, ...), condition=%wide.region_12.13_spmd.clone, body=%wide.region_10.12_spmd.clone.sunk | while | flops 2733376000 | bytes 263003056 | solution.py:272
  511.8 9.5 fusion.212
  524.4 10.9 multiply_reduce_fusion.4
  541.1 9.3 multiply_convert_fusion.7
  581.0 9.5 fusion.212
  593.6 10.9 multiply_reduce_fusion.4
  610.3 9.3 multiply_convert_fusion.7
  650.8 9.5 fusion.212
  663.3 10.9 multiply_reduce_fusion.4
  680.1 9.3 multiply_convert_fusion.7
  720.5 9.5 fusion.212
  733.1 10.9 multiply_reduce_fusion.4
  749.8 9.3 multiply_convert_fusion.7
  788.5 16.0 copy.82
  804.5 50.7 %all_to_all.63 = bf16[1,2048,3,256]{3,2,0,1:T(4,128)(2,1)S(1)} all-to-all(bf16[1,2048,3,256]{3,2,0,1:T(4,128)(2,1)S(1)} %copy.82), channel_id=1, replica_groups=mesh['head'=4,'seq'=8] {'head'}, dimensions={1} | all-to-all | bytes 6291456 | tf_op jit(solution)/shard_map/all_to_all | solution.py:286
  941.8 10.4 broadcast_multiply_fusion
  954.0 41.1 %all-reduce.18 = (f32[6144]{0:T(1024)S(1)}, f32[3072]{0:T(1024)S(1)}, f32[1024]{0:T(1024)S(1)}, f32[2048]{0:T(1024)S(1)}, f32[1024]{0:T(1024)S(1)}) all-reduce(f32[6144]{0:T(1024)S(1)} %broadcast_multiply_fusion.1, f32[3072]{0:T(1024)S(1)} %convert_reduce_fusion, ...), channel_id=4, replica_groups=mesh['head'=4,'seq'=8] {'head','seq'}, use_global_device_ids=true, to_apply=%region_18.19.clone | all-reduce | flops 13312 | bytes 106496
  1006.7 70.3 %reduce-scatter.13.cloned.1.call-done = f32[32,1024]{1,0:T(8,128)} async-done(((f32[1024,1024]{1,0:T(8,128)}), f32[32,1024]{1,0:T(8,128)}) %reduce-scatter.13.cloned.1.call-update) | async-done | bytes 131088 | tf_op jit(solution)/shard_map/reduce_scatter | solution.py:335
  1077.0 184.1 %reduce-scatter.15.cloned.1.call-done = f32[32,2048]{1,0:T(8,128)} async-done(((f32[1024,2048]{1,0:T(8,128)}), f32[32,2048]{1,0:T(8,128)}) %reduce-scatter.15.cloned.1.call-update) | async-done | bytes 262160 | tf_op jit(solution)/shard_map/reduce_scatter | solution.py:337
  1261.1 186.9 %reduce-scatter.17.cloned.1.call-done = f32[64,1024]{1,0:T(8,128)} async-done(((f32[2048,1024]{1,0:T(8,128)}), f32[64,1024]{1,0:T(8,128)}) %reduce-scatter.17.cloned.1.call-update) | async-done | bytes 262160 | tf_op jit(solution)/shard_map/reduce_scatter | solution.py:339
  1448.0 162.5 %reduce-scatter.11.cloned.1.call-done = f32[32,3072]{1,0:T(8,128)} async-done(((f32[1024,3072]{1,0:T(8,128)}), f32[32,3072]{1,0:T(8,128)}) %reduce-scatter.11.cloned.1.call-update) | async-done | bytes 393232 | tf_op jit(solution)/shard_map/reduce_scatter | solution.py:333
  1610.5 251.5 %reduce-scatter.9.cloned.1.call-done = f32[32,6144]{1,0:T(8,128)} async-done(((f32[1024,6144]{1,0:T(8,128)}), f32[32,6144]{1,0:T(8,128)}) %reduce-scatter.9.cloned.1.call-update) | async-done | bytes 786448 | tf_op jit(solution)/shard_map/reduce_scatter | solution.py:331
  (435 shorter events, 484.5 us)
Async XLA Ops:
  7.2 53.1 %copy-start.10 = (bf16[1,512,1024]{2,1,0:T(8,128)(2,1)S(1)}, bf16[1,512,1024]{2,1,0:T(8,128)(2,1)}, u32[]{:S(2)}) copy-start(bf16[1,512,1024]{2,1,0:T(8,128)(2,1)} %param.20) | copy-start | bytes 3145732
  7.2 103.3 %copy-start.44 = (bf16[1,2,1024]{2,1,0:T(2,128)(2,1)S(1)}, bf16[1,2,1024]{2,1,0:T(2,128)(2,1)}, u32[]{:S(2)}) copy-start(bf16[1,2,1024]{2,1,0:T(2,128)(2,1)} %param.21) | copy-start | bytes 12292
  7.2 103.3 %all-gather.6.cloned.1.call-start = ((), (), s32[]{:S(2)}) async-start(), calls=%async_computation.10 | async-start | bytes 12976128 | tf_op jit(solution)/shard_map/all_gather | solution.py:94
  7.9 173.3 %all-gather.8.cloned.1.call-start = ((), (), s32[]{:S(2)}) async-start(), calls=%async_computation.11 | async-start | bytes 6488064 | tf_op jit(solution)/shard_map/all_gather | solution.py:96
  8.7 404.6 %all-gather.10.cloned.1.call-start = ((), (), s32[]{:S(2)}) async-start(), calls=%async_computation.12 | async-start | bytes 2162688 | tf_op jit(solution)/shard_map/all_gather | solution.py:98
  9.4 416.9 %all-gather.12.cloned.1.call-start = ((), (), s32[]{:S(2)}) async-start(), calls=%async_computation.13 | async-start | bytes 4325376 | tf_op jit(solution)/shard_map/all_gather | solution.py:100
  58.8 130.0 %copy-start.50 = (f32[1,512]{1,0:T(1,128)}, f32[1,512]{1,0:T(1,128)S(1)}, u32[]{:S(2)}) copy-start(f32[1,512]{1,0:T(1,128)S(1)} %convert_element_type.223) | copy-start | bytes 6148
  58.8 130.0 %copy-start.68 = (pred[1024]{0:T(1024)(128)(4,1)}, pred[1024]{0:T(1024)(128)(4,1)S(1)}, u32[]{:S(2)}) copy-start(pred[1024]{0:T(1024)(128)(4,1)S(1)} %fusion.114) | copy-start | bytes 3076
  58.8 130.0 %copy-start.40 = (f32[1024]{0:T(1024)}, f32[1024]{0:T(1024)S(1)}, u32[]{:S(2)}) copy-start(f32[1024]{0:T(1024)S(1)} %fusion.113) | copy-start | bytes 12292
  60.3 61.7 %copy-start.48 = (f32[512]{0:T(512)}, f32[512]{0:T(512)S(1)}, u32[]{:S(2)}) copy-start(f32[512]{0:T(512)S(1)} %broadcast_multiply_fusion.3) | copy-start | bytes 6148
  60.7 56.1 %copy-start.54 = (f32[512]{0:T(512)}, f32[512]{0:T(512)S(1)}, u32[]{:S(2)}) copy-start(f32[512]{0:T(512)S(1)} %fusion.67) | copy-start | bytes 6148
  60.7 61.2 %copy-start.56 = (f32[512]{0:T(512)}, f32[512]{0:T(512)S(1)}, u32[]{:S(2)}) copy-start(f32[512]{0:T(512)S(1)} %fusion.126) | copy-start | bytes 6148
  60.7 56.1 %copy-start.38 = (s32[1,512]{1,0:T(1,128)S(1)}, s32[1,512]{1,0:T(1,128)}, u32[]{:S(2)}) copy-start(s32[1,512]{1,0:T(1,128)} %param.22) | copy-start | bytes 6148
  127.0 59.7 %copy-start.27 = (bf16[512,1024]{1,0:T(8,128)(2,1)}, bf16[512,1024]{1,0:T(8,128)(2,1)S(1)}, u32[]{:S(2)}) copy-start(bf16[512,1024]{1,0:T(8,128)(2,1)S(1)} %fusion.83) | copy-start | bytes 3145732
  204.6 58.8 %copy-start.64 = (s32[1,512]{1,0:T(1,128)S(1)}, s32[1,512]{1,0:T(1,128)}, u32[]{:S(2)}) copy-start(s32[1,512]{1,0:T(1,128)} %param.23) | copy-start | bytes 6148
  204.6 64.9 %all-to-all-start = ((bf16[1,512,3,1024]{1,2,0,3:T(4,128)(2,1)}), bf16[1,512,3,1024]{1,2,0,3:T(4,128)(2,1)}, u32[]{:S(2)}, u32[]{:S(2)}) async-start(bf16[1,512,3,1024]{1,2,0,3:T(4,128)(2,1)} %copy.71), calls=%async_computation | async-start | bytes 8388608 | tf_op jit(solution)/shard_map/all_to_all | solution.py:131
  209.7 223.5 %all-gather.14.cloned.1.call-start = ((), (), s32[]{:S(2)}) async-start(), calls=%async_computation.14 | async-start | bytes 4325376 | tf_op jit(solution)/shard_map/all_gather | solution.py:102
  388.4 18.8 %all-to-all-start.1 = ((bf16[4,2,65536]{2,1,0:T(2,128)(2,1)}), bf16[4,2,65536]{2,1,0:T(2,128)(2,1)}, u32[]{:S(2)}, u32[]{:S(2)}) async-start(bf16[4,2,65536]{2,1,0:T(2,128)(2,1)} %reshape.1484), calls=%async_computation.1 | async-start | bytes 2097152 | tf_op jit(solution)/shard_map/all_to_all | solution.py:174
  392.7 62.3 %copy-start.36 = (f32[1,512]{1,0:T(1,128)}, f32[1,512]{1,0:T(1,128)S(1)}, u32[]{:S(2)}) copy-start(f32[1,512]{1,0:T(1,128)S(1)} %convert_element_type.227) | copy-start | bytes 6148
  392.7 20.6 %copy-start.42 = (f32[1024]{0:T(1024)}, f32[1024]{0:T(1024)S(1)}, u32[]{:S(2)}) copy-start(f32[1024]{0:T(1024)S(1)} %convert_element_type.226) | copy-start | bytes 12292
  392.8 54.9 %copy-start.65 = (f32[2048]{0:T(1024)}, f32[2048]{0:T(1024)S(1)}, u32[]{:S(2)}) copy-start(f32[2048]{0:T(1024)S(1)} %convert_element_type.229) | copy-start | bytes 24580
  392.8 54.9 %copy-start.62 = (f32[1024]{0:T(1024)}, f32[1024]{0:T(1024)S(1)}, u32[]{:S(2)}) copy-start(f32[1024]{0:T(1024)S(1)} %convert_element_type.231) | copy-start | bytes 12292
  418.9 28.9 %copy-start.8 = (f32[1,512,1024]{2,1,0:T(8,128)}, f32[1,512,1024]{2,1,0:T(8,128)S(1)}, u32[]{:S(2)}) copy-start(f32[1,512,1024]{2,1,0:T(8,128)S(1)} %get-tuple-element.300) | copy-start | bytes 6291460
  418.9 28.9 %copy-start.46 = (f32[512]{0:T(512)}, f32[512]{0:T(512)S(1)}, u32[]{:S(2)}) copy-start(f32[512]{0:T(512)S(1)} %broadcast_multiply_fusion.2) | copy-start | bytes 6148
  420.8 26.9 %copy-start.52 = (f32[512]{0:T(512)}, f32[512]{0:T(512)S(1)}, u32[]{:S(2)}) copy-start(f32[512]{0:T(512)S(1)} %fusion.127) | copy-start | bytes 6148
  478.3 18.8 %all-to-all-start.2 = ((bf16[4,2,65536]{2,1,0:T(2,128)(2,1)}), bf16[4,2,65536]{2,1,0:T(2,128)(2,1)}, u32[]{:S(2)}, u32[]{:S(2)}) async-start(bf16[4,2,65536]{2,1,0:T(2,128)(2,1)} %reshape.1486), calls=%async_computation.2 | async-start | bytes 2097152 | tf_op jit(solution)/shard_map/all_to_all | solution.py:223
  482.5 452.2 %reduce-scatter.19.cloned.1.call-start = ((), (), s32[]{:S(2)}) async-start(), calls=%async_computation.20 | async-start | bytes 1966080
  902.1 174.9 %reduce-scatter.13.cloned.1.call-start = ((), (), s32[]{:S(2)}) async-start(), calls=%async_computation.17 | async-start | bytes 4325376 | tf_op jit(solution)/shard_map/reduce_scatter | solution.py:335
  907.0 354.1 %reduce-scatter.15.cloned.1.call-start = ((), (), s32[]{:S(2)}) async-start(), calls=%async_computation.18 | async-start | bytes 8650752 | tf_op jit(solution)/shard_map/reduce_scatter | solution.py:337
  914.8 533.2 %reduce-scatter.17.cloned.1.call-start = ((), (), s32[]{:S(2)}) async-start(), calls=%async_computation.19 | async-start | bytes 8650752 | tf_op jit(solution)/shard_map/reduce_scatter | solution.py:339
  924.7 685.8 %reduce-scatter.11.cloned.1.call-start = ((), (), s32[]{:S(2)}) async-start(), calls=%async_computation.16 | async-start | bytes 12976128 | tf_op jit(solution)/shard_map/reduce_scatter | solution.py:333
  934.6 927.4 %reduce-scatter.9.cloned.1.call-start = ((), (), s32[]{:S(2)}) async-start(), calls=%async_computation.15 | async-start | bytes 25952256 | tf_op jit(solution)/shard_map/reduce_scatter | solution.py:331
  (78 other events, 355.1 us)
Sparse Core Ops, SparseCore 0:
  10.9 99.5 all-gather.5
  113.4 67.7 all-gather.7
  184.2 58.0 all-gather.9
  245.2 60.9 all-gather.11
  309.1 60.6 all-gather.13
  902.2 27.1 reduce-scatter.18
  932.4 144.6 reduce-scatter.12
  1080.0 181.0 reduce-scatter.14
  1264.1 183.8 reduce-scatter.16
  1455.5 154.9 reduce-scatter.10
  1617.5 244.4 reduce-scatter.8
where the time goes:
time: 1880 us; the launch traced here: 1870 us
  waiting for transfers between devices  991 us (53%)
  matrix products  300 us (16%)
  blocking collectives  200 us (11%)
  local copies, waits for them, and re-layouts  178 us (9%)
  other arithmetic  154 us (8%)
    reduce_scatter x1, waiting for transfers between devices, body(): lax.psum_scatter(grad_ada, ('head', 'seq'), scatter_dimension=0, tiled=True)  252 us
    reduce_scatter x1, waiting for transfers between devices, body(): lax.psum_scatter(grad_down, ('head', 'seq'), scatter_dimension=0, tiled=T...  187 us
    reduce_scatter x1, waiting for transfers between devices, body(): lax.psum_scatter(grad_up, ('head', 'seq'), scatter_dimension=0, tiled=True)  184 us
    reduce_scatter x1, waiting for transfers between devices, body(): lax.psum_scatter(grad_qkv, ('head', 'seq'), scatter_dimension=0, tiled=True)  163 us
    unnamed x2, blocking collectives  85 us
    reduce_scatter x1, waiting for transfers between devices, body(): lax.psum_scatter(grad_out, ('head', 'seq'), scatter_dimension=0, tiled=True)  70.3 us
    dot_general x8, matrix products, block_scores(): jnp.einsum('qhd,khd->hqk', query_block.reshape(block_rows, head_count, he...  56.7 us
    all_gather x1, waiting for transfers between devices, body(): lax.all_gather(w_qkv, ('head', 'seq'), axis=0, tiled=True)  54.1 us
  transfers between devices with their start and end apart: 14, of which 9 were waited for; matrix products, arithmetic and copies ran while one was open for 12% of the time, Pallas kernels for 0%

commit v1 on v0

v1 whole, which is shorter than its diff:
```python
import functools
import math

import jax
import jax.numpy as jnp
from jax import lax
from jax.experimental import pallas as pl
from jax.experimental.pallas import tpu as pltpu
from jax.sharding import PartitionSpec as P

HD=64
LOG2E=math.log2(math.e)
NEG=-1e30
bf=jnp.bfloat16; f32=jnp.float32
NT=(((1,),(1,)),((),()))
NN=(((1,),(0,)),((),()))
def dot(a,b,dims=NN): return lax.dot_general(a,b,dims,preferred_element_type=f32)

def fwd_kernel(lo_ref,hi_ref,qkv_ref,auxq_ref,auxk_ref,o_ref,lse_ref,k2,vx,q2,s_scr,m_scr,acc,*,T,nh):
    qt=pl.program_id(0)
    W=nh*HD
    L=qkv_ref.shape[0]
    nk=L//T
    lane=lax.broadcasted_iota(jnp.int32,(T,128),1)
    @pl.when(qt==0)
    def _():
        @pl.loop(0,nk)
        def _(t):
            r=pl.ds(pl.multiple_of(t*T,T),T)
            for h in range(nh):
                k=qkv_ref[r,W+h*HD:W+(h+1)*HD]
                k2[h,t]=jnp.concatenate([k,k],axis=1)
                v=qkv_ref[r,2*W+h*HD:2*W+(h+1)*HD]
                one=jnp.where(lax.broadcasted_iota(jnp.int32,(T,HD),1)==0,1.0,0.0).astype(bf)
                vx[h,t]=jnp.concatenate([v,one],axis=1)
    lo=lo_ref[qt]; hi=hi_ref[qt]
    r=pl.ds(pl.multiple_of(qt*T,T),T)
    for h in range(nh):
        q=qkv_ref[r,h*HD:(h+1)*HD].astype(f32)*(HD**-0.5*LOG2E)
        qh=q.astype(bf)
        ql=(q-qh.astype(f32)).astype(bf)
        q2[h]=jnp.concatenate([qh,ql],axis=1)
    auxq=auxq_ref[r,:]
    eye=lax.broadcasted_iota(jnp.int32,(T,T),0)==lax.broadcasted_iota(jnp.int32,(T,T),1)
    def mx(s):
        m=s[:,:128]
        for j in range(1,T//128): m=jnp.maximum(m,s[:,j*128:(j+1)*128])
        return m
    ak=auxk_ref[r,:]
    for h in range(nh):
        raw=dot(q2[h],k2[h,qt],NT)
        s=dot(jnp.concatenate([q2[h],auxq],axis=1),jnp.concatenate([k2[h,qt],ak],axis=1),NT)
        s=jnp.where(eye,raw,s)
        s_scr[h,qt]=s
        m_scr[h]=mx(s)
    @pl.loop(lo,hi-1)
    def _(t):
        kt=jnp.where(t>=qt,t+1,t)
        ak=auxk_ref[pl.ds(pl.multiple_of(kt*T,T),T),:]
        for h in range(nh):
            s=dot(jnp.concatenate([q2[h],auxq],axis=1),jnp.concatenate([k2[h,kt],ak],axis=1),NT)
            s_scr[h,kt]=s
            m_scr[h]=jnp.maximum(m_scr[h],mx(s))
    for h in range(nh):
        m_scr[h]=jnp.broadcast_to(jnp.max(m_scr[h],axis=1,keepdims=True),(T,128))
        acc[h]=jnp.zeros((T,128),f32)
    @pl.loop(lo,hi)
    def _(kt):
        for h in range(nh):
            s=s_scr[h,kt]; m=m_scr[h]
            p=jnp.exp2(s-jnp.concatenate([m]*(T//128),axis=1)).astype(bf)
            acc[h]+=dot(p,vx[h,kt])
    lse=jnp.zeros((T,128),f32)
    for h in range(nh):
        a=acc[h]
        l=a[:,HD:HD+1]
        o_ref[:,h*HD:(h+1)*HD]=(a[:,:HD]/l).astype(bf)
        lse=jnp.where(lane==h,m_scr[h]+jnp.log2(l),lse)
    lse_ref[...]=lse

def attn_fwd(qkv,lo,hi,auxq,auxk,T):
    L,W3=qkv.shape; W=W3//3; nh=W//HD; nk=L//T
    return pl.pallas_call(
        functools.partial(fwd_kernel,T=T,nh=nh),
        out_shape=(jax.ShapeDtypeStruct((L,W),bf),jax.ShapeDtypeStruct((L,128),f32)),
        grid_spec=pltpu.PrefetchScalarGridSpec(num_scalar_prefetch=2,grid=(nk,),
            in_specs=[pl.BlockSpec((L,W3),lambda i,*_:(0,0)),pl.BlockSpec((L,128),lambda i,*_:(0,0)),pl.BlockSpec((L,128),lambda i,*_:(0,0))],
            out_specs=[pl.BlockSpec((T,W),lambda i,*_:(i,0)),pl.BlockSpec((T,128),lambda i,*_:(i,0))],
            scratch_shapes=[pltpu.VMEM((nh,nk,T,128),bf),pltpu.VMEM((nh,nk,T,128),bf),pltpu.VMEM((nh,T,128),bf),
                pltpu.VMEM((nh,nk,T,T),f32),pltpu.VMEM((nh,T,128),f32),pltpu.VMEM((nh,T,128),f32)]),
        compiler_params=pltpu.CompilerParams(vmem_limit_bytes=60*2**20),
        name="attn_fwd",
    )(lo,hi,qkv,auxq,auxk)

def bwd_kernel(lo_ref,hi_ref,qkv_ref,o_ref,do_ref,lse_ref,auxq_ref,auxk_ref,dqkv_ref,q2,qa,k2,dox,vx,kT,dqT,dk,dv,*,T,nh):
    kt=pl.program_id(0)
    W=nh*HD
    L=qkv_ref.shape[0]
    nk=L//T
    lane=lax.broadcasted_iota(jnp.int32,(T,128),1)
    lane64=lax.broadcasted_iota(jnp.int32,(T,HD),1)
    @pl.when(kt==0)
    def _():
        dqT[...]=jnp.zeros_like(dqT)
        @pl.loop(0,nk)
        def _(t):
            r=pl.ds(pl.multiple_of(t*T,T),T)
            lse=lse_ref[r,:]
            aq=auxq_ref[r,:].astype(f32)
            kT[t]=qkv_ref[r,W:2*W].T
            for h in range(nh):
                q=qkv_ref[r,h*HD:(h+1)*HD].astype(f32)*(HD**-0.5*LOG2E)
                qh=q.astype(bf)
                ql=(q-qh.astype(f32)).astype(bf)
                q2[h,t]=jnp.concatenate([qh,ql],axis=1)
                k=qkv_ref[r,W+h*HD:W+(h+1)*HD]
                k2[h,t]=jnp.concatenate([k,k],axis=1)
                v=qkv_ref[r,2*W+h*HD:2*W+(h+1)*HD]
                vx[h,t]=jnp.concatenate([v,jnp.where(lane64<2,1.0,0.0).astype(bf)],axis=1)
                nl=-lse[:,h:h+1]
                l1=nl.astype(bf).astype(f32); l2=(nl-l1).astype(bf).astype(f32); l3=nl-l1-l2
                qa[h,t]=jnp.where(lane==0,l1,jnp.where(lane==1,l2,jnp.where(lane==2,l3,aq))).astype(bf)
                do=do_ref[r,h*HD:(h+1)*HD]
                nd=-jnp.sum(do.astype(f32)*o_ref[r,h*HD:(h+1)*HD].astype(f32),axis=1,keepdims=True)
                d1=nd.astype(bf).astype(f32); d2=nd-d1
                dox[h,t]=jnp.concatenate([do,jnp.where(lane64==0,d1,jnp.where(lane64==1,d2,0.0)).astype(bf)],axis=1)
    r=pl.ds(pl.multiple_of(kt*T,T),T)
    ak=auxk_ref[r,:]
    lo=lo_ref[kt]; hi=hi_ref[kt]
    def tile(qt,diag):
        rq=pl.ds(pl.multiple_of(qt*T,T),T)
        for h in range(nh):
            kx=jnp.concatenate([k2[h,kt],ak],axis=1)
            s=dot(kx,jnp.concatenate([q2[h,qt],qa[h,qt]],axis=1),NT)
            if diag:
                eye=lax.broadcasted_iota(jnp.int32,(T,T),0)==lax.broadcasted_iota(jnp.int32,(T,T),1)
                qr=jnp.where(lane<3,qa[h,qt].astype(f32),0.0).astype(bf)
                raw=dot(kx,jnp.concatenate([q2[h,qt],qr],axis=1),NT)
                s=jnp.where(eye,raw,s)
            p=jnp.exp2(s)
            dp=dot(vx[h,kt],dox[h,qt],NT)
            ds=(p*dp).astype(bf)
            pb=p.astype(bf)
            g=h//2
            rv=dot(pb,do_ref[rq,g*128:(g+1)*128])
            rk=dot(ds,qkv_ref[rq,g*128:(g+1)*128])
            dv[h]+=rv
            dk[h]+=rk
            dqT[qt,h*HD:(h+1)*HD,:]+=dot(kT[kt,h*HD:(h+1)*HD,:],ds)
    dk[...]=jnp.zeros_like(dk); dv[...]=jnp.zeros_like(dv)
    tile(kt,True)
    @pl.loop(lo,hi-1)
    def _(t):
        tile(jnp.where(t>=kt,t+1,t),False)
    for g in range(nh//2):
        dqkv_ref[r,W+g*128:W+(g+1)*128]=(jnp.where(lane<HD,dk[2*g],dk[2*g+1])*HD**-0.5).astype(bf)
        dqkv_ref[r,2*W+g*128:2*W+(g+1)*128]=jnp.where(lane<HD,dv[2*g],dv[2*g+1]).astype(bf)
    @pl.when(kt==nk-1)
    def _():
        @pl.loop(0,nk)
        def _(t):
            dqkv_ref[pl.ds(pl.multiple_of(t*T,T),T),0:W]=(dqT[t].T*HD**-0.5).astype(bf)

def attn_bwd(qkv,o,do,lse,lo,hi,auxq,auxk,T):
    L,W3=qkv.shape; W=W3//3; nh=W//HD; nk=L//T
    full=lambda w: pl.BlockSpec((L,w),lambda i,*_:(0,0))
    return pl.pallas_call(
        functools.partial(bwd_kernel,T=T,nh=nh),
        out_shape=jax.ShapeDtypeStruct((L,W3),bf),
        grid_spec=pltpu.PrefetchScalarGridSpec(num_scalar_prefetch=2,grid=(nk,),
            in_specs=[full(W3),full(W),full(W),full(128),full(128),full(128)],
            out_specs=full(W3),
            scratch_shapes=[pltpu.VMEM((nh,nk,T,128),bf)]*5+[pltpu.VMEM((nk,W,T),bf),pltpu.VMEM((nk,W,T),f32),
                pltpu.VMEM((nh,T,128),f32),pltpu.VMEM((nh,T,128),f32)]),
        compiler_params=pltpu.CompilerParams(vmem_limit_bytes=60*2**20),
        name="attn_bwd",
    )(lo,hi,qkv,o,do,lse,auxq,auxk)

def tables(seg,mask,T):
    L=seg.shape[0]; nk=L//T
    s=seg.reshape(nk,T); m=mask.reshape(nk,T)
    has=jnp.stack([jnp.any(s==c,axis=1) for c in (0,1)],1)
    real=jnp.stack([jnp.any((s==c)&(m==1),axis=1) for c in (0,1)],1)
    use=jnp.any(has[:,None,:]&real[None,:,:],axis=2)|jnp.eye(nk,dtype=bool)
    idx=jnp.arange(nk,dtype=jnp.int32)
    qlo=jnp.min(jnp.where(use,idx[None,:],nk),axis=1); qhi=jnp.max(jnp.where(use,idx[None,:],-1),axis=1)+1
    klo=jnp.min(jnp.where(use,idx[:,None],nk),axis=0); khi=jnp.max(jnp.where(use,idx[:,None],-1),axis=0)+1
    return [a.astype(jnp.int32) for a in (qlo,qhi,klo,khi)]
def aux(seg,mask):
    L=seg.shape[0]
    lane=lax.broadcasted_iota(jnp.int32,(L,128),1)
    sg=seg[:,None]; pad=(mask==0)[:,None]
    aq=jnp.where(lane==3,jnp.where(sg!=0,NEG,0.),jnp.where(lane==4,jnp.where(sg!=1,NEG,0.),jnp.where(lane==5,NEG,0.))).astype(bf)
    ak=jnp.where(lane<3,1.,jnp.where(lane==3,(sg==0).astype(f32),jnp.where(lane==4,(sg==1).astype(f32),jnp.where(lane==5,pad.astype(f32),0.)))).astype(bf)
    return aq,ak

bf=jnp.bfloat16; f32=jnp.float32
EPS=1e-6
NN=(((1,),(0,)),((),()))
NT=(((1,),(1,)),((),()))
TN=(((0,),(0,)),((),()))
def dot(a,b,dims=NN): return lax.dot_general(a,b,dims,preferred_element_type=f32)
V=pl.BlockSpec(memory_space=pltpu.VMEM)

def moments(x):
    c=jnp.mean(x,-1,keepdims=True)
    xc=x-c
    rs=lax.rsqrt(jnp.mean(xc*xc,-1,keepdims=True)+EPS)
    return xc*rs, rs
def pick(seg,emb,i,D):
    return jnp.where(seg==0,emb[0:1,i*D:(i+1)*D],emb[1:2,i*D:(i+1)*D])
def sums(x,seg):
    a=jnp.sum(jnp.where(seg==0,x,0.0),0,keepdims=True); b=jnp.sum(jnp.where(seg==1,x,0.0),0,keepdims=True)
    return a,b
def partner(v):
    w=v.shape[1]
    lane=lax.broadcasted_iota(jnp.int32,v.shape,1)
    return jnp.where(lane%2==0,pltpu.roll(v,w-1,1),pltpu.roll(v,1,1))
def gelu_both(v):
    c=math.sqrt(2/math.pi)
    v2=v*v
    t=jnp.tanh(c*v*(1.0+0.044715*v2))
    h=0.5*(1.0+t)
    return v*h, h+0.5*v*(1.0-t*t)*(c*(1.0+3*0.044715*v2))

def qkv_kernel(x_ref,seg_ref,emb_ref,w_ref,b_ref,cos_ref,sin_ref,n_ref,p_ref,*,R,nd,W):
    F,D=x_ref.shape
    @pl.loop(0,F//R)
    def _(i):
        r=pl.ds(pl.multiple_of(i*R,R),R)
        seg=seg_ref[r,:]
        n,_=moments(x_ref[r,:].astype(f32))
        y=(n*(1.0+pick(seg,emb_ref,1,D))+pick(seg,emb_ref,0,D)).astype(bf)
        n_ref[r,:]=y
        cos=jnp.concatenate([cos_ref[r,:]]*(W//128),1); sin=jnp.concatenate([sin_ref[r,:]]*(W//128),1)
        for d in range(nd):
            for j in range(3):
                c=(d*3+j)*W
                v=dot(y,w_ref[:,c:c+W])+b_ref[0:1,c:c+W]
                if j<2: v=v*cos+partner(v)*sin
                p_ref[d,r,j*W:(j+1)*W]=v.astype(bf)

def qkv_proj(x,seg,emb,w,b,cos,sin,nd,R=128):
    F,D=x.shape; W=D//nd
    return pl.pallas_call(functools.partial(qkv_kernel,R=R,nd=nd,W=W),
        out_shape=(jax.ShapeDtypeStruct((F,D),bf),jax.ShapeDtypeStruct((nd,F,3*W),bf)),
        in_specs=[V]*7,out_specs=(V,V),
        compiler_params=pltpu.CompilerParams(vmem_limit_bytes=60*2**20),name="qkv_proj",
        cost_estimate=pl.CostEstimate(flops=2*F*D*3*D,bytes_accessed=14*2**20,transcendentals=0))(x,seg,emb,w,b,cos,sin)

def mid_kernel(x_ref,a_ref,c_ref,seg_ref,msk_ref,emb_ref,wo_ref,bo_ref,wu_ref,bu_ref,wd_ref,bd_ref,
               out_ref,dm_ref,da_ref,go_ref,gu_ref,gd_ref,gb_ref,ge_ref,
               n2s,acts,dhs,dfs,dps,dgelu,*,R):
    F,D=x_ref.shape; H=wu_ref.shape[1]; CH=512
    gb_ref[...]=jnp.zeros_like(gb_ref); ge_ref[...]=jnp.zeros_like(ge_ref)
    @pl.loop(0,F//R)
    def _(i):
        r=pl.ds(pl.multiple_of(i*R,R),R)
        seg=seg_ref[r,:]; msk=msk_ref[r,:]
        def acc(k,x):
            a,b=sums(x,seg)
            ge_ref[0:1,k*D:(k+1)*D]+=a; ge_ref[1:2,k*D:(k+1)*D]+=b
        branch=(dot(a_ref[r,:],wo_ref[...])+bo_ref[0:1,:])*msk
        g1=pick(seg,emb_ref,2,D)
        middle=x_ref[r,:].astype(f32)+g1*branch
        n,rs=moments(middle)
        sc2=1.0+pick(seg,emb_ref,4,D)
        n2=(n*sc2+pick(seg,emb_ref,3,D)).astype(bf)
        n2s[r,:]=n2
        feed=jnp.broadcast_to(bd_ref[0:1,:],(R,D))
        for j in range(H//CH):
            c=slice(j*CH,(j+1)*CH)
            h=dot(n2,wu_ref[:,c])+bu_ref[0:1,c]
            a,g=gelu_both(h)
            a=a.astype(bf)
            acts[r,c]=a; dgelu[:,c]=g
            feed+=dot(a,wd_ref[c,:])
        up=c_ref[r,:].astype(f32)
        g2=pick(seg,emb_ref,5,D)
        out_ref[r,:]=(middle+g2*feed).astype(bf)
        df=(up*g2).astype(bf)
        dfs[r,:]=df
        acc(3,up*feed)
        gb_ref[2:3,0:D]+=jnp.sum(df.astype(f32),0,keepdims=True)
        dn=jnp.zeros((R,D),f32)
        for j in range(H//CH):
            c=slice(j*CH,(j+1)*CH)
            dh=(dot(df,wd_ref[c,:],NT)*dgelu[:,c]).astype(bf)
            dhs[r,c]=dh
            gb_ref[1:2,c]+=jnp.sum(dh.astype(f32),0,keepdims=True)
            dn+=dot(dh,wu_ref[:,c],NT)
        acc(1,dn); acc(2,dn*n)
        dn=dn*sc2
        dmid=up+(dn-jnp.mean(dn,-1,keepdims=True)-n*jnp.mean(dn*n,-1,keepdims=True))*rs
        dm_ref[r,:]=dmid
        acc(0,dmid*branch)
        dp=(dmid*g1*msk).astype(bf)
        dps[r,:]=dp
        gb_ref[0:1,0:D]+=jnp.sum(dp.astype(f32),0,keepdims=True)
        da_ref[r,:]=dot(dp,wo_ref[...],NT).astype(bf)
    @pl.loop(0,D//256)
    def _(i):
        c=pl.ds(pl.multiple_of(i*256,256),256)
        go_ref[c,:]=dot(a_ref[:,c],dps[...],TN).astype(bf)
        gu_ref[c,:]=dot(n2s[:,c],dhs[...],TN).astype(bf)
    @pl.loop(0,H//256)
    def _(i):
        c=pl.ds(pl.multiple_of(i*256,256),256)
        gd_ref[c,:]=dot(acts[:,c],dfs[...],TN).astype(bf)

def mid(x,a,c,seg,msk,emb,wo,bo,wu,bu,wd,bd,R=128):
    F,D=x.shape; H=wu.shape[1]
    S=jax.ShapeDtypeStruct
    return pl.pallas_call(functools.partial(mid_kernel,R=R),
        out_shape=(S((F,D),bf),S((F,D),f32),S((F,D),bf),S((D,D),bf),S((D,H),bf),S((H,D),bf),S((8,H),f32),S((8,4*D),f32)),
        in_specs=[V]*12,out_specs=(V,)*8,
        scratch_shapes=[pltpu.VMEM((F,D),bf),pltpu.VMEM((F,H),bf),pltpu.VMEM((F,H),bf),pltpu.VMEM((F,D),bf),pltpu.VMEM((F,D),bf),pltpu.VMEM((R,H),f32)],
        compiler_params=pltpu.CompilerParams(vmem_limit_bytes=62*2**20),name="mid",
        cost_estimate=pl.CostEstimate(flops=6*F*D*(D+2*H),bytes_accessed=30*2**20,transcendentals=F*H))(x,a,c,seg,msk,emb,wo,bo,wu,bu,wd,bd)

def tail_kernel(x_ref,n1_ref,dm_ref,g_ref,seg_ref,emb_ref,w_ref,cos_ref,sin_ref,gf_ref,gw_ref,gb_ref,ge_ref,dps,*,R,nd,W):
    F,D=x_ref.shape
    gb_ref[...]=jnp.zeros_like(gb_ref); ge_ref[...]=jnp.zeros_like(ge_ref)
    @pl.loop(0,F//R)
    def _(i):
        r=pl.ds(pl.multiple_of(i*R,R),R)
        seg=seg_ref[r,:]
        cos=jnp.concatenate([cos_ref[r,:]]*(W//128),1); sin=jnp.concatenate([sin_ref[r,:]]*(W//128),1)
        dn=jnp.zeros((R,D),f32)
        for d in range(nd):
            for j in range(3):
                c=(d*3+j)*W
                v=g_ref[d,r,j*W:(j+1)*W]
                if j<2:
                    v=v.astype(f32)
                    v=(v*cos-partner(v)*sin).astype(bf)
                dps[r,c:c+W]=v
                gb_ref[0:1,c:c+W]+=jnp.sum(v.astype(f32),0,keepdims=True)
        for j in range(3*D//512):
            dn+=dot(dps[r,j*512:(j+1)*512],w_ref[:,j*512:(j+1)*512],NT)
        n,rs=moments(x_ref[r,:].astype(f32))
        for k,x in ((0,dn),(1,dn*n)):
            a,b=sums(x,seg)
            ge_ref[0:1,k*D:(k+1)*D]+=a; ge_ref[1:2,k*D:(k+1)*D]+=b
        dn=dn*(1.0+pick(seg,emb_ref,1,D))
        gf_ref[r,:]=dm_ref[r,:]+(dn-jnp.mean(dn,-1,keepdims=True)-n*jnp.mean(dn*n,-1,keepdims=True))*rs
    @pl.loop(0,D//256)
    def _(i):
        c=pl.ds(pl.multiple_of(i*256,256),256)
        for j in range(3):
            gw_ref[c,j*D:(j+1)*D]=dot(n1_ref[:,c],dps[:,j*D:(j+1)*D],TN).astype(bf)

def tail(x,n1,dm,g,seg,emb,w,cos,sin,R=128):
    F,D=x.shape; nd=g.shape[0]; W=D//nd
    S=jax.ShapeDtypeStruct
    return pl.pallas_call(functools.partial(tail_kernel,R=R,nd=nd,W=W),
        out_shape=(S((F,D),f32),S((D,3*D),bf),S((8,3*D),f32),S((8,2*D),f32)),
        in_specs=[V]*9,out_specs=(V,)*4,
        scratch_shapes=[pltpu.VMEM((F,3*D),bf)],
        compiler_params=pltpu.CompilerParams(vmem_limit_bytes=60*2**20),name="tail",
        cost_estimate=pl.CostEstimate(flops=4*F*D*3*D,bytes_accessed=20*2**20,transcendentals=0))(x,n1,dm,g,seg,emb,w,cos,sin)

HS=("head","seq")

def body(frames,time_embed,segment_ids,frame_mask,positions,w_ada,b_ada,w_qkv,b_qkv,w_out,b_out,w_up,b_up,w_down,b_down,cotangent):
    _,F,D=frames.shape
    nd=lax.axis_size("head"); ns=lax.axis_size("seq"); dev=lax.axis_index("head")*ns+lax.axis_index("seq")
    W=D//nd
    E=b_ada.shape[0]; E6=w_ada.shape[1]; K=w_ada.shape[0]
    x=frames[0]; cot=cotangent[0]; seg=segment_ids[0]; msk=frame_mask[0]
    def reorder(w): return w.reshape(-1,3,nd,W).transpose(0,2,1,3).reshape(-1,3*D)
    def restore(w): return w.reshape(-1,nd,3,W).transpose(0,2,1,3).reshape(-1,3*D)
    g=lambda w: lax.all_gather(w,HS,axis=0,tiled=True)
    wq=g(reorder(w_qkv))
    bias=g(jnp.concatenate([b_qkv,b_out,b_up,b_down])[None,:]).astype(f32)
    n0,n1,n2,n3=b_qkv.shape[0],b_out.shape[0],b_up.shape[0],b_down.shape[0]
    bq=reorder(bias[:,:n0].reshape(1,-1))
    bo=bias[:,n0:n0+n1].reshape(1,-1); bu=bias[:,n0+n1:n0+n1+n2].reshape(1,-1); bd=bias[:,n0+n1+n2:].reshape(1,-1)
    wo=g(w_out); wu=g(w_up); wd=g(w_down)
    time_all=lax.all_gather(time_embed,"seq",axis=0,tiled=True).astype(f32)
    act_all=jax.nn.silu(time_all).astype(bf)
    act_own=lax.dynamic_slice_in_dim(act_all,dev*K,K,2)
    part=jnp.einsum("rsd,de->rse",act_own,w_ada,preferred_element_type=f32)
    part=part+lax.dynamic_update_slice(jnp.zeros((E6,),f32),b_ada.astype(f32),(dev*E,))
    emb=lax.psum(lax.psum_scatter(part,"seq",scatter_dimension=0,tiled=True),"head")[0]
    column=lax.iota(jnp.int32,128)
    pair=(column%HD//2).astype(f32)
    angles=positions[0].astype(f32)[:,None]*(10000.0**(-(2.0*pair)/HD))
    cos=jnp.cos(angles); sin=jnp.where(column%2==0,-jnp.sin(angles),jnp.sin(angles))
    segc=seg[:,None]; mskc=msk.astype(f32)[:,None]
    normed,packed=qkv_proj(x,segc,emb,wq,bq,cos,sin,nd)
    qkv=lax.all_to_all(packed,"head",split_axis=0,concat_axis=0,tiled=True).reshape(nd*F,3*W)
    seg_row=lax.all_gather(seg,"head",axis=0,tiled=True); msk_row=lax.all_gather(msk,"head",axis=0,tiled=True)
    T=256
    qlo,qhi,klo,khi=tables(seg_row,msk_row,T)
    aq,ak=aux(seg_row,msk_row)
    o,lse=attn_fwd(qkv,qlo,qhi,aq,ak,T)
    def back(a):
        return lax.all_to_all(a.reshape(nd,F,-1),"head",split_axis=0,concat_axis=0,tiled=True)
    att=back(o).transpose(1,0,2).reshape(F,D)
    out,dmid,datt,gout,gup,gdown,gb,ge=mid(x,att,cot,segc,mskc,emb,wo,bo,wu,bu,wd,bd)
    do=lax.all_to_all(datt.reshape(F,nd,W).transpose(1,0,2),"head",split_axis=0,concat_axis=0,tiled=True).reshape(nd*F,W)
    dqkv=attn_bwd(qkv,o,do,lse,klo,khi,aq,ak,T)
    gx,gqkv,gbq,ge1=tail(x,normed,dmid,back(dqkv),segc,emb,wq,cos,sin)
    rs=lambda w: lax.psum_scatter(w,HS,scatter_dimension=0,tiled=True).astype(f32)
    demb=lax.psum(jnp.concatenate([ge1[:2],ge[:2]],axis=1),"head").astype(bf)
    demb_all=lax.all_gather(demb[None],"seq",axis=0,tiled=True)
    gada=jnp.einsum("rsd,rse->de",act_own,demb_all,preferred_element_type=f32)
    gbada=jnp.sum(lax.dynamic_slice_in_dim(demb_all,dev*E,E,2).astype(f32),(0,1))
    dact=jnp.einsum("rse,de->rsd",demb_all,w_ada,preferred_element_type=f32)
    dact=lax.all_to_all(dact,"seq",split_axis=0,concat_axis=0,tiled=True)
    dact=lax.all_gather(dact,"head",axis=0,tiled=True).transpose(1,0,2).reshape(2,D)
    _,pull=jax.vjp(jax.nn.silu,time_embed[0].astype(f32))
    gtime=pull(dact)[0][None]
    gbias=jnp.concatenate([restore(gbq[0:1]).reshape(-1,n0),gb[0,:D].reshape(-1,n1),gb[1].reshape(-1,n2),gb[2,:D].reshape(-1,n3)],axis=1)
    gbias=lax.psum_scatter(gbias,HS,scatter_dimension=0,tiled=True)[0]
    return (out[None],gx[None],gtime,gada,gbada,restore(rs(gqkv)),gbias[:n0],rs(gout),gbias[n0:n0+n1],rs(gup),gbias[n0+n1:n0+n1+n2],rs(gdown),gbias[n0+n1+n2:])


def solution(mesh):
    row=P("seq","head",None); ids=P("seq","head"); mat=P(HS,None); vec=P(HS); tim=P("seq",None,None)
    in_specs=(row,tim,ids,ids,ids)+(mat,vec)*5+(row,)
    out_specs=(row,row,tim)+(mat,vec)*5
    return jax.shard_map(body,mesh=mesh,in_specs=in_specs,out_specs=out_specs,check_vma=False)
```

time: 1880 us -> 905 us (0.48)
  waiting for transfers between devices: 991 us -> 379 us
  matrix products: 300 us -> 1.76 us
  Pallas kernels: 0 us -> 185 us
  local copies, waits for them, and re-layouts: 178 us -> 23.3 us
  other arithmetic: 154 us -> 13.6 us
  blocking collectives: 200 us -> 269 us
    reduce_scatter x5 -> x4, waiting for transfers between devices: 855 us -> 272 us  [body(): lax.psum_scatter(w, HS, scatter_dimension=0, tiled=True).astype(f32)]
    dot_general x45 -> x3, matrix products: 300 us -> 1.76 us  [the longest x1 1.27 us: body(): jnp.einsum('rsd,rse->de', act_own, demb_all, preferred_element_type=f32)]
    pallas_call x0 -> x5, Pallas kernels: none -> 185 us  [the longest x1 68.1 us: attn_bwd(): pl.pallas_call(functools.partial(bwd_kernel, T=T, nh=nh), out_shape=jax.S...]
    all_gather x3 -> x5, blocking collectives: 63.9 us -> 122 us  [the longest x1 41.5 us: body(): msk_row = lax.all_gather(msk, 'head', axis=0, tiled=True)]
    all_gather x5 -> x4, waiting for transfers between devices: 104 us -> 51.1 us  [body(): g = lambda w: lax.all_gather(w, HS, axis=0, tiled=True)]
    unnamed x171 -> x27, local copies, waits for them, and re-layouts: 48.4 us -> 2.46 us
    reduce_sum x12 -> x1, other arithmetic: 34.1 us -> 0.66 us  [body(): jnp.sum(lax.dynamic_slice_in_dim(demb_all, dev * E, E, 2).astype(f32), (0...]
    convert_element_type x11 -> x8, other arithmetic: 38 us -> 7.53 us  [the longest x3 4.75 us: body(): lax.psum_scatter(w, HS, scatter_dimension=0, tiled=True).astype(f32)]
  transfers between devices with their start and end apart: 14 -> 13, of which waited for: 9 -> 7; matrix products, arithmetic and copies ran while one was open for 12% -> 4% of each run, Pallas kernels for 0% -> 16%
where the time goes in v1:
time: 905 us; the launch traced here: 904 us
  waiting for transfers between devices  379 us (42%)
  blocking collectives  269 us (30%)
  Pallas kernels  185 us (20%)
  local copies, waits for them, and re-layouts  23.3 us (3%)
  between operations  16 us (2%)
  starting transfers between devices  15.8 us (2%)
  other arithmetic  13.6 us (2%)
    reduce_scatter x4, waiting for transfers between devices, body(): lax.psum_scatter(w, HS, scatter_dimension=0, tiled=True).astype(f32)  272 us
    unnamed x2, blocking collectives  81.7 us
    pallas_call x1, Pallas kernels, attn_bwd(): pl.pallas_call(functools.partial(bwd_kernel, T=T, nh=nh), out_shape=jax.S...  68.1 us
    all_gather x4, waiting for transfers between devices, body(): g = lambda w: lax.all_gather(w, HS, axis=0, tiled=True)  51.1 us
    pallas_call x1, Pallas kernels, mid(): pl.pallas_call(functools.partial(mid_kernel, R=R), out_shape=(S((F, D), b...  44.5 us
    all_to_all x1, blocking collectives, back(): lax.all_to_all(a.reshape(nd, F, -1), 'head', split_axis=0, concat_axis=0,...  42.3 us
    all_gather x1, blocking collectives, body(): msk_row = lax.all_gather(msk, 'head', axis=0, tiled=True)  41.5 us
    pallas_call x1, Pallas kernels, attn_fwd(): pl.pallas_call(functools.partial(fwd_kernel, T=T, nh=nh), out_shape=(jax....  40 us
  transfers between devices with their start and end apart: 13, of which 7 were waited for; matrix products, arithmetic and copies ran while one was open for 4% of the time, Pallas kernels for 16%

profile of v1, /device:TPU:0, one launch (start us, length us, event | category | flops | bytes accessed | tf_op | source)
XLA Modules:
  0.0 903.6 jit_solution(1230783527306355844)
XLA Ops:
  8.2 32.5 %all_gather.32 = bf16[8,2,1024]{2,1,0:T(2,128)(2,1)S(1)} all-gather(bf16[1,2,1024]{2,1,0:T(2,128)(2,1)} %param.17), channel_id=1, replica_groups=mesh['head'=4,'seq'=8] {'seq'}, dimensions={0}, use_global_device_ids=true | all-gather | bytes 36864 | tf_op jit(solution)/shard_map/all_gather | solution.py:380
  47.2 40.0 %all-reduce = bf16[7168]{0:T(1024)(128)(2,1)S(1)} all-reduce(bf16[7168]{0:T(1024)(128)(2,1)S(1)} %dynamic-update-slice), channel_id=4, replica_groups=mesh['head'=4,'seq'=8] {'head','seq'}, use_global_device_ids=true, to_apply=%add | all-reduce | flops 7168 | bytes 28672
  89.5 5.4 all-gather
  94.9 1.8 negate_select_fusion
  96.8 27.5 %all-reduce.5.cloned.1.call-done = f32[8,2,6144]{2,1,0:T(2,128)} async-done(((f32[8,2,6144]{2,1,0:T(2,128)}), f32[8,2,6144]{2,1,0:T(2,128)}) %all-reduce.5.cloned.1.call-update) | async-done | bytes 393232
  124.2 1.4 dynamic-slice_bitcast_fusion
  125.7 11.5 %psum.14.emb_ref = f32[2,6144]{1,0:T(2,128)} all-reduce(f32[2,6144]{1,0:T(2,128)S(1)} %dynamic-slice_bitcast_fusion), channel_id=1, replica_groups=mesh['head'=4,'seq'=8] {'head'}, use_global_device_ids=true, to_apply=%region_8.9 | all-reduce | flops 12288 | bytes 98304 | tf_op jit(solution)/shard_map/psum | solution.py:385
  137.2 10.7 %qkv_proj.1 = (bf16[512,1024]{1,0:T(8,128)(2,1)}, bf16[4,512,768]{2,1,0:T(8,128)(2,1)}) custom-call(bf16[512,1024]{1,0:T(8,128)(2,1)} %bitcast.83, s32[512,1]{1,0:T(8,128)} %copy.127.seg_ref, f32[2,6144]{1,0:T(2,128)} %psum.14.emb_ref, bf16[1024,3072]{1,0:T(8,128)(2,1)} %all-gather.10.cloned.1.call-done.w_ref, f32[1,3072]{1,0:T(1,128)} %reshape.160.b_ref, ...), custom_call_target="tpu_custom_call" | custom-call | flops 3221225472 | bytes 14680064 | tf_op jit(solution)/shard_map/qkv_proj/pallas_call | solution.py:245
  147.9 4.8 all-to-all-start
  152.9 41.5 %all-gather.1 = s32[1,2048]{1,0:T(1,128)S(1)} all-gather(s32[1,512]{1,0:T(1,128)S(1)} %copy-done.5), channel_id=3, replica_groups=mesh['head'=4,'seq'=8] {'head'}, dimensions={1}, use_global_device_ids=true | all-gather | bytes 10240 | tf_op jit(solution)/shard_map/all_gather | solution.py:393
  195.9 2.7 select_convert_fusion
  198.6 40.0 %attn_fwd.1 = (bf16[2048,256]{1,0:T(8,128)(2,1)}, f32[2048,128]{1,0:T(8,128)}) custom-call(s32[8]{0:T(128)} %get-tuple-element.56.lo_ref, s32[8]{0:T(128)} %broadcast_add_fusion.1.hi_ref, bf16[2048,768]{1,0:T(8,128)(2,1)} %bitcast.11.qkv_ref, bf16[2048,128]{1,0:T(8,128)(2,1)} %get-tuple-element.70.auxq_ref, bf16[2048,128]{1,0:T(8,128)(2,1)} %get-tuple-element.69.auxk_ref), custom_call_target="tpu_custom_call" | custom-call | tf_op jit(solution)/shard_map/attn_fwd/pallas_call | solution.py:83
  238.6 3.5 all-to-all-start.1
  245.3 11.2 %all-to-all-done.1 = bf16[4,512,256]{2,1,0:T(8,128)(2,1)S(1)} async-done(((bf16[4,512,256]{2,1,0:T(8,128)(2,1)}), bf16[4,512,256]{2,1,0:T(8,128)(2,1)S(1)}, u32[]{:S(2)}, u32[]{:S(2)}) %all-to-all-start.1) | async-done | bytes 1048608 | tf_op jit(solution)/shard_map/all_to_all | solution.py:399
  257.7 51.1 %all-gather.16.cloned.1.call-done.wd_ref = bf16[2048,1024]{1,0:T(8,128)(2,1)} async-done(((bf16[64,1024]{1,0:T(8,128)(2,1)}), bf16[2048,1024]{1,0:T(8,128)(2,1)}) %all-gather.16.cloned.1.call-update) | async-done | bytes 4194320 | tf_op jit(solution)/shard_map/all_gather | solution.py:373
  308.7 44.5 %mid.1 = (bf16[512,1024]{1,0:T(8,128)(2,1)}, f32[512,1024]{1,0:T(8,128)}, bf16[512,1024]{1,0:T(8,128)(2,1)}, bf16[1024,1024]{1,0:T(8,128)(2,1)}, bf16[1024,2048]...) custom-call(bf16[512,1024]{1,0:T(8,128)(2,1)} %bitcast.84, ...), custom_call_target="tpu_custom_call" | custom-call | flops 16106127360 | bytes 31457280 | tf_op jit(solution)/shard_map/mid/pallas_call | solution.py:314
  356.3 3.5 all-to-all-start.2
  360.4 13.9 %all-to-all-done.2 = bf16[4,512,256]{2,1,0:T(8,128)(2,1)S(1)} async-done(((bf16[4,512,256]{2,1,0:T(8,128)(2,1)}), bf16[4,512,256]{2,1,0:T(8,128)(2,1)S(1)}, u32[]{:S(2)}, u32[]{:S(2)}) %all-to-all-start.2) | async-done | bytes 1048608 | tf_op jit(solution)/shard_map/all_to_all | solution.py:402
  375.2 68.1 %attn_bwd.1 = bf16[2048,768]{1,0:T(8,128)(2,1)} custom-call(s32[8]{0:T(128)} %get-tuple-element.55.lo_ref, s32[8]{0:T(128)} %broadcast_add_fusion.hi_ref, bf16[2048,768]{1,0:T(8,128)(2,1)} %bitcast.11.qkv_ref, bf16[2048,256]{1,0:T(8,128)(2,1)} %get-tuple-element.30.o_ref, bf16[2048,256]{1,0:T(8,128)(2,1)} %bitcast.62, ...), custom_call_target="tpu_custom_call" | custom-call | tf_op jit(solution)/shard_map/attn_bwd/pallas_call | solution.py:167
  443.3 42.3 %all_to_all.25.g_ref = bf16[4,512,768]{2,1,0:T(8,128)(2,1)} all-to-all(bf16[4,512,768]{2,1,0:T(8,128)(2,1)} %bitcast.59), channel_id=1, replica_groups=mesh['head'=4,'seq'=8] {'head'}, dimensions={0} | all-to-all | bytes 6291456 | tf_op jit(solution)/shard_map/all_to_all | solution.py:399
  485.6 22.1 %tail.1 = (f32[512,1024]{1,0:T(8,128)}, bf16[1024,3072]{1,0:T(8,128)(2,1)}, f32[8,3072]{1,0:T(8,128)}, f32[8,2048]{1,0:T(8,128)}) custom-call(bf16[512,1024]{1,0:T(8,128)(2,1)} %bitcast.85, bf16[512,1024]{1,0:T(8,128)(2,1)} %get-tuple-element.32.n1_ref, f32[512,1024]{1,0:T(8,128)} %get-tuple-element.33.dm_ref, bf16[4,512,768]{2,1,0:T(8,128)(2,1)} %all_to_all.25.g_ref, ...), custom_call_target="tpu_custom_call" | custom-call | flops 6442450944 | bytes 20971520 | tf_op jit(solution)/shard_map/tail/pallas_call | solution.py:356
  512.5 11.3 %psum.15 = bf16[2,6144]{1,0:T(2,128)(2,1)S(1)} all-reduce(f32[2,6144]{1,0:T(2,128)S(1)} %pad_maximum_fusion), channel_id=1, replica_groups=mesh['head'=4,'seq'=8] {'head'}, use_global_device_ids=true, to_apply=%region_11.12 | all-reduce | flops 12288 | bytes 73728 | tf_op jit(solution)/shard_map/psum | solution.py:406
  523.8 37.7 %all-gather.4 = bf16[8,2,6144]{2,1,0:T(2,128)(2,1)S(1)} all-gather(bf16[1,2,6144]{2,1,0:T(2,128)(2,1)S(1)} %bitcast.68), channel_id=5, replica_groups=mesh['head'=4,'seq'=8] {'seq'}, dimensions={0}, use_global_device_ids=true | all-gather | bytes 221184 | tf_op jit(solution)/shard_map/all_gather | solution.py:407
  562.4 3.3 all-to-all-start.4
  565.8 41.7 %all-reduce.2 = f32[32,224]{1,0:T(8,128)S(1)} all-reduce(f32[32,224]{1,0:T(8,128)S(1)} %pad_maximum_fusion.1), channel_id=8, replica_groups=mesh['head'=4,'seq'=8] {'head','seq'}, use_global_device_ids=true, to_apply=%region_14.15.clone | all-reduce | flops 7168 | bytes 57344
  611.1 5.2 all_gather.39
  617.0 1.5 convert_element_type.97
  618.5 16.0 %reduce-scatter.9.cloned.1.call-done = bf16[32,2048]{1,0:T(8,128)(2,1)} async-done(((bf16[1024,2048]{1,0:T(8,128)(2,1)}), bf16[32,2048]{1,0:T(8,128)(2,1)}) %reduce-scatter.9.cloned.1.call-update) | async-done | bytes 131088 | tf_op jit(solution)/shard_map/reduce_scatter | solution.py:405
  634.5 1.6 convert_element_type.98
  636.1 141.0 %reduce-scatter.11.cloned.1.call-done = bf16[64,1024]{1,0:T(8,128)(2,1)} async-done(((bf16[2048,1024]{1,0:T(8,128)(2,1)}), bf16[64,1024]{1,0:T(8,128)(2,1)}) %reduce-scatter.11.cloned.1.call-update) | async-done | bytes 131088 | tf_op jit(solution)/shard_map/reduce_scatter | solution.py:405
  777.1 1.6 convert_element_type.99
  778.7 115.1 %reduce-scatter.5.cloned.1.call-done = bf16[32,3072]{1,0:T(8,128)(2,1)} async-done(((bf16[1024,3072]{1,0:T(8,128)(2,1)}), bf16[32,3072]{1,0:T(8,128)(2,1)}) %reduce-scatter.5.cloned.1.call-update) | async-done | bytes 196624 | tf_op jit(solution)/shard_map/reduce_scatter | solution.py:405
  (119 shorter events, 31.5 us)
Async XLA Ops:
  8.0 33.4 %copy-start = (bf16[32,6144]{1,0:T(8,128)(2,1)S(1)}, bf16[32,6144]{1,0:T(8,128)(2,1)}, u32[]{:S(2)}) copy-start(bf16[32,6144]{1,0:T(8,128)(2,1)} %param.21) | copy-start | bytes 1179652
  8.0 80.9 %copy-start.11 = (u32[32]{0:T(128)S(1)}, u32[32]{0:T(128)}, u32[]{:S(2)}) copy-start(u32[32]{0:T(128)} %constant.110) | copy-start | bytes 388
  8.0 38.8 %copy-start.10 = (bf16[96]{0:T(256)(128)(2,1)S(1)}, bf16[96]{0:T(256)(128)(2,1)}, u32[]{:S(2)}) copy-start(bf16[96]{0:T(256)(128)(2,1)} %param.24) | copy-start | bytes 580
  8.1 38.8 %copy-start.9 = (bf16[32]{0:T(256)(128)(2,1)S(1)}, bf16[32]{0:T(256)(128)(2,1)}, u32[]{:S(2)}) copy-start(bf16[32]{0:T(256)(128)(2,1)} %param.26) | copy-start | bytes 196
  8.1 38.8 %copy-start.8 = (bf16[64]{0:T(256)(128)(2,1)S(1)}, bf16[64]{0:T(256)(128)(2,1)}, u32[]{:S(2)}) copy-start(bf16[64]{0:T(256)(128)(2,1)} %param.28) | copy-start | bytes 388
  8.1 38.8 %copy-start.7 = (bf16[32]{0:T(256)(128)(2,1)S(1)}, bf16[32]{0:T(256)(128)(2,1)}, u32[]{:S(2)}) copy-start(bf16[32]{0:T(256)(128)(2,1)} %param.30) | copy-start | bytes 196
  8.1 79.9 %copy-start.6 = (s32[1,512]{1,0:T(1,128)S(1)}, s32[1,512]{1,0:T(1,128)}, u32[]{:S(2)}) copy-start(s32[1,512]{1,0:T(1,128)} %param.20) | copy-start | bytes 6148
  8.1 79.9 %copy-start.4 = (s32[1,512]{1,0:T(1,128)S(1)}, s32[1,512]{1,0:T(1,128)}, u32[]{:S(2)}) copy-start(s32[1,512]{1,0:T(1,128)} %param.18) | copy-start | bytes 6148
  8.1 116.1 %all-reduce.5.cloned.1.call-start = ((), (), s32[]{:S(2)}) async-start(), calls=%async_computation.17 | async-start | bytes 786432
  42.8 94.4 %all-gather.10.cloned.1.call-start = ((), (), s32[]{:S(2)}) async-start(), calls=%async_computation.9 | async-start | bytes 6488064 | tf_op jit(solution)/shard_map/all_gather | solution.py:373
  44.9 212.7 %all-gather.12.cloned.1.call-start = ((), (), s32[]{:S(2)}) async-start(), calls=%async_computation.10 | async-start | bytes 2162688 | tf_op jit(solution)/shard_map/all_gather | solution.py:373
  45.5 212.1 %all-gather.14.cloned.1.call-start = ((), (), s32[]{:S(2)}) async-start(), calls=%async_computation.11 | async-start | bytes 4325376 | tf_op jit(solution)/shard_map/all_gather | solution.py:373
  46.1 262.6 %all-gather.16.cloned.1.call-start = ((), (), s32[]{:S(2)}) async-start(), calls=%async_computation.12 | async-start | bytes 4325376 | tf_op jit(solution)/shard_map/all_gather | solution.py:373
  147.9 4.9 copy-start.5
  147.9 50.7 %all-to-all-start = ((bf16[4,512,768]{2,1,0:T(8,128)(2,1)}), bf16[4,512,768]{2,1,0:T(8,128)(2,1)}, u32[]{:S(2)}, u32[]{:S(2)}) async-start(bf16[4,512,768]{2,1,0:T(8,128)(2,1)} %get-tuple-element.29), calls=%async_computation | async-start | bytes 6291456 | tf_op jit(solution)/shard_map/all_to_all | solution.py:392
  238.6 18.0 %all-to-all-start.1 = ((bf16[4,512,256]{2,1,0:T(8,128)(2,1)}), bf16[4,512,256]{2,1,0:T(8,128)(2,1)S(1)}, u32[]{:S(2)}, u32[]{:S(2)}) async-start(bf16[4,512,256]{2,1,0:T(8,128)(2,1)} %bitcast.61), calls=%async_computation.1 | async-start | bytes 2097152 | tf_op jit(solution)/shard_map/all_to_all | solution.py:399
  242.1 374.9 %reduce-scatter.7.cloned.1.call-start = ((), (), s32[]{:S(2)}) async-start(), calls=%async_computation.14 | async-start | bytes 2162688 | tf_op jit(solution)/shard_map/reduce_scatter | solution.py:405
  353.3 281.2 %reduce-scatter.9.cloned.1.call-start = ((), (), s32[]{:S(2)}) async-start(), calls=%async_computation.15 | async-start | bytes 4325376 | tf_op jit(solution)/shard_map/reduce_scatter | solution.py:405
  354.0 1.2 copy-start.2
  354.0 423.1 %reduce-scatter.11.cloned.1.call-start = ((), (), s32[]{:S(2)}) async-start(), calls=%async_computation.16 | async-start | bytes 4325376 | tf_op jit(solution)/shard_map/reduce_scatter | solution.py:405
  356.3 18.0 %all-to-all-start.2 = ((bf16[4,512,256]{2,1,0:T(8,128)(2,1)}), bf16[4,512,256]{2,1,0:T(8,128)(2,1)S(1)}, u32[]{:S(2)}, u32[]{:S(2)}) async-start(bf16[4,512,256]{2,1,0:T(8,128)(2,1)} %bitcast.57), calls=%async_computation.2 | async-start | bytes 2097152 | tf_op jit(solution)/shard_map/all_to_all | solution.py:402
  359.8 534.1 %reduce-scatter.5.cloned.1.call-start = ((), (), s32[]{:S(2)}) async-start(), calls=%async_computation.13 | async-start | bytes 6488064 | tf_op jit(solution)/shard_map/reduce_scatter | solution.py:405
  374.2 1.0 copy-start.1
  507.7 108.7 %copy-start.3 = (bf16[1,2,1024]{2,1,0:T(2,128)(2,1)S(1)}, bf16[1,2,1024]{2,1,0:T(2,128)(2,1)}, u32[]{:S(2)}) copy-start(bf16[1,2,1024]{2,1,0:T(2,128)(2,1)} %param.17) | copy-start | bytes 12292
  562.4 48.7 %all-to-all-start.4 = ((f32[8,2,32]{2,1,0:T(2,128)}), f32[8,2,32]{2,1,0:T(2,128)S(1)}, u32[]{:S(2)}, u32[]{:S(2)}) async-start(f32[8,2,32]{2,1,0:T(2,128)} %copy.134), calls=%async_computation.4 | async-start | bytes 16384 | tf_op jit(solution)/shard_map/all_to_all | solution.py:411
Sparse Core Ops, SparseCore 0:
  42.9 81.3 all-reduce.4
Sparse Core Ops, SparseCore 1:
  47.1 71.2 all-gather.9
  121.7 58.1 all-gather.11
  183.3 60.9 all-gather.13
  247.8 60.8 all-gather.15
  353.3 137.0 reduce-scatter.6
  492.6 141.8 reduce-scatter.8
  636.6 140.4 reduce-scatter.10
  782.6 111.2 reduce-scatter.4

commit v2 on v1

--- a/solution.py
+++ b/solution.py
@@ -8,13 +8,23 @@
 from jax.experimental.pallas import tpu as pltpu
 from jax.sharding import PartitionSpec as P
 
+bf = jnp.bfloat16
+f32 = jnp.float32
+HS = ("head", "seq")
+ANY = pl.BlockSpec(memory_space=pl.ANY)
+V = pl.BlockSpec(memory_space=pltpu.VMEM)
+NN = (((1,), (0,)), ((), ()))
+NT = (((1,), (1,)), ((), ()))
+TN = (((0,), (0,)), ((), ()))
+
+
+def dot(a, b, dims=NN):
+    return lax.dot_general(a, b, dims, preferred_element_type=f32)
+
+
 HD=64
 LOG2E=math.log2(math.e)
 NEG=-1e30
-bf=jnp.bfloat16; f32=jnp.float32
-NT=(((1,),(1,)),((),()))
-NN=(((1,),(0,)),((),()))
-def dot(a,b,dims=NN): return lax.dot_general(a,b,dims,preferred_element_type=f32)
 
 def fwd_kernel(lo_ref,hi_ref,qkv_ref,auxq_ref,auxk_ref,o_ref,lse_ref,k2,vx,q2,s_scr,m_scr,acc,*,T,nh):
     qt=pl.program_id(0)
@@ -194,13 +204,7 @@
     ak=jnp.where(lane<3,1.,jnp.where(lane==3,(sg==0).astype(f32),jnp.where(lane==4,(sg==1).astype(f32),jnp.where(lane==5,pad.astype(f32),0.)))).astype(bf)
     return aq,ak
 
-bf=jnp.bfloat16; f32=jnp.float32
 EPS=1e-6
-NN=(((1,),(0,)),((),()))
-NT=(((1,),(1,)),((),()))
-TN=(((0,),(0,)),((),()))
-def dot(a,b,dims=NN): return lax.dot_general(a,b,dims,preferred_element_type=f32)
-V=pl.BlockSpec(memory_space=pltpu.VMEM)
 
 def moments(x):
     c=jnp.mean(x,-1,keepdims=True)
@@ -248,11 +252,17 @@
         compiler_params=pltpu.CompilerParams(vmem_limit_bytes=60*2**20),name="qkv_proj",
         cost_estimate=pl.CostEstimate(flops=2*F*D*3*D,bytes_accessed=14*2**20,transcendentals=0))(x,seg,emb,w,b,cos,sin)
 
-def mid_kernel(x_ref,a_ref,c_ref,seg_ref,msk_ref,emb_ref,wo_ref,bo_ref,wu_ref,bu_ref,wd_ref,bd_ref,
-               out_ref,dm_ref,da_ref,go_ref,gu_ref,gd_ref,gb_ref,ge_ref,
-               n2s,acts,dhs,dfs,dps,dgelu,*,R):
-    F,D=x_ref.shape; H=wu_ref.shape[1]; CH=512
+def mid_kernel(x_ref,a_ref,c_ref,seg_ref,msk_ref,emb_ref,w_ref,bo_ref,bu_ref,bd_ref,
+               out_ref,dm_ref,da_ref,gw_ref,gb_ref,ge_ref,
+               wo_ref,wu_ref,wd_ref,n2s,acts,dhs,dfs,dps,dgelu,sem,*,R):
+    F,D=x_ref.shape; H=bu_ref.shape[1]; CH=512
+    loads=[pltpu.make_async_copy(w_ref.at[:,pl.ds(o,n)],r,sem.at[i]) for i,(o,n,r) in enumerate(((2*H,D,wo_ref),(0,H,wu_ref),(H,H,wd_ref)))]
+    for l in loads: l.start()
     gb_ref[...]=jnp.zeros_like(gb_ref); ge_ref[...]=jnp.zeros_like(ge_ref)
+    for l in loads: l.wait()
+    def down(j):
+        t,o=divmod(j*CH,D)
+        return slice(o,o+CH),slice(t*D,(t+1)*D)
     @pl.loop(0,F//R)
     def _(i):
         r=pl.ds(pl.multiple_of(i*R,R),R)
@@ -274,7 +284,7 @@
             a,g=gelu_both(h)
             a=a.astype(bf)
             acts[r,c]=a; dgelu[:,c]=g
-            feed+=dot(a,wd_ref[c,:])
+            feed+=dot(a,wd_ref[down(j)])
         up=c_ref[r,:].astype(f32)
         g2=pick(seg,emb_ref,5,D)
         out_ref[r,:]=(middle+g2*feed).astype(bf)
@@ -285,7 +295,7 @@
         dn=jnp.zeros((R,D),f32)
         for j in range(H//CH):
             c=slice(j*CH,(j+1)*CH)
-            dh=(dot(df,wd_ref[c,:],NT)*dgelu[:,c]).astype(bf)
+            dh=(dot(df,wd_ref[down(j)],NT)*dgelu[:,c]).astype(bf)
             dhs[r,c]=dh
             gb_ref[1:2,c]+=jnp.sum(dh.astype(f32),0,keepdims=True)
             dn+=dot(dh,wu_ref[:,c],NT)
@@ -301,22 +311,21 @@
     @pl.loop(0,D//256)
     def _(i):
         c=pl.ds(pl.multiple_of(i*256,256),256)
-        go_ref[c,:]=dot(a_ref[:,c],dps[...],TN).astype(bf)
-        gu_ref[c,:]=dot(n2s[:,c],dhs[...],TN).astype(bf)
-    @pl.loop(0,H//256)
-    def _(i):
-        c=pl.ds(pl.multiple_of(i*256,256),256)
-        gd_ref[c,:]=dot(acts[:,c],dfs[...],TN).astype(bf)
-
-def mid(x,a,c,seg,msk,emb,wo,bo,wu,bu,wd,bd,R=128):
-    F,D=x.shape; H=wu.shape[1]
-    S=jax.ShapeDtypeStruct
+        gw_ref[c,2*H:2*H+D]=dot(a_ref[:,c],dps[...],TN).astype(bf)
+        gw_ref[c,0:H]=dot(n2s[:,c],dhs[...],TN).astype(bf)
+        for t in range(H//D):
+            e=pl.ds(pl.multiple_of(t*D+i*256,256),256)
+            gw_ref[c,H+t*D:H+(t+1)*D]=dot(acts[:,e],dfs[...],TN).astype(bf)
+
+def mid(x,a,c,seg,msk,emb,w,bo,bu,bd,R=128):
+    F,D=x.shape; H=bu.shape[1]
+    S=jax.ShapeDtypeStruct; M=pltpu.VMEM
     return pl.pallas_call(functools.partial(mid_kernel,R=R),
-        out_shape=(S((F,D),bf),S((F,D),f32),S((F,D),bf),S((D,D),bf),S((D,H),bf),S((H,D),bf),S((8,H),f32),S((8,4*D),f32)),
-        in_specs=[V]*12,out_specs=(V,)*8,
-        scratch_shapes=[pltpu.VMEM((F,D),bf),pltpu.VMEM((F,H),bf),pltpu.VMEM((F,H),bf),pltpu.VMEM((F,D),bf),pltpu.VMEM((F,D),bf),pltpu.VMEM((R,H),f32)],
+        out_shape=(S((F,D),bf),S((F,D),f32),S((F,D),bf),S((D,2*H+D),bf),S((8,H),f32),S((8,4*D),f32)),
+        in_specs=[V]*6+[ANY]+[V]*3,out_specs=(V,)*6,
+        scratch_shapes=[M((D,D),bf),M((D,H),bf),M((D,H),bf),M((F,D),bf),M((F,H),bf),M((F,H),bf),M((F,D),bf),M((F,D),bf),M((R,H),f32),pltpu.SemaphoreType.DMA((3,))],
         compiler_params=pltpu.CompilerParams(vmem_limit_bytes=62*2**20),name="mid",
-        cost_estimate=pl.CostEstimate(flops=6*F*D*(D+2*H),bytes_accessed=30*2**20,transcendentals=F*H))(x,a,c,seg,msk,emb,wo,bo,wu,bu,wd,bd)
+        cost_estimate=pl.CostEstimate(flops=6*F*D*(D+2*H),bytes_accessed=30*2**20,transcendentals=F*H))(x,a,c,seg,msk,emb,w,bo,bu,bd)
 
 def tail_kernel(x_ref,n1_ref,dm_ref,g_ref,seg_ref,emb_ref,w_ref,cos_ref,sin_ref,gf_ref,gw_ref,gb_ref,ge_ref,dps,*,R,nd,W):
     F,D=x_ref.shape
@@ -360,37 +369,387 @@
         compiler_params=pltpu.CompilerParams(vmem_limit_bytes=60*2**20),name="tail",
         cost_estimate=pl.CostEstimate(flops=4*F*D*3*D,bytes_accessed=20*2**20,transcendentals=0))(x,n1,dm,g,seg,emb,w,cos,sin)
 
-HS=("head","seq")
+def sizes(nd,ns):
+    Y=2**((ns.bit_length()-1)//2)
+    return nd//2,Y,ns//Y
+
+class Place:
+    def __init__(self,nd,ns):
+        self.nd,self.ns=nd,ns
+        self.X,self.Y,self.Z=sizes(nd,ns)
+        self.h=lax.axis_index("head"); self.s=lax.axis_index("seq")
+        self.x,self.c=self.h//2,self.h%2
+        self.z,self.y=self.s//self.Y,self.s%self.Y
+    def at(self,x=None,c=None,z=None,y=None):
+        x=self.x if x is None else x; c=self.c if c is None else c
+        z=self.z if z is None else z; y=self.y if y is None else y
+        return (x*2+c,z*self.Y+y)
+
+def near_first(n):
+    out=[]
+    for d in range(1,n//2+1):
+        out.append(d)
+        if n-d!=d: out.append(n-d)
+    return out
+
+def remote(src,dst,ss,rs,dev):
+    cp=pltpu.make_async_remote_copy(src_ref=src,dst_ref=dst,send_sem=ss,recv_sem=rs,device_id=dev,device_id_type=pl.DeviceIdType.MESH)
+    cp.start()
+    return cp
+
+def greet_all(p):
+    b=pltpu.get_barrier_semaphore()
+    @pl.loop(0,p.nd)
+    def _(dh):
+        @pl.loop(0,p.ns)
+        def _(ds):
+            @pl.when(dh+ds>0)
+            def _():
+                pl.semaphore_signal(b,inc=1,device_id=(lax.rem(p.h+dh,p.nd),lax.rem(p.s+ds,p.ns)),device_id_type=pl.DeviceIdType.MESH)
+    pl.semaphore_wait(b,p.nd*p.ns-1)
+
+class Gather:
+    @staticmethod
+    def sems(nd,ns):
+        X,Y,Z=sizes(nd,ns)
+        D=pltpu.SemaphoreType.DMA
+        one=[D((Z,)),D((Z,X)),D((Z,Y)),D((Z,X,Y)),D((Z,X,Y)),D((Z,)),D((2,Z,X,Y))]
+        return one+one+[D(())]
+    def __init__(self,p,shard,out,sems):
+        self.p,self.shard,self.out=p,shard,out
+        self.ss,self.rs,self.ls=sems[:7],sems[7:14],sems[14]
+        self.all=[]; self.half=shard.shape[-1]//2
+        self.two={}; self.three={}
+    def send(self,k,idx,src,dst,dev):
+        cp=remote(src,dst,self.ss[k].at[idx],self.rs[k].at[idx],dev)
+        self.all.append(cp); return cp
+    def cols(self,part): return pl.ds(part*self.half,self.half)
+    def loc(self,x,z,y,part=None):
+        r=self.out.at[x,self.p.c,z,y]
+        return r if part is None else r.at[:,self.cols(part)]
+    def start(self):
+        p=self.p
+        self.zc={}
+        for dz in near_first(p.Z):
+            self.zc[dz]=self.send(0,(dz,),self.shard,self.loc(p.x,p.z,p.y),p.at(z=lax.rem(p.z+dz,p.Z)))
+        self.local=pltpu.make_async_copy(self.shard,self.loc(p.x,p.z,p.y),self.ls)
+        self.local.start()
+        self.second(0)
+    def second(self,dz):
+        p=self.p; zz=lax.rem(p.z+p.Z-dz,p.Z)
+        if dz: self.zc[dz].wait_recv()
+        def src(part=None):
+            if dz: return self.loc(p.x,zz,p.y,part)
+            return self.shard if part is None else self.shard.at[:,self.cols(part)]
+        for dx in near_first(p.X):
+            self.two[0,dz,dx]=self.send(1,(dz,dx),src(0),self.loc(p.x,zz,p.y,0),p.at(x=lax.rem(p.x+dx,p.X)))
+        for dy in near_first(p.Y):
+            self.two[1,dz,dy]=self.send(2,(dz,dy),src(1),self.loc(p.x,zz,p.y,1),p.at(y=lax.rem(p.y+dy,p.Y)))
+        self.send(5,(dz,),src(),self.loc(p.x,zz,p.y),p.at(c=1-p.c))
+        for dy in near_first(p.Y):
+            self.three[0,dz,0,dy]=self.send(3,(dz,0,dy),src(0),self.loc(p.x,zz,p.y,0),p.at(y=lax.rem(p.y+dy,p.Y)))
+        for dx in near_first(p.X):
+            self.three[1,dz,dx,0]=self.send(4,(dz,dx,0),src(1),self.loc(p.x,zz,p.y,1),p.at(x=lax.rem(p.x+dx,p.X)))
+    def third(self,dz):
+        p=self.p; zz=lax.rem(p.z+p.Z-dz,p.Z)
+        for dx in near_first(p.X):
+            self.two[0,dz,dx].wait_recv()
+            l=self.loc(lax.rem(p.x+p.X-dx,p.X),zz,p.y,0)
+            for dy in near_first(p.Y):
+                self.three[0,dz,dx,dy]=self.send(3,(dz,dx,dy),l,l,p.at(y=lax.rem(p.y+dy,p.Y)))
+            self.send(6,(0,dz,dx,0),l,l,p.at(c=1-p.c))
+        for dy in near_first(p.Y):
+            self.two[1,dz,dy].wait_recv()
+            l=self.loc(p.x,zz,lax.rem(p.y+p.Y-dy,p.Y),1)
+            for dx in near_first(p.X):
+                self.three[1,dz,dx,dy]=self.send(4,(dz,dx,dy),l,l,p.at(x=lax.rem(p.x+dx,p.X)))
+            self.send(6,(1,dz,0,dy),l,l,p.at(c=1-p.c))
+    def fourth(self,dz):
+        p=self.p; zz=lax.rem(p.z+p.Z-dz,p.Z)
+        for part in (0,1):
+            for dx in range(p.X):
+                for dy in range(p.Y):
+                    if (part,dz,dx,dy) not in self.three: continue
+                    self.three[part,dz,dx,dy].wait_recv()
+                    l=self.loc(lax.rem(p.x+p.X-dx,p.X),zz,lax.rem(p.y+p.Y-dy,p.Y),part)
+                    self.send(6,(part,dz,dx,dy),l,l,p.at(c=1-p.c))
+    def finish(self):
+        waited=set()
+        for cp in self.zc.values(): waited.add(id(cp))
+        for d in (self.two,self.three):
+            for cp in d.values(): waited.add(id(cp))
+        for cp in self.all:
+            if id(cp) not in waited: cp.wait_recv()
+            cp.wait_send()
+        self.local.wait()
+
+def entry_kernel(nd,ns,nw,*refs):
+    shards=refs[:nw]; bias,time,ids,wada=refs[nw:nw+4]
+    outs=refs[nw+4:2*nw+4]; bias_all,ids_all,emb,act=refs[2*nw+4:2*nw+8]
+    time_all,part,r1,r2,bs,br,isd,ir,ts,tr,e1s,e1r,e2s,e2r=refs[2*nw+8:2*nw+22]
+    gs=refs[2*nw+22:]
+    p=Place(nd,ns); n=len(Gather.sems(nd,ns))
+    greet_all(p)
+    tail=[]
+    first=[]
+    for ds in range(1,ns):
+        first.append(remote(time,time_all.at[p.s],ts.at[ds],tr.at[ds],(p.h,lax.rem(p.s+ds,ns))))
+    g=[Gather(p,shards[i],outs[i],gs[i*n:(i+1)*n]) for i in range(nw)]
+    for a in g: a.start()
+    me=p.h*ns+p.s
+    for dh in range(1,nd):
+        tail.append(remote(ids,ids_all.at[p.h],isd.at[dh],ir.at[dh],(lax.rem(p.h+dh,nd),p.s)))
+    @pl.loop(0,nd)
+    def _(dh):
+        @pl.loop(0,ns)
+        def _(ds):
+            @pl.when(dh+ds>0)
+            def _():
+                remote(bias,bias_all.at[me],bs.at[dh,ds],br.at[dh,ds],(lax.rem(p.h+dh,nd),lax.rem(p.s+ds,ns)))
+    l1=pltpu.make_async_copy(bias,bias_all.at[me],bs.at[0,0]); l1.start()
+    l2=pltpu.make_async_copy(ids,ids_all.at[p.h],isd.at[0]); l2.start()
+    time_all[p.s]=time[...]
+    for cp in first: cp.wait()
+    D=time.shape[1]; K=wada.shape[0]; E=wada.shape[1]//8
+    v=time_all[...].reshape(ns*8,D)
+    low=(v/(1.0+jnp.exp(-v))).astype(bf)
+    kk=D//(nd*ns)
+    row=lax.broadcasted_iota(jnp.int32,(D,128),0); col=lax.broadcasted_iota(jnp.int32,(D,128),1)
+    pickm=jnp.where((row==me*kk+col)&(col<kk),1.0,0.0).astype(bf)
+    own=dot(low,pickm).astype(bf)
+    act[...]=own
+    for j in range(8):
+        pj=dot(own[:,:K],wada[:,j*E:(j+1)*E])
+        for s in range(ns):
+            part[s,2*j:2*j+2,:]=pj[8*s:8*s+2,:]
+    one=[remote(part.at[lax.rem(p.s+ds,ns)],r1.at[ds],e1s.at[ds],e1r.at[ds],(p.h,lax.rem(p.s+ds,ns))) for ds in range(1,ns)]
+    order=[0]+near_first(p.Z)
+    for a in g:
+        for i,dz in enumerate(order):
+            if dz: a.second(dz)
+            if i: a.third(order[i-1])
+        a.third(order[-1])
+    tot=part[p.s]
+    for ds in range(1,ns):
+        one[ds-1].wait()
+        tot=tot+r1[ds]
+    r2[p.h]=tot
+    two=[remote(r2.at[p.h],r2.at[p.h],e2s.at[dh],e2r.at[dh],(lax.rem(p.h+dh,nd),p.s)) for dh in range(1,nd)]
+    for a in g:
+        for dz in order: a.fourth(dz)
+    for cp in two: cp.wait()
+    tot=r2[0]
+    for i in range(1,nd): tot=tot+r2[i]
+    emb[...]=tot
+    for a in g: a.finish()
+    for cp in tail: cp.wait()
+    l1.wait(); l2.wait()
+    @pl.loop(0,nd)
+    def _(dh):
+        @pl.loop(0,ns)
+        def _(ds):
+            @pl.when(dh+ds>0)
+            def _():
+                pltpu.make_async_remote_copy(src_ref=bias,dst_ref=bias_all.at[me],send_sem=bs.at[dh,ds],recv_sem=br.at[dh,ds],device_id=(lax.rem(p.h+dh,nd),lax.rem(p.s+ds,ns)),device_id_type=pl.DeviceIdType.MESH).wait()
+
+def entry(nd,ns,shards,bias,time,ids,wada):
+    X,Y,Z=sizes(nd,ns)
+    S=jax.ShapeDtypeStruct
+    D=pltpu.SemaphoreType.DMA
+    nw=len(shards); E=wada.shape[1]//8
+    outs=[S((X,2,Z,Y)+a.shape,a.dtype) for a in shards]+[S((nd*ns,)+bias.shape,bias.dtype),S((nd,)+ids.shape,ids.dtype),S((16,E),f32),S((ns*8,128),bf)]
+    scr=[pltpu.VMEM((ns,8,time.shape[1]),f32),pltpu.VMEM((ns,16,E),f32),pltpu.VMEM((ns,16,E),f32),pltpu.VMEM((nd,16,E),f32),
+         D((nd,ns)),D((nd,ns)),D((nd,)),D((nd,)),D((ns,)),D((ns,)),D((ns,)),D((ns,)),D((nd,)),D((nd,))]
+    for _ in shards: scr+=Gather.sems(nd,ns)
+    return pl.pallas_call(functools.partial(entry_kernel,nd,ns,nw),out_shape=tuple(outs),
+        in_specs=[ANY]*(nw+1)+[V,ANY,V],out_specs=tuple([ANY]*(nw+2)+[V,V]),scratch_shapes=scr,
+        compiler_params=pltpu.CompilerParams(collective_id=0,has_side_effects=True,vmem_limit_bytes=40*2**20),name="entry")(*shards,bias,time,ids,wada)
+
+class Scatter:
+    @staticmethod
+    def scratch(nd,ns,k,w,dt):
+        X,Y,Z=sizes(nd,ns); M=pltpu.VMEM; D=pltpu.SemaphoreType.DMA
+        h=w//2
+        return [M((X,Z,Y,k,w),dt),M((X,Z,Y,k,w),dt),M((Y,X,Z,k,h),dt),M((X,Z,Y,k,h),dt),M((X,Z,k,h),dt),M((Y,Z,k,h),dt),M((Z,k,w),dt)]+\
+            [D((X,)),D((X,)),D((X,)),D((Y,)),D((Y,)),D((X,)),D((X,)),D((X,)),D((X,)),D((Y,)),D((Y,)),D((Z,)),D((Z,))]
+    count=20
+    def __init__(self,p,src,col,w,scr):
+        self.p,self.src,self.w=p,src,w
+        self.cs=pl.ds(col,w); self.h=w//2
+        self.own,self.cin,self.ya,self.xb,self.xa,self.yb,self.zr=scr[:7]
+        self.ls,self.c1,self.c2,self.a1,self.a2,self.b1,self.b2,self.d1,self.d2,self.e1,self.e2,self.z1,self.z2=scr[7:]
+        self.A=pl.ds(0,self.h); self.B=pl.ds(self.h,self.h); self.sent=[]
+    def start(self):
+        p=self.p
+        self.l=[];self.cc=[]
+        for x in range(p.X):
+            self.cc.append(remote(self.src.at[x,1-p.c,:,:,:,self.cs],self.cin.at[x],self.c1.at[x],self.c2.at[x],p.at(c=1-p.c)))
+            l=pltpu.make_async_copy(self.src.at[x,p.c,:,:,:,self.cs],self.own.at[x],self.ls.at[x]); l.start(); self.l.append(l)
+        self.sent+=self.cc
+    def add(self,i,x,cols):
+        self.own[i+(slice(None),cols)]=(self.own[i+(slice(None),cols)].astype(f32)+x.astype(f32)).astype(self.own.dtype)
+    def second(self):
+        p=self.p
+        for x in range(p.X):
+            self.l[x].wait(); self.cc[x].wait_recv()
+            @pl.loop(0,p.Z)
+            def _(z):
+                for y in range(p.Y):
+                    self.add((x,z,y),self.cin[x,z,y],slice(None))
+        self.a=[];self.b=[]
+        for dy in near_first(p.Y):
+            y=lax.rem(p.y+dy,p.Y)
+            self.a.append((dy,remote(self.own.at[:,:,y,:,self.A],self.ya.at[dy],self.a1.at[dy],self.a2.at[dy],p.at(y=y))))
+        for dx in near_first(p.X):
+            x=lax.rem(p.x+dx,p.X)
+            self.b.append((dx,remote(self.own.at[x,:,:,:,self.B],self.xb.at[dx],self.b1.at[dx],self.b2.at[dx],p.at(x=x))))
+        self.sent+=[c for _,c in self.a+self.b]
+    def third(self):
+        p=self.p
+        for dy,c in self.a:
+            c.wait_recv()
+            @pl.loop(0,p.Z)
+            def _(z):
+                for x in range(p.X): self.add((x,z,p.y),self.ya[dy,x,z],slice(0,self.h))
+        for dx,c in self.b:
+            c.wait_recv()
+            @pl.loop(0,p.Z)
+            def _(z):
+                for y in range(p.Y): self.add((p.x,z,y),self.xb[dx,z,y],slice(self.h,self.w))
+        self.a=[];self.b=[]
+        for dx in near_first(p.X):
+            x=lax.rem(p.x+dx,p.X)
+            self.a.append((dx,remote(self.own.at[x,:,p.y,:,self.A],self.xa.at[dx],self.d1.at[dx],self.d2.at[dx],p.at(x=x))))
+        for dy in near_first(p.Y):
+            y=lax.rem(p.y+dy,p.Y)
+            self.b.append((dy,remote(self.own.at[p.x,:,y,:,self.B],self.yb.at[dy],self.e1.at[dy],self.e2.at[dy],p.at(y=y))))
+        self.sent+=[c for _,c in self.a+self.b]
+    def fourth(self):
+        p=self.p
+        for dx,c in self.a:
+            c.wait_recv()
+            for z in range(p.Z): self.add((p.x,z,p.y),self.xa[dx,z],slice(0,self.h))
+        for dy,c in self.b:
+            c.wait_recv()
+            for z in range(p.Z): self.add((p.x,z,p.y),self.yb[dy,z],slice(self.h,self.w))
+        self.zc=[]
+        for dz in near_first(p.Z):
+            z=lax.rem(p.z+dz,p.Z)
+            self.zc.append((dz,remote(self.own.at[p.x,z,p.y],self.zr.at[dz],self.z1.at[dz],self.z2.at[dz],p.at(z=z))))
+        self.sent+=[c for _,c in self.zc]
+    def last(self,out,cols):
+        p=self.p
+        t=self.own[p.x,p.z,p.y].astype(f32)
+        for dz,c in self.zc:
+            c.wait_recv()
+            t=t+self.zr[dz].astype(f32)
+        out[:,cols]=t
+    def finish(self):
+        for c in self.sent: c.wait_send()
+
+def exit_kernel(nd,ns,plan,*refs):
+    na=max(a for a,_,_ in plan)+1
+    srcs=refs[:na]; ge,act,wada=refs[na:na+3]
+    outs=refs[na+3:2*na+3]; gada,gbada,dact=refs[2*na+3:2*na+6]
+    hsum,demb,dscr,hs,hr,qs,qr,ds_,dr=refs[2*na+6:2*na+15]
+    sc=refs[2*na+15:]
+    p=Place(nd,ns); me=p.h*ns+p.s
+    greet_all(p)
+    hsum[p.h]=ge[...]
+    hc=[remote(hsum.at[p.h],hsum.at[p.h],hs.at[dh],hr.at[dh],(lax.rem(p.h+dh,nd),p.s)) for dh in range(1,nd)]
+    it=[Scatter(p,srcs[a],c,w,sc[i*Scatter.count:(i+1)*Scatter.count]) for i,(a,c,w) in enumerate(plan)]
+    for s in it: s.start()
+    n=len(it); E=ge.shape[1]; K=wada.shape[0]; R=ns*16
+    qc=[]
+    for t in range(n+3):
+        if t<n: it[t].second()
+        if 0<=t-1<n: it[t-1].third()
+        if 0<=t-2<n: it[t-2].fourth()
+        if 0<=t-3<n: it[t-3].last(outs[plan[t-3][0]],slice(plan[t-3][1],plan[t-3][1]+plan[t-3][2]))
+        if t==0:
+            for c in hc: c.wait()
+            tot=hsum[0]
+            for i in range(1,nd): tot=tot+hsum[i]
+            demb[p.s]=tot.astype(bf)
+            qc=[remote(demb.at[p.s],demb.at[p.s],qs.at[d],qr.at[d],(p.h,lax.rem(p.s+d,ns))) for d in range(1,ns)]
+        if t==1:
+            for c in qc: c.wait()
+            flat=demb[...].reshape(R,E)
+            r0=lax.broadcasted_iota(jnp.int32,(R,ns*8),0); c0=lax.broadcasted_iota(jnp.int32,(R,ns*8),1)
+            spread=dot(jnp.where((r0//16==c0//8)&(r0%2==c0%8),1.0,0.0).astype(bf),act[...])
+            rr=lax.broadcasted_iota(jnp.int32,(R,128),0)%16//2
+            rk=lax.broadcasted_iota(jnp.int32,(R,K),0)%16//2
+            tot=jnp.zeros((R,K),f32)
+            for j in range(8):
+                m=jnp.where(rr==j,spread,0.0).astype(bf)
+                gada[:,j*E:(j+1)*E]=dot(m,flat,TN)[:K,:]
+                tot=jnp.where(rk==j,dot(flat,wada[:,j*E:(j+1)*E],NT),tot)
+            r8=lax.broadcasted_iota(jnp.int32,(8,R),0); c8=lax.broadcasted_iota(jnp.int32,(8,R),1)
+            gbada[...]=dot(jnp.where(c8%16//2==r8,1.0,0.0).astype(bf),flat)
+            dscr[...]=jnp.concatenate([tot,jnp.zeros((R,128-K),f32)],1).reshape(ns,16,128)
+            dact[me]=dscr[p.s]
+            @pl.loop(0,nd)
+            def _(dh):
+                @pl.loop(0,ns)
+                def _(d):
+                    @pl.when(dh+d>0)
+                    def _():
+                        s=lax.rem(p.s+d,ns)
+                        remote(dscr.at[s],dact.at[me],ds_.at[dh,d],dr.at[dh,d],(lax.rem(p.h+dh,nd),s))
+    for s in it: s.finish()
+    @pl.loop(0,nd)
+    def _(dh):
+        @pl.loop(0,ns)
+        def _(d):
+            @pl.when(dh+d>0)
+            def _():
+                s=lax.rem(p.s+d,ns)
+                pltpu.make_async_remote_copy(src_ref=dscr.at[s],dst_ref=dact.at[me],send_sem=ds_.at[dh,d],recv_sem=dr.at[dh,d],device_id=(lax.rem(p.h+dh,nd),s),device_id_type=pl.DeviceIdType.MESH).wait()
+
+def exit_(nd,ns,srcs,plan,ge,act,wada):
+    S=jax.ShapeDtypeStruct; D=pltpu.SemaphoreType.DMA
+    E=ge.shape[1]; K,E6=wada.shape
+    outs=[S(a.shape[-2:],f32) for a in srcs]+[S((K,E6),f32),S((8,E),f32),S((nd*ns,16,128),f32)]
+    scr=[pltpu.VMEM((nd,16,E),f32),pltpu.VMEM((ns,16,E),bf),pltpu.VMEM((ns,16,128),f32),D((nd,)),D((nd,)),D((ns,)),D((ns,)),D((nd,ns)),D((nd,ns))]
+    for a,c,w in plan: scr+=Scatter.scratch(nd,ns,srcs[a].shape[-2],w,srcs[a].dtype)
+    return pl.pallas_call(functools.partial(exit_kernel,nd,ns,tuple(plan)),out_shape=tuple(outs),
+        in_specs=[ANY]*len(srcs)+[V]*3,out_specs=tuple([V]*len(outs)),scratch_shapes=scr,
+        compiler_params=pltpu.CompilerParams(collective_id=1,has_side_effects=True,vmem_limit_bytes=60*2**20),name="exit")(*srcs,ge,act,wada)
+
 
 def body(frames,time_embed,segment_ids,frame_mask,positions,w_ada,b_ada,w_qkv,b_qkv,w_out,b_out,w_up,b_up,w_down,b_down,cotangent):
     _,F,D=frames.shape
     nd=lax.axis_size("head"); ns=lax.axis_size("seq"); dev=lax.axis_index("head")*ns+lax.axis_index("seq")
+    X,Y,Z=sizes(nd,ns); N=nd*ns
     W=D//nd
-    E=b_ada.shape[0]; E6=w_ada.shape[1]; K=w_ada.shape[0]
-    x=frames[0]; cot=cotangent[0]; seg=segment_ids[0]; msk=frame_mask[0]
+    E=b_ada.shape[0]; E6=w_ada.shape[1]; K=w_ada.shape[0]; H=w_up.shape[1]; nt=H//D
+    x=frames[0]; cot=cotangent[0]
     def reorder(w): return w.reshape(-1,3,nd,W).transpose(0,2,1,3).reshape(-1,3*D)
     def restore(w): return w.reshape(-1,nd,3,W).transpose(0,2,1,3).reshape(-1,3*D)
-    g=lambda w: lax.all_gather(w,HS,axis=0,tiled=True)
-    wq=g(reorder(w_qkv))
-    bias=g(jnp.concatenate([b_qkv,b_out,b_up,b_down])[None,:]).astype(f32)
-    n0,n1,n2,n3=b_qkv.shape[0],b_out.shape[0],b_up.shape[0],b_down.shape[0]
-    bq=reorder(bias[:,:n0].reshape(1,-1))
-    bo=bias[:,n0:n0+n1].reshape(1,-1); bu=bias[:,n0+n1:n0+n1+n2].reshape(1,-1); bd=bias[:,n0+n1+n2:].reshape(1,-1)
-    wo=g(w_out); wu=g(w_up); wd=g(w_down)
-    time_all=lax.all_gather(time_embed,"seq",axis=0,tiled=True).astype(f32)
-    act_all=jax.nn.silu(time_all).astype(bf)
-    act_own=lax.dynamic_slice_in_dim(act_all,dev*K,K,2)
-    part=jnp.einsum("rsd,de->rse",act_own,w_ada,preferred_element_type=f32)
-    part=part+lax.dynamic_update_slice(jnp.zeros((E6,),f32),b_ada.astype(f32),(dev*E,))
-    emb=lax.psum(lax.psum_scatter(part,"seq",scatter_dimension=0,tiled=True),"head")[0]
+    def hide(w): return w.reshape(-1,N,nt,K).transpose(0,2,1,3).reshape(-1,H)
+    def unhide(w): return w.reshape(-1,nt,N,K).transpose(0,2,1,3).reshape(-1,H)
+    rest=jnp.concatenate([hide(w_up),w_down.reshape(nt,K,D).transpose(1,0,2).reshape(K,H),w_out],axis=1)
+    bs=(b_qkv,b_out,b_up,b_down,b_ada); ends=[0]
+    for b in bs: ends.append(ends[-1]+b.shape[0])
+    wide=-(-ends[-1]//256)*256
+    bias=jnp.zeros((16,wide),bf).at[0,:ends[-1]].set(jnp.concatenate(bs))
+    time8=jnp.zeros((8,D),f32).at[:2].set(time_embed[0].astype(f32))
+    ids=jnp.zeros((8,F),jnp.int32).at[0].set(segment_ids[0]).at[1].set(frame_mask[0])
+    wq,bias_all,ids_all,emb,act=entry(nd,ns,[reorder(w_qkv)],bias,time8,ids,w_ada)
+    rest_all=lax.all_gather(rest,HS,axis=0,tiled=True)
+    wq=wq.reshape(D,3*D)
+    bias_all=bias_all[:,0,:].astype(f32)
+    bq,bo,bu,bd,ba=[bias_all[:,ends[i]:ends[i+1]].reshape(1,-1) for i in range(5)]
+    bq=reorder(bq); bu=hide(bu)
+    emb=emb.reshape(8,2,-1).transpose(1,0,2).reshape(2,E6)+ba
+    seg_row=ids_all[:,0,:].reshape(-1); msk_row=ids_all[:,1,:].reshape(-1)
     column=lax.iota(jnp.int32,128)
     pair=(column%HD//2).astype(f32)
     angles=positions[0].astype(f32)[:,None]*(10000.0**(-(2.0*pair)/HD))
     cos=jnp.cos(angles); sin=jnp.where(column%2==0,-jnp.sin(angles),jnp.sin(angles))
-    segc=seg[:,None]; mskc=msk.astype(f32)[:,None]
+    segc=segment_ids[0][:,None]; mskc=frame_mask[0].astype(f32)[:,None]
     normed,packed=qkv_proj(x,segc,emb,wq,bq,cos,sin,nd)
     qkv=lax.all_to_all(packed,"head",split_axis=0,concat_axis=0,tiled=True).reshape(nd*F,3*W)
-    seg_row=lax.all_gather(seg,"head",axis=0,tiled=True); msk_row=lax.all_gather(msk,"head",axis=0,tiled=True)
     T=256
     qlo,qhi,klo,khi=tables(seg_row,msk_row,T)
     aq,ak=aux(seg_row,msk_row)
@@ -398,23 +757,24 @@
     def back(a):
         return lax.all_to_all(a.reshape(nd,F,-1),"head",split_axis=0,concat_axis=0,tiled=True)
     att=back(o).transpose(1,0,2).reshape(F,D)
-    out,dmid,datt,gout,gup,gdown,gb,ge=mid(x,att,cot,segc,mskc,emb,wo,bo,wu,bu,wd,bd)
+    out,dmid,datt,grest,gb,ge=mid(x,att,cot,segc,mskc,emb,rest_all,bo,bu,bd)
     do=lax.all_to_all(datt.reshape(F,nd,W).transpose(1,0,2),"head",split_axis=0,concat_axis=0,tiled=True).reshape(nd*F,W)
     dqkv=attn_bwd(qkv,o,do,lse,klo,khi,aq,ak,T)
     gx,gqkv,gbq,ge1=tail(x,normed,dmid,back(dqkv),segc,emb,wq,cos,sin)
-    rs=lambda w: lax.psum_scatter(w,HS,scatter_dimension=0,tiled=True).astype(f32)
-    demb=lax.psum(jnp.concatenate([ge1[:2],ge[:2]],axis=1),"head").astype(bf)
-    demb_all=lax.all_gather(demb[None],"seq",axis=0,tiled=True)
-    gada=jnp.einsum("rsd,rse->de",act_own,demb_all,preferred_element_type=f32)
-    gbada=jnp.sum(lax.dynamic_slice_in_dim(demb_all,dev*E,E,2).astype(f32),(0,1))
-    dact=jnp.einsum("rse,de->rsd",demb_all,w_ada,preferred_element_type=f32)
-    dact=lax.all_to_all(dact,"seq",split_axis=0,concat_axis=0,tiled=True)
-    dact=lax.all_gather(dact,"head",axis=0,tiled=True).transpose(1,0,2).reshape(2,D)
+    shape=(X,2,Z,Y,K)
+    gbias=jnp.concatenate([restore(gbq[0:1]).reshape(N,-1),gb[0,:D].reshape(N,-1),unhide(gb[1:2]).reshape(N,-1),gb[2,:D].reshape(N,-1)],axis=1)
+    wide=-(-ends[4]//256)*256
+    gbias=jnp.zeros((N,8,wide),f32).at[:,0,:ends[4]].set(gbias).reshape(X,2,Z,Y,8,wide)
+    ge=jnp.concatenate([ge1[:2],ge[:2]],axis=1).reshape(2,8,-1).transpose(1,0,2).reshape(16,-1)
+    plan=[(0,j*D,D) for j in range(2*nt+1)]+[(2,0,wide)]+[(1,j*D,D) for j in range(3)]
+    grest,gqkv,gbias,gada,gbada,dact=exit_(nd,ns,[grest.reshape(shape+(2*H+D,)),gqkv.reshape(shape+(3*D,)),gbias],plan,ge,act,w_ada)
+    dact=dact[:,:,:K].reshape(N,8,2,K).sum(1).transpose(1,0,2).reshape(2,D)
     _,pull=jax.vjp(jax.nn.silu,time_embed[0].astype(f32))
     gtime=pull(dact)[0][None]
-    gbias=jnp.concatenate([restore(gbq[0:1]).reshape(-1,n0),gb[0,:D].reshape(-1,n1),gb[1].reshape(-1,n2),gb[2,:D].reshape(-1,n3)],axis=1)
-    gbias=lax.psum_scatter(gbias,HS,scatter_dimension=0,tiled=True)[0]
-    return (out[None],gx[None],gtime,gada,gbada,restore(rs(gqkv)),gbias[:n0],rs(gout),gbias[n0:n0+n1],rs(gup),gbias[n0+n1:n0+n1+n2],rs(gdown),gbias[n0+n1+n2:])
+    gbada=lax.dynamic_slice_in_dim(gbada.reshape(-1),dev*E,E,0)
+    gbs=[gbias[0,ends[i]:ends[i+1]] for i in range(4)]
+    gdown=grest[:,H:2*H].reshape(K,nt,D).transpose(1,0,2).reshape(nt*K,D)
+    return (out[None],gx[None],gtime,gada,gbada,restore(gqkv),gbs[0],grest[:,2*H:],gbs[1],unhide(grest[:,:H]),gbs[2],gdown,gbs[3])
 
 
 def solution(mesh):

time: 905 us -> 534 us (0.59)
  waiting for transfers between devices: 379 us -> 91.5 us
  blocking collectives: 269 us -> 0 us
  Pallas kernels: 185 us -> 358 us
  local copies, waits for them, and re-layouts: 23.3 us -> 39.6 us
    reduce_scatter x4 -> x0, waiting for transfers between devices: 272 us -> none  [body(): lax.psum_scatter(w, HS, scatter_dimension=0, tiled=True).astype(f32)]
    pallas_call x0 -> x2, Pallas kernels: none -> 174 us  [the longest x1 102 us: exit_(): pl.pallas_call(functools.partial(exit_kernel, nd, ns, tuple(plan)), out_s...]
    all_gather x5 -> x0, blocking collectives: 122 us -> none  [the longest x1 41.5 us: body(): msk_row = lax.all_gather(msk, 'head', axis=0, tiled=True)]
    unnamed x2 -> x0, blocking collectives: 81.7 us -> none
    all_gather x4 -> x1, waiting for transfers between devices: 51.1 us -> 0.01 us  [body(): rest_all = lax.all_gather(rest, HS, axis=0, tiled=True)]
    all_to_all x1 -> x0, blocking collectives: 42.3 us -> none  [back(): lax.all_to_all(a.reshape(nd, F, -1), 'head', split_axis=0, concat_axis=0,...]
    all_to_all x1 -> x2, waiting for transfers between devices: 11.2 us -> 44.9 us  [back(): lax.all_to_all(a.reshape(nd, F, -1), 'head', split_axis=0, concat_axis=0,...]
    all_to_all x1, waiting for transfers between devices: 0.01 us -> 32.7 us  [body(): lax.all_to_all(packed, 'head', split_axis=0, concat_axis=0, tiled=True)]
  transfers between devices with their start and end apart: 13 -> 5, of which waited for: 7 -> 4; matrix products, arithmetic and copies ran while one was open for 4% -> 3% of each run, Pallas kernels for 16% -> 23%
where the time goes in v2:
time: 534 us; the launch traced here: 528 us
  Pallas kernels  358 us (67%)
  waiting for transfers between devices  91.5 us (17%)
  local copies, waits for them, and re-layouts  39.6 us (7%)
  starting transfers between devices  14.9 us (3%)
  between operations  14.6 us (3%)
  other arithmetic  9.72 us (2%)
    pallas_call x1, Pallas kernels, exit_(): pl.pallas_call(functools.partial(exit_kernel, nd, ns, tuple(plan)), out_s...  102 us
    pallas_call x1, Pallas kernels, entry(): pl.pallas_call(functools.partial(entry_kernel, nd, ns, nw), out_shape=tup...  71.8 us
    pallas_call x1, Pallas kernels, attn_bwd(): pl.pallas_call(functools.partial(bwd_kernel, T=T, nh=nh), out_shape=jax.S...  68.1 us
    all_to_all x2, waiting for transfers between devices, back(): lax.all_to_all(a.reshape(nd, F, -1), 'head', split_axis=0, concat_axis=0,...  44.9 us
    pallas_call x1, Pallas kernels, mid(): pl.pallas_call(functools.partial(mid_kernel, R=R), out_shape=(S((F, D), b...  42.8 us
    pallas_call x1, Pallas kernels, attn_fwd(): pl.pallas_call(functools.partial(fwd_kernel, T=T, nh=nh), out_shape=(jax....  39.9 us
    all_to_all x1, waiting for transfers between devices, body(): lax.all_to_all(packed, 'head', split_axis=0, concat_axis=0, tiled=True)  32.7 us
    pallas_call x1, Pallas kernels, tail(): pl.pallas_call(functools.partial(tail_kernel, R=R, nd=nd, W=W), out_shape...  22.1 us
  transfers between devices with their start and end apart: 5, of which 4 were waited for; matrix products, arithmetic and copies ran while one was open for 3% of the time, Pallas kernels for 23%

profile of v2, /device:TPU:0, one launch (start us, length us, event | category | flops | bytes accessed | tf_op | source)
XLA Modules:
  0.0 527.9 jit_solution(224899674320414388)
XLA Ops:
  7.3 1.4 reshape.404
  9.4 1.0 copy.133
  10.5 1.6 pad_maximum_fusion
  12.9 71.8 %entry.1 = (bf16[2,2,4,2,32,3072]{5,4,3,2,1,0:T(8,128)(2,1)S(1)}, bf16[32,16,512]{2,1,0:T(8,128)(2,1)S(1)}, s32[4,8,512]{2,1,0:T(8,128)S(1)}, f32[16,768]{1,0:T(8,128)S(1)}, bf16[64,128]{1,0:T(8,128)(2,1)S(1)}) custom-call(bf16[32,3072]{1,0:T(8,128)(2,1)S(1)} %reshape.395.refs_0_, bf16[16,512]{1,0:T(8,128)(2,1)S(1)} %scatter.20.refs_1_, ...), custom_call_target="tpu_custom_call" | custom-call | tf_op jit(solution)/shard_map/entry/pallas_call | solution.py:564
  85.4 2.7 copy-done.2
  90.0 1.8 negate_select_fusion
  92.4 10.7 %qkv_proj.1 = (bf16[512,1024]{1,0:T(8,128)(2,1)}, bf16[4,512,768]{2,1,0:T(8,128)(2,1)}) custom-call(bf16[512,1024]{1,0:T(8,128)(2,1)} %bitcast.134, s32[512,1]{1,0:T(8,128)} %copy.130.seg_ref, f32[2,6144]{1,0:T(2,128)} %broadcast_add_fusion.emb_ref, bf16[1024,3072]{1,0:T(8,128)(2,1)} %bitcast.86, f32[1,3072]{1,0:T(1,128)} %reshape.400.b_ref, ...), custom_call_target="tpu_custom_call" | custom-call | flops 3221225472 | bytes 14680064 | tf_op jit(solution)/shard_map/qkv_proj/pallas_call | solution.py:249
  103.1 3.7 all-to-all-start
  108.4 2.7 select_convert_fusion
  111.1 32.7 %all-to-all-done = bf16[4,512,768]{2,1,0:T(8,128)(2,1)S(1)} async-done(((bf16[4,512,768]{2,1,0:T(8,128)(2,1)}), bf16[4,512,768]{2,1,0:T(8,128)(2,1)S(1)}, u32[]{:S(2)}, u32[]{:S(2)}) %all-to-all-start) | async-done | bytes 3145760 | tf_op jit(solution)/shard_map/all_to_all | solution.py:752
  143.8 1.7 copy-done.3
  145.6 39.9 %attn_fwd.1 = (bf16[2048,256]{1,0:T(8,128)(2,1)}, f32[2048,128]{1,0:T(8,128)}) custom-call(s32[8]{0:T(128)} %get-tuple-element.135.lo_ref, s32[8]{0:T(128)} %broadcast_add_fusion.2.hi_ref, bf16[2048,768]{1,0:T(8,128)(2,1)} %bitcast.88, bf16[2048,128]{1,0:T(8,128)(2,1)} %get-tuple-element.153.auxq_ref, bf16[2048,128]{1,0:T(8,128)(2,1)} %get-tuple-element.152.auxk_ref), custom_call_target="tpu_custom_call" | custom-call | tf_op jit(solution)/shard_map/attn_fwd/pallas_call | solution.py:93
  185.5 3.7 all-to-all-start.1
  192.3 11.2 %all-to-all-done.1 = bf16[4,512,256]{2,1,0:T(8,128)(2,1)S(1)} async-done(((bf16[4,512,256]{2,1,0:T(8,128)(2,1)}), bf16[4,512,256]{2,1,0:T(8,128)(2,1)S(1)}, u32[]{:S(2)}, u32[]{:S(2)}) %all-to-all-start.1) | async-done | bytes 1048608 | tf_op jit(solution)/shard_map/all_to_all | solution.py:758
  203.5 1.1 copy.150
  204.6 42.8 %mid.1 = (bf16[512,1024]{1,0:T(8,128)(2,1)}, f32[512,1024]{1,0:T(8,128)}, bf16[512,1024]{1,0:T(8,128)(2,1)}, bf16[1024,5120]{1,0:T(8,128)(2,1)}, f32[8,2048]{1,0:T(8,128)}, /*index=5*/f32[8,4096]{1,0:T(8,128)}) custom-call(bf16[512,1024]{1,0:T(8,128)(2,1)} %bitcast.135, bf16[512,1024]{1,0:T(8,128)(2,1)} %bitcast.101, bf16[512,1024]{1,0:T(8,128)(2,1)} %bitcast.133, ...), custom_call_target="tpu_custom_call" | custom-call | flops 16106127360 | bytes 31457280 | tf_op jit(solution)/shard_map/mid/pallas_call | solution.py:323
  247.4 2.3 copy.160
  249.6 3.5 all-to-all-start.2
  253.7 13.9 %all-to-all-done.2 = bf16[4,512,256]{2,1,0:T(8,128)(2,1)S(1)} async-done(((bf16[4,512,256]{2,1,0:T(8,128)(2,1)}), bf16[4,512,256]{2,1,0:T(8,128)(2,1)S(1)}, u32[]{:S(2)}, u32[]{:S(2)}) %all-to-all-start.2) | async-done | bytes 1048608 | tf_op jit(solution)/shard_map/all_to_all | solution.py:761
  267.6 1.0 copy-done.4
  268.6 68.1 %attn_bwd.1 = bf16[2048,768]{1,0:T(8,128)(2,1)} custom-call(s32[8]{0:T(128)} %get-tuple-element.134.lo_ref, s32[8]{0:T(128)} %broadcast_add_fusion.1.hi_ref, bf16[2048,768]{1,0:T(8,128)(2,1)} %bitcast.89, bf16[2048,256]{1,0:T(8,128)(2,1)} %get-tuple-element.103.o_ref, bf16[2048,256]{1,0:T(8,128)(2,1)} %bitcast.96, f32[2048,128]{1,0:T(8,128)} %get-tuple-element.108.lse_ref, ...), custom_call_target="tpu_custom_call" | custom-call | tf_op jit(solution)/shard_map/attn_bwd/pallas_call | solution.py:177
  336.7 3.9 all-to-all-start.3
  343.6 33.7 %all-to-all-done.3.g_ref = bf16[4,512,768]{2,1,0:T(8,128)(2,1)S(1)} async-done(((bf16[4,512,768]{2,1,0:T(8,128)(2,1)}), bf16[4,512,768]{2,1,0:T(8,128)(2,1)S(1)}, u32[]{:S(2)}, u32[]{:S(2)}) %all-to-all-start.3) | async-done | bytes 3145760 | tf_op jit(solution)/shard_map/all_to_all | solution.py:758
  377.3 1.7 copy-done.5
  379.0 22.1 %tail.1 = (f32[512,1024]{1,0:T(8,128)}, bf16[1024,3072]{1,0:T(8,128)(2,1)}, f32[8,3072]{1,0:T(8,128)}, f32[8,2048]{1,0:T(8,128)}) custom-call(bf16[512,1024]{1,0:T(8,128)(2,1)} %bitcast.136, bf16[512,1024]{1,0:T(8,128)(2,1)} %get-tuple-element.105.n1_ref, f32[512,1024]{1,0:T(8,128)} %get-tuple-element.106.dm_ref, bf16[4,512,768]{2,1,0:T(8,128)(2,1)} %copy-done.5, ...), custom_call_target="tpu_custom_call" | custom-call | flops 6442450944 | bytes 20971520 | tf_op jit(solution)/shard_map/tail/pallas_call | solution.py:365
  404.5 102.2 %exit.1 = (f32[32,5120]{1,0:T(8,128)}, f32[32,3072]{1,0:T(8,128)}, f32[8,256]{1,0:T(8,128)}, f32[32,6144]{1,0:T(8,128)}, f32[8,768]{1,0:T(8,128)}, /*index=5*/f32[32,16,128]{2,1,0:T(8,128)}) custom-call(bf16[2,2,4,2,32,5120]{5,4,3,2,1,0:T(8,128)(2,1)} %bitcast.91, bf16[2,2,4,2,32,3072]{5,4,3,2,1,0:T(8,128)(2,1)} %bitcast.92, ...), custom_call_target="tpu_custom_call" | custom-call | tf_op jit(solution)/shard_map/exit/pallas_call | solution.py:715
  506.7 1.1 fusion.8
  507.8 1.6 slice.166
  509.4 1.3 slice_bitcast_fusion
  510.6 1.2 slice_bitcast_fusion.1
  511.8 1.2 slice_bitcast_fusion.3
  514.2 2.1 reshape.428
  (122 shorter events, 21.9 us)
Async XLA Ops:
  7.2 5.0 copy-start.9
  7.2 5.4 %copy-start.19 = (bf16[192]{0:T(256)(128)(2,1)S(1)}, bf16[192]{0:T(256)(128)(2,1)}, u32[]{:S(2)}) copy-start(bf16[192]{0:T(256)(128)(2,1)} %param.32) | copy-start | bytes 1156
  7.2 5.4 %copy-start.15 = (bf16[96]{0:T(256)(128)(2,1)S(1)}, bf16[96]{0:T(256)(128)(2,1)}, u32[]{:S(2)}) copy-start(bf16[96]{0:T(256)(128)(2,1)} %param.34) | copy-start | bytes 580
  7.2 5.4 %copy-start.16 = (bf16[32]{0:T(256)(128)(2,1)S(1)}, bf16[32]{0:T(256)(128)(2,1)}, u32[]{:S(2)}) copy-start(bf16[32]{0:T(256)(128)(2,1)} %param.36) | copy-start | bytes 196
  7.2 5.4 %copy-start.17 = (bf16[64]{0:T(256)(128)(2,1)S(1)}, bf16[64]{0:T(256)(128)(2,1)}, u32[]{:S(2)}) copy-start(bf16[64]{0:T(256)(128)(2,1)} %param.38) | copy-start | bytes 388
  7.2 5.4 %copy-start.18 = (bf16[32]{0:T(256)(128)(2,1)S(1)}, bf16[32]{0:T(256)(128)(2,1)}, u32[]{:S(2)}) copy-start(bf16[32]{0:T(256)(128)(2,1)} %param.40) | copy-start | bytes 196
  7.2 5.5 %copy-start.12 = (s32[1,512]{1,0:T(1,128)S(1)}, s32[1,512]{1,0:T(1,128)}, u32[]{:S(2)}) copy-start(s32[1,512]{1,0:T(1,128)} %param.28) | copy-start | bytes 6148
  7.3 5.6 %copy-start.13 = (s32[1,512]{1,0:T(1,128)S(1)}, s32[1,512]{1,0:T(1,128)}, u32[]{:S(2)}) copy-start(s32[1,512]{1,0:T(1,128)} %param.29) | copy-start | bytes 6148
  7.3 5.6 %copy-start.11 = (bf16[1,2,1024]{2,1,0:T(2,128)(2,1)S(1)}, bf16[1,2,1024]{2,1,0:T(2,128)(2,1)}, u32[]{:S(2)}) copy-start(bf16[1,2,1024]{2,1,0:T(2,128)(2,1)} %param.27) | copy-start | bytes 12292
  7.3 5.6 %copy-start = (bf16[32,6144]{1,0:T(8,128)(2,1)S(1)}, bf16[32,6144]{1,0:T(8,128)(2,1)}, u32[]{:S(2)}) copy-start(bf16[32,6144]{1,0:T(8,128)(2,1)} %refs_5_.1) | copy-start | bytes 1179652
  7.3 197.3 %all-gather.2.cloned.1.call-start = ((), (), s32[]{:S(2)}) async-start(), calls=%async_computation.4 | async-start | bytes 10813440 | tf_op jit(solution)/shard_map/all_gather | solution.py:739
  8.8 80.3 %copy-start.14 = (s32[1,512]{1,0:T(1,128)S(1)}, s32[1,512]{1,0:T(1,128)}, u32[]{:S(2)}) copy-start(s32[1,512]{1,0:T(1,128)} %param.30) | copy-start | bytes 6148
  84.8 0.6 copy-start.1
  85.4 2.7 copy-start.2
  103.1 40.7 %all-to-all-start = ((bf16[4,512,768]{2,1,0:T(8,128)(2,1)}), bf16[4,512,768]{2,1,0:T(8,128)(2,1)S(1)}, u32[]{:S(2)}, u32[]{:S(2)}) async-start(bf16[4,512,768]{2,1,0:T(8,128)(2,1)} %get-tuple-element.102), calls=%async_computation | async-start | bytes 6291456 | tf_op jit(solution)/shard_map/all_to_all | solution.py:752
  143.8 1.8 copy-start.3
  185.5 18.0 %all-to-all-start.1 = ((bf16[4,512,256]{2,1,0:T(8,128)(2,1)}), bf16[4,512,256]{2,1,0:T(8,128)(2,1)S(1)}, u32[]{:S(2)}, u32[]{:S(2)}) async-start(bf16[4,512,256]{2,1,0:T(8,128)(2,1)} %bitcast.95), calls=%async_computation.1 | async-start | bytes 2097152 | tf_op jit(solution)/shard_map/all_to_all | solution.py:758
  249.6 18.0 %all-to-all-start.2 = ((bf16[4,512,256]{2,1,0:T(8,128)(2,1)}), bf16[4,512,256]{2,1,0:T(8,128)(2,1)S(1)}, u32[]{:S(2)}, u32[]{:S(2)}) async-start(bf16[4,512,256]{2,1,0:T(8,128)(2,1)} %bitcast.78), calls=%async_computation.2 | async-start | bytes 2097152 | tf_op jit(solution)/shard_map/all_to_all | solution.py:761
  267.6 1.0 copy-start.4
  336.7 40.6 %all-to-all-start.3 = ((bf16[4,512,768]{2,1,0:T(8,128)(2,1)}), bf16[4,512,768]{2,1,0:T(8,128)(2,1)S(1)}, u32[]{:S(2)}, u32[]{:S(2)}) async-start(bf16[4,512,768]{2,1,0:T(8,128)(2,1)} %bitcast.90), calls=%async_computation.3 | async-start | bytes 6291456 | tf_op jit(solution)/shard_map/all_to_all | solution.py:758
  377.3 1.7 copy-start.5
  506.7 9.6 %copy-start.7 = (f32[32,3072]{1,0:T(8,128)S(1)}, f32[32,3072]{1,0:T(8,128)}, u32[]{:S(2)}) copy-start(f32[32,3072]{1,0:T(8,128)} %get-tuple-element.120) | copy-start | bytes 1179652
  514.2 4.5 copy-start.8
  514.2 5.3 %copy-start.10 = (f32[8,768]{1,0:T(8,128)S(1)}, f32[8,768]{1,0:T(8,128)}, u32[]{:S(2)}) copy-start(f32[8,768]{1,0:T(8,128)} %get-tuple-element.119) | copy-start | bytes 73732
  514.2 5.9 %copy-start.6 = (f32[32,6144]{1,0:T(8,128)S(1)}, f32[32,6144]{1,0:T(8,128)}, u32[]{:S(2)}) copy-start(f32[32,6144]{1,0:T(8,128)} %get-tuple-element.176) | copy-start | bytes 2359300
Sparse Core Ops, SparseCore 0:
  12.3 112.8 all-gather.1

commit v3 on v2

--- a/solution.py
+++ b/solution.py
@@ -565,156 +565,236 @@
         in_specs=[ANY]*(nw+1)+[V,ANY,V],out_specs=tuple([ANY]*(nw+2)+[V,V]),scratch_shapes=scr,
         compiler_params=pltpu.CompilerParams(collective_id=0,has_side_effects=True,vmem_limit_bytes=40*2**20),name="entry")(*shards,bias,time,ids,wada)
 
-class Scatter:
+class Reduce:
+    def __init__(self,p,parts,scr,own=None,src=None,col=0):
+        self.p,self.parts,self.src=p,parts,src
+        it=iter(scr)
+        self.own=own if own is not None else next(it)
+        self.c=p.c if own is not None else 0
+        self.w=self.own.shape[-1]; self.cs=pl.ds(col,self.w)
+        self.cin=next(it); self.c1,self.c2,self.ls=next(it),next(it),next(it)
+        self.bufs=[[(next(it),next(it),next(it)) for _ in o] for _,_,o in parts]
+        self.sent=[]; self.stage=0
     @staticmethod
-    def scratch(nd,ns,k,w,dt):
-        X,Y,Z=sizes(nd,ns); M=pltpu.VMEM; D=pltpu.SemaphoreType.DMA
-        h=w//2
-        return [M((X,Z,Y,k,w),dt),M((X,Z,Y,k,w),dt),M((Y,X,Z,k,h),dt),M((X,Z,Y,k,h),dt),M((X,Z,k,h),dt),M((Y,Z,k,h),dt),M((Z,k,w),dt)]+\
-            [D((X,)),D((X,)),D((X,)),D((Y,)),D((Y,)),D((X,)),D((X,)),D((X,)),D((X,)),D((Y,)),D((Y,)),D((Z,)),D((Z,))]
-    count=20
-    def __init__(self,p,src,col,w,scr):
-        self.p,self.src,self.w=p,src,w
-        self.cs=pl.ds(col,w); self.h=w//2
-        self.own,self.cin,self.ya,self.xb,self.xa,self.yb,self.zr=scr[:7]
-        self.ls,self.c1,self.c2,self.a1,self.a2,self.b1,self.b2,self.d1,self.d2,self.e1,self.e2,self.z1,self.z2=scr[7:]
-        self.A=pl.ds(0,self.h); self.B=pl.ds(self.h,self.h); self.sent=[]
+    def scratch(nd,ns,k,w,dt,parts,own):
+        X,Y,Z=sizes(nd,ns); M=pltpu.VMEM; D=pltpu.SemaphoreType.DMA; n={"x":X,"y":Y,"z":Z}
+        out=[] if own else [M((X,1,Z,Y,k,w),dt)]
+        out+=[M((X,Z,Y,k,w),dt),D((X,)),D((X,)),D((X,))]
+        for lo,hi,order in parts:
+            for i,a in enumerate(order):
+                left=tuple(n[b] for b in "xzy" if b in order[i+1:])
+                out+=[M((max(n[a]-1,1),)+left+(k,hi-lo),dt),D((n[a],)),D((n[a],))]
+        return out
     def start(self):
+        p=self.p; self.l=[]; self.cc=[]
+        for x in range(p.X):
+            s=self.own.at[x,1-p.c] if self.src is None else self.src.at[x,1-p.c,:,:,:,self.cs]
+            self.cc.append(remote(s,self.cin.at[x],self.c1.at[x],self.c2.at[x],p.at(c=1-p.c)))
+            if self.src is not None:
+                l=pltpu.make_async_copy(self.src.at[x,p.c,:,:,:,self.cs],self.own.at[x,0],self.ls.at[x]); l.start(); self.l.append(l)
+        self.sent+=self.cc
+    def place(self,order,i,v):
+        p=self.p; mine={"x":p.x,"y":p.y,"z":p.z}
+        ix={b:(mine[b] if b in order[:i] else v if b==order[i] else slice(None)) for b in "xyz"}
+        return (ix["x"],self.c,ix["z"],ix["y"])
+    def add(self,i,x,cols):
+        i=i+(slice(None),slice(*cols))
+        self.own[i]=(self.own[i].astype(f32)+x.astype(f32)).astype(self.own.dtype)
+    def send(self,part,i):
+        p=self.p; lo,hi,order=self.parts[part]; a=order[i]
+        n={"x":p.X,"y":p.Y,"z":p.Z}[a]; me={"x":p.x,"y":p.y,"z":p.z}[a]
+        buf,s1,s2=self.bufs[part][i]; out=[]
+        for d in near_first(n):
+            v=lax.rem(me+d,n)
+            out.append((d,remote(self.own.at[self.place(order,i,v)+(slice(None),pl.ds(lo,hi-lo))],buf.at[d-1],s1.at[d],s2.at[d],p.at(**{a:v}))))
+        self.sent+=[c for _,c in out]
+        return out
+    def step(self):
+        p=self.p; st=self.stage; self.stage+=1
+        if st==0:
+            for x in range(p.X):
+                if self.src is not None: self.l[x].wait()
+                self.cc[x].wait_recv()
+                @pl.loop(0,p.Z)
+                def _(z):
+                    for y in range(p.Y): self.add((x,self.c,z,y),self.cin[x,z,y],(0,self.w))
+            self.go=[self.send(k,0) for k in range(len(self.parts))]
+            return
+        go=[]
+        for k,(lo,hi,order) in enumerate(self.parts):
+            buf=self.bufs[k][st-1][0]; left=[b for b in "xzy" if b in order[st:]]
+            n={"x":p.X,"y":p.Y,"z":p.Z}; mine={"x":p.x,"y":p.y,"z":p.z}
+            for d,c in self.go[k]:
+                c.wait_recv()
+                def one(at,d=d):
+                    ix={**mine,**at}
+                    self.add((ix["x"],self.c,ix["z"],ix["y"]),buf[(d-1,)+tuple(at[b] for b in left)],(lo,hi))
+                if len(left)==2:
+                    @pl.loop(0,n[left[0]])
+                    def _(u):
+                        for v in range(n[left[1]]): one({left[0]:u,left[1]:v})
+                else:
+                    @pl.loop(0,n[left[0]])
+                    def _(u): one({left[0]:u})
+            go.append(self.send(k,st))
+        self.go=go
+    def last(self,out,col=0):
         p=self.p
-        self.l=[];self.cc=[]
-        for x in range(p.X):
-            self.cc.append(remote(self.src.at[x,1-p.c,:,:,:,self.cs],self.cin.at[x],self.c1.at[x],self.c2.at[x],p.at(c=1-p.c)))
-            l=pltpu.make_async_copy(self.src.at[x,p.c,:,:,:,self.cs],self.own.at[x],self.ls.at[x]); l.start(); self.l.append(l)
-        self.sent+=self.cc
-    def add(self,i,x,cols):
-        self.own[i+(slice(None),cols)]=(self.own[i+(slice(None),cols)].astype(f32)+x.astype(f32)).astype(self.own.dtype)
-    def second(self):
-        p=self.p
-        for x in range(p.X):
-            self.l[x].wait(); self.cc[x].wait_recv()
-            @pl.loop(0,p.Z)
-            def _(z):
-                for y in range(p.Y):
-                    self.add((x,z,y),self.cin[x,z,y],slice(None))
-        self.a=[];self.b=[]
-        for dy in near_first(p.Y):
-            y=lax.rem(p.y+dy,p.Y)
-            self.a.append((dy,remote(self.own.at[:,:,y,:,self.A],self.ya.at[dy],self.a1.at[dy],self.a2.at[dy],p.at(y=y))))
-        for dx in near_first(p.X):
-            x=lax.rem(p.x+dx,p.X)
-            self.b.append((dx,remote(self.own.at[x,:,:,:,self.B],self.xb.at[dx],self.b1.at[dx],self.b2.at[dx],p.at(x=x))))
-        self.sent+=[c for _,c in self.a+self.b]
-    def third(self):
-        p=self.p
-        for dy,c in self.a:
-            c.wait_recv()
-            @pl.loop(0,p.Z)
-            def _(z):
-                for x in range(p.X): self.add((x,z,p.y),self.ya[dy,x,z],slice(0,self.h))
-        for dx,c in self.b:
-            c.wait_recv()
-            @pl.loop(0,p.Z)
-            def _(z):
-                for y in range(p.Y): self.add((p.x,z,y),self.xb[dx,z,y],slice(self.h,self.w))
-        self.a=[];self.b=[]
-        for dx in near_first(p.X):
-            x=lax.rem(p.x+dx,p.X)
-            self.a.append((dx,remote(self.own.at[x,:,p.y,:,self.A],self.xa.at[dx],self.d1.at[dx],self.d2.at[dx],p.at(x=x))))
-        for dy in near_first(p.Y):
-            y=lax.rem(p.y+dy,p.Y)
-            self.b.append((dy,remote(self.own.at[p.x,:,y,:,self.B],self.yb.at[dy],self.e1.at[dy],self.e2.at[dy],p.at(y=y))))
-        self.sent+=[c for _,c in self.a+self.b]
-    def fourth(self):
-        p=self.p
-        for dx,c in self.a:
-            c.wait_recv()
-            for z in range(p.Z): self.add((p.x,z,p.y),self.xa[dx,z],slice(0,self.h))
-        for dy,c in self.b:
-            c.wait_recv()
-            for z in range(p.Z): self.add((p.x,z,p.y),self.yb[dy,z],slice(self.h,self.w))
-        self.zc=[]
-        for dz in near_first(p.Z):
-            z=lax.rem(p.z+dz,p.Z)
-            self.zc.append((dz,remote(self.own.at[p.x,z,p.y],self.zr.at[dz],self.z1.at[dz],self.z2.at[dz],p.at(z=z))))
-        self.sent+=[c for _,c in self.zc]
-    def last(self,out,cols):
-        p=self.p
-        t=self.own[p.x,p.z,p.y].astype(f32)
-        for dz,c in self.zc:
-            c.wait_recv()
-            t=t+self.zr[dz].astype(f32)
-        out[:,cols]=t
+        for k,(lo,hi,order) in enumerate(self.parts):
+            buf=self.bufs[k][2][0]
+            t=self.own[p.x,self.c,p.z,p.y,:,lo:hi].astype(f32)
+            for d,c in self.go[k]:
+                c.wait_recv()
+                t=t+buf[d-1].astype(f32)
+            out[:,col+lo:col+hi]=t
     def finish(self):
         for c in self.sent: c.wait_send()
 
-def exit_kernel(nd,ns,plan,*refs):
-    na=max(a for a,_,_ in plan)+1
-    srcs=refs[:na]; ge,act,wada=refs[na:na+3]
-    outs=refs[na+3:2*na+3]; gada,gbada,dact=refs[2*na+3:2*na+6]
-    hsum,demb,dscr,hs,hr,qs,qr,ds_,dr=refs[2*na+6:2*na+15]
-    sc=refs[2*na+15:]
-    p=Place(nd,ns); me=p.h*ns+p.s
-    greet_all(p)
-    hsum[p.h]=ge[...]
-    hc=[remote(hsum.at[p.h],hsum.at[p.h],hs.at[dh],hr.at[dh],(lax.rem(p.h+dh,nd),p.s)) for dh in range(1,nd)]
-    it=[Scatter(p,srcs[a],c,w,sc[i*Scatter.count:(i+1)*Scatter.count]) for i,(a,c,w) in enumerate(plan)]
-    for s in it: s.start()
-    n=len(it); E=ge.shape[1]; K=wada.shape[0]; R=ns*16
-    qc=[]
-    for t in range(n+3):
-        if t<n: it[t].second()
-        if 0<=t-1<n: it[t-1].third()
-        if 0<=t-2<n: it[t-2].fourth()
-        if 0<=t-3<n: it[t-3].last(outs[plan[t-3][0]],slice(plan[t-3][1],plan[t-3][1]+plan[t-3][2]))
-        if t==0:
-            for c in hc: c.wait()
-            tot=hsum[0]
-            for i in range(1,nd): tot=tot+hsum[i]
-            demb[p.s]=tot.astype(bf)
-            qc=[remote(demb.at[p.s],demb.at[p.s],qs.at[d],qr.at[d],(p.h,lax.rem(p.s+d,ns))) for d in range(1,ns)]
-        if t==1:
-            for c in qc: c.wait()
-            flat=demb[...].reshape(R,E)
-            r0=lax.broadcasted_iota(jnp.int32,(R,ns*8),0); c0=lax.broadcasted_iota(jnp.int32,(R,ns*8),1)
-            spread=dot(jnp.where((r0//16==c0//8)&(r0%2==c0%8),1.0,0.0).astype(bf),act[...])
-            rr=lax.broadcasted_iota(jnp.int32,(R,128),0)%16//2
-            rk=lax.broadcasted_iota(jnp.int32,(R,K),0)%16//2
-            tot=jnp.zeros((R,K),f32)
-            for j in range(8):
-                m=jnp.where(rr==j,spread,0.0).astype(bf)
-                gada[:,j*E:(j+1)*E]=dot(m,flat,TN)[:K,:]
-                tot=jnp.where(rk==j,dot(flat,wada[:,j*E:(j+1)*E],NT),tot)
-            r8=lax.broadcasted_iota(jnp.int32,(8,R),0); c8=lax.broadcasted_iota(jnp.int32,(8,R),1)
-            gbada[...]=dot(jnp.where(c8%16//2==r8,1.0,0.0).astype(bf),flat)
-            dscr[...]=jnp.concatenate([tot,jnp.zeros((R,128-K),f32)],1).reshape(ns,16,128)
-            dact[me]=dscr[p.s]
-            @pl.loop(0,nd)
-            def _(dh):
-                @pl.loop(0,ns)
-                def _(d):
-                    @pl.when(dh+d>0)
-                    def _():
-                        s=lax.rem(p.s+d,ns)
-                        remote(dscr.at[s],dact.at[me],ds_.at[dh,d],dr.at[dh,d],(lax.rem(p.h+dh,nd),s))
-    for s in it: s.finish()
-    @pl.loop(0,nd)
+def everyone(p,f):
+    @pl.loop(0,p.nd)
     def _(dh):
-        @pl.loop(0,ns)
+        @pl.loop(0,p.ns)
         def _(d):
             @pl.when(dh+d>0)
-            def _():
-                s=lax.rem(p.s+d,ns)
-                pltpu.make_async_remote_copy(src_ref=dscr.at[s],dst_ref=dact.at[me],send_sem=ds_.at[dh,d],recv_sem=dr.at[dh,d],device_id=(lax.rem(p.h+dh,nd),s),device_id_type=pl.DeviceIdType.MESH).wait()
-
-def exit_(nd,ns,srcs,plan,ge,act,wada):
-    S=jax.ShapeDtypeStruct; D=pltpu.SemaphoreType.DMA
-    E=ge.shape[1]; K,E6=wada.shape
-    outs=[S(a.shape[-2:],f32) for a in srcs]+[S((K,E6),f32),S((8,E),f32),S((nd*ns,16,128),f32)]
-    scr=[pltpu.VMEM((nd,16,E),f32),pltpu.VMEM((ns,16,E),bf),pltpu.VMEM((ns,16,128),f32),D((nd,)),D((nd,)),D((ns,)),D((ns,)),D((nd,ns)),D((nd,ns))]
-    for a,c,w in plan: scr+=Scatter.scratch(nd,ns,srcs[a].shape[-2],w,srcs[a].dtype)
-    return pl.pallas_call(functools.partial(exit_kernel,nd,ns,tuple(plan)),out_shape=tuple(outs),
-        in_specs=[ANY]*len(srcs)+[V]*3,out_specs=tuple([V]*len(outs)),scratch_shapes=scr,
-        compiler_params=pltpu.CompilerParams(collective_id=1,has_side_effects=True,vmem_limit_bytes=60*2**20),name="exit")(*srcs,ge,act,wada)
+            def _(): f(dh,d,(lax.rem(p.h+dh,p.nd),lax.rem(p.s+d,p.ns)))
+
+def make_remote(src,dst,ss,rs,dev):
+    return pltpu.make_async_remote_copy(src_ref=src,dst_ref=dst,send_sem=ss,recv_sem=rs,device_id=dev,device_id_type=pl.DeviceIdType.MESH)
+
+REST=(lambda w:((0,w,"yzx"),)); QKV=(lambda w:((0,w//2,"yxz"),(w//2,w,"xyz")))
+
+def final_kernel(nd,ns,R,refs,scr):
+    (g_ref,rest_ref,x_hbm,n1_hbm,dm_hbm,wq_hbm,cos_ref,sin_ref,seg_ref,emb_ref,gbm_ref,gem_ref,act,wada)=refs[:14]
+    (gf_ref,rest_out,qkv_out,bias_all,gada,gbada,dact)=refs[14:]
+    (g,x_ref,n1_ref,dm_ref,w_ref,dps,gw,gbv,gev,bsc,bout,hsum,demb,dscr)=scr[:14]
+    (gs,gr,gl,ld,hs,hr,qs,qr,ds_,dr,bs,br)=scr[14:26]
+    pools=scr[26:]
+    p=Place(nd,ns); me=p.h*ns+p.s
+    F,D=x_ref.shape; W=D//nd; E=D*6//8; K=wada.shape[0]; H=gbm_ref.shape[1]; NR=F//R
+    nr=(2*H+D)//D
+    greet_all(p)
+    loads=[pltpu.make_async_copy(a,b,ld.at[i]) for i,(a,b) in enumerate(((x_hbm,x_ref),(wq_hbm,w_ref),(dm_hbm,dm_ref),(n1_hbm,n1_ref)))]
+    sends=[]; own=[]
+    for i in range(NR):
+        r=pl.ds(i*R,R)
+        sends.append([remote(g_ref.at[lax.rem(p.h+d,nd),r],g.at[p.h,r],gs.at[i,d],gr.at[i,d],(lax.rem(p.h+d,nd),p.s)) for d in range(1,nd)])
+        c=pltpu.make_async_copy(g_ref.at[p.h,r],g.at[p.h,r],gl.at[i]); c.start(); own.append(c)
+    for l in loads: l.start()
+    it=iter(pools)
+    take=lambda n: [next(it) for _ in range(n)]
+    rest=[]
+    for j in range(nr):
+        rest.append(Reduce(p,REST(D),take(len(Reduce.scratch(nd,ns,K,D,bf,REST(D),False))),src=rest_ref,col=j*D))
+        rest[-1].start()
+    qkv=[Reduce(p,QKV(D),take(len(Reduce.scratch(nd,ns,K,D,bf,QKV(D),True))),own=gw.at[j]) for j in range(3)]
+    bias=Reduce(p,QKV(256),take(len(Reduce.scratch(nd,ns,8,256,f32,QKV(256),True))),own=bsc)
+    gbv[...]=jnp.zeros_like(gbv); gev[...]=jnp.zeros_like(gev); bsc[...]=jnp.zeros_like(bsc)
+    for a in rest: a.step()
+    for l in loads: l.wait()
+    def tile(i):
+        for c in sends[i]: c.wait_recv()
+        own[i].wait()
+        r=slice(i*R,(i+1)*R)
+        seg=seg_ref[r,:]
+        cos=jnp.concatenate([cos_ref[r,:]]*(W//128),1); sin=jnp.concatenate([sin_ref[r,:]]*(W//128),1)
+        dn=jnp.zeros((R,D),f32)
+        for d in range(nd):
+            for j in range(3):
+                c=(d*3+j)*W
+                v=g[d,r,j*W:(j+1)*W]
+                if j<2:
+                    v=v.astype(f32)
+                    v=(v*cos-partner(v)*sin).astype(bf)
+                dps[r,c:c+W]=v
+                gbv[0:1,c:c+W]+=jnp.sum(v.astype(f32),0,keepdims=True)
+        for j in range(3*D//512):
+            dn+=dot(dps[r,j*512:(j+1)*512],w_ref[:,j*512:(j+1)*512],NT)
+        n,rs=moments(x_ref[r,:].astype(f32))
+        for k,x in ((0,dn),(1,dn*n)):
+            a,b=sums(x,seg)
+            gev[0:1,k*D:(k+1)*D]+=a; gev[1:2,k*D:(k+1)*D]+=b
+        dn=dn*(1.0+pick(seg,emb_ref,1,D))
+        gf_ref[r,:]=dm_ref[r,:]+(dn-jnp.mean(dn,-1,keepdims=True)-n*jnp.mean(dn*n,-1,keepdims=True))*rs
+    def weight(j):
+        B=D//nd
+        for h in range(nd):
+            v=dot(n1_ref[:,h*B:(h+1)*B],dps[:,j*D:(j+1)*D],TN).astype(bf)
+            gw[j,h//2,h%2]=v.reshape(p.Z,p.Y,K,D)
+        qkv[j].start()
+    todo=[a.step for a in rest]+[a.step for a in rest]
+    per=-(-len(todo)//NR)
+    for i in range(NR):
+        tile(i)
+        if i<NR-1:
+            for f in todo[i*per:(i+1)*per]: f()
+    gev[0:2,2*D:]=gem_ref[0:2,:]
+    for j in range(8):
+        for t in range(2): hsum[p.h,2*j+t:2*j+t+1,:]=gev[t:t+1,j*E:(j+1)*E]
+    hc=[remote(hsum.at[p.h],hsum.at[p.h],hs.at[d],hr.at[d],(lax.rem(p.h+d,nd),p.s)) for d in range(1,nd)]
+    vec=jnp.concatenate([gbv[0:1,:],gbm_ref[0:1,0:D],gbm_ref[1:2,:],gbm_ref[2:3,0:D]],1)
+    for q in range(vec.shape[1]//256):
+        h,s=divmod(q,ns)
+        bsc[h//2,h%2,s//p.Y,s%p.Y,0:1,:]=vec[:,q*256:(q+1)*256]
+    bias.start()
+    weight(0)
+    weight(1)
+    qkv[0].step(); bias.step()
+    weight(2)
+    qkv[1].step(); qkv[2].step()
+    for f in todo[(NR-1)*per:]: f()
+    bias.step()
+    for c in hc: c.wait()
+    tot=hsum[0]
+    for i in range(1,nd): tot=tot+hsum[i]
+    demb[p.s]=tot.astype(bf)
+    qc=[remote(demb.at[p.s],demb.at[p.s],qs.at[d],qr.at[d],(p.h,lax.rem(p.s+d,ns))) for d in range(1,ns)]
+    qkv[0].step(); bias.step()
+    qkv[1].step()
+    qkv[2].step()
+    for j,a in enumerate(rest): a.last(rest_out,j*D)
+    bias.last(bout)
+    everyone(p,lambda dh,d,dev: remote(bout,bias_all.at[me],bs.at[dh,d],br.at[dh,d],dev))
+    bias_all[me]=bout[...]
+    for c in qc: c.wait()
+    Q=ns*16
+    flat=demb[...].reshape(Q,E)
+    r0=lax.broadcasted_iota(jnp.int32,(Q,ns*8),0); c0=lax.broadcasted_iota(jnp.int32,(Q,ns*8),1)
+    spread=dot(jnp.where((r0//16==c0//8)&(r0%2==c0%8),1.0,0.0).astype(bf),act[...])
+    rr=lax.broadcasted_iota(jnp.int32,(Q,128),0)%16//2
+    rk=lax.broadcasted_iota(jnp.int32,(Q,K),0)%16//2
+    tot=jnp.zeros((Q,K),f32)
+    for j in range(8):
+        m=jnp.where(rr==j,spread,0.0).astype(bf)
+        gada[:,j*E:(j+1)*E]=dot(m,flat,TN)[:K,:]
+        tot=jnp.where(rk==j,dot(flat,wada[:,j*E:(j+1)*E],NT),tot)
+    dscr[...]=jnp.concatenate([tot,jnp.zeros((Q,128-K),f32)],1).reshape(ns,16,128)
+    dact[me]=dscr[p.s]
+    everyone(p,lambda dh,d,dev: remote(dscr.at[dev[1]],dact.at[me],ds_.at[dh,d],dr.at[dh,d],dev))
+    r8=lax.broadcasted_iota(jnp.int32,(8,Q),0); c8=lax.broadcasted_iota(jnp.int32,(8,Q),1)
+    gbada[...]=dot(jnp.where(c8%16//2==r8,1.0,0.0).astype(bf),flat)
+    for a in qkv: a.step()
+    for j in range(3): qkv[j].last(qkv_out,j*D)
+    for a in rest+qkv+[bias]: a.finish()
+    for i in range(NR):
+        for c in sends[i]: c.wait_send()
+    everyone(p,lambda dh,d,dev: make_remote(bout,bias_all.at[me],bs.at[dh,d],br.at[dh,d],dev).wait())
+    everyone(p,lambda dh,d,dev: make_remote(dscr.at[dev[1]],dact.at[me],ds_.at[dh,d],dr.at[dh,d],dev).wait())
+
+def final(nd,ns,dqkv,rest,x,n1,dm,wq,cos,sin,seg,emb,gb,ge,act,wada,R=128):
+    F,D=x.shape; K,E6=wada.shape; E=E6//8; H=gb.shape[1]; N=nd*ns; W=D//nd; NR=F//R
+    X,Y,Z=sizes(nd,ns)
+    S=jax.ShapeDtypeStruct; M=pltpu.VMEM; A=pltpu.SemaphoreType.DMA
+    outs=[S((F,D),f32),S((K,2*H+D),f32),S((K,3*D),f32),S((N,8,256),f32),S((K,E6),f32),S((8,E),f32),S((N,16,128),f32)]
+    scr=[M((nd,F,3*W),bf),M((F,D),bf),M((F,D),bf),M((F,D),f32),M((D,3*D),bf),M((F,3*D),bf),M((3,X,2,Z,Y,K,D),bf),M((8,3*D),f32),M((8,E6),f32),
+         M((X,2,Z,Y,8,256),f32),M((8,256),f32),M((nd,16,E),f32),M((ns,16,E),bf),M((ns,16,128),f32),
+         A((NR,nd)),A((NR,nd)),A((NR,)),A((4,)),A((nd,)),A((nd,)),A((ns,)),A((ns,)),A((nd,ns)),A((nd,ns)),A((nd,ns)),A((nd,ns))]
+    for _ in range((2*H+D)//D): scr+=Reduce.scratch(nd,ns,K,D,bf,REST(D),False)
+    for _ in range(3): scr+=Reduce.scratch(nd,ns,K,D,bf,QKV(D),True)
+    scr+=Reduce.scratch(nd,ns,8,256,f32,QKV(256),True)
+    def k(*refs): final_kernel(nd,ns,R,refs[:14+len(outs)],refs[14+len(outs):])
+    return pl.pallas_call(k,out_shape=tuple(outs),in_specs=[ANY]*6+[V]*8,out_specs=(V,)*len(outs),scratch_shapes=scr,
+        compiler_params=pltpu.CompilerParams(collective_id=1,has_side_effects=True,vmem_limit_bytes=63*2**20),name="final")(
+        dqkv,rest,x,n1,dm,wq,cos,sin,seg,emb,gb,ge,act,wada)
 
 
 def body(frames,time_embed,segment_ids,frame_mask,positions,w_ada,b_ada,w_qkv,b_qkv,w_out,b_out,w_up,b_up,w_down,b_down,cotangent):
@@ -760,19 +840,17 @@
     out,dmid,datt,grest,gb,ge=mid(x,att,cot,segc,mskc,emb,rest_all,bo,bu,bd)
     do=lax.all_to_all(datt.reshape(F,nd,W).transpose(1,0,2),"head",split_axis=0,concat_axis=0,tiled=True).reshape(nd*F,W)
     dqkv=attn_bwd(qkv,o,do,lse,klo,khi,aq,ak,T)
-    gx,gqkv,gbq,ge1=tail(x,normed,dmid,back(dqkv),segc,emb,wq,cos,sin)
-    shape=(X,2,Z,Y,K)
-    gbias=jnp.concatenate([restore(gbq[0:1]).reshape(N,-1),gb[0,:D].reshape(N,-1),unhide(gb[1:2]).reshape(N,-1),gb[2,:D].reshape(N,-1)],axis=1)
-    wide=-(-ends[4]//256)*256
-    gbias=jnp.zeros((N,8,wide),f32).at[:,0,:ends[4]].set(gbias).reshape(X,2,Z,Y,8,wide)
-    ge=jnp.concatenate([ge1[:2],ge[:2]],axis=1).reshape(2,8,-1).transpose(1,0,2).reshape(16,-1)
-    plan=[(0,j*D,D) for j in range(2*nt+1)]+[(2,0,wide)]+[(1,j*D,D) for j in range(3)]
-    grest,gqkv,gbias,gada,gbada,dact=exit_(nd,ns,[grest.reshape(shape+(2*H+D,)),gqkv.reshape(shape+(3*D,)),gbias],plan,ge,act,w_ada)
+    gx,grest,gqkv,gbias,gada,gbada,dact=final(nd,ns,dqkv.reshape(nd,F,3*W),grest.reshape(X,2,Z,Y,K,2*H+D),x,normed,dmid,wq,cos,sin,segc,emb,gb,ge,act,w_ada)
     dact=dact[:,:,:K].reshape(N,8,2,K).sum(1).transpose(1,0,2).reshape(2,D)
     _,pull=jax.vjp(jax.nn.silu,time_embed[0].astype(f32))
     gtime=pull(dact)[0][None]
     gbada=lax.dynamic_slice_in_dim(gbada.reshape(-1),dev*E,E,0)
-    gbs=[gbias[0,ends[i]:ends[i+1]] for i in range(4)]
+    gbias=gbias[:,0,:].reshape(-1)
+    gbs=[]; at=0
+    for k,order in ((3*D,restore),(D,None),(H,unhide),(D,None)):
+        v=gbias[at:at+k]; at+=k
+        if order: v=order(v[None])[0]
+        gbs.append(lax.dynamic_slice_in_dim(v,dev*(k//N),k//N,0))
     gdown=grest[:,H:2*H].reshape(K,nt,D).transpose(1,0,2).reshape(nt*K,D)
     return (out[None],gx[None],gtime,gada,gbada,restore(gqkv),gbs[0],grest[:,2*H:],gbs[1],unhide(grest[:,:H]),gbs[2],gdown,gbs[3])
 

time: 534 us -> 532 us (level)
  waiting for transfers between devices: 91.5 us -> 58 us
  Pallas kernels: 358 us -> 391 us
    all_to_all x2 -> x1, waiting for transfers between devices: 44.9 us -> 11.3 us  [back(): lax.all_to_all(a.reshape(nd, F, -1), 'head', split_axis=0, concat_axis=0,...]
    pallas_call x2 -> x1, Pallas kernels: 124 us -> 158 us  [final(): pl.pallas_call(k, out_shape=tuple(outs), in_specs=[ANY] * 6 + [V] * 8, ou...]
  transfers between devices with their start and end apart: 5 -> 4, of which waited for: 4 -> 3; matrix products, arithmetic and copies ran while one was open for 3% -> 3% of each run, Pallas kernels for 23% -> 23%
where the time goes in v3:
time: 532 us; the launch traced here: 524 us
  Pallas kernels  391 us (73%)
  waiting for transfers between devices  58 us (11%)
  local copies, waits for them, and re-layouts  38.4 us (7%)
  between operations  14.8 us (3%)
  starting transfers between devices  11.5 us (2%)
  other arithmetic  10.6 us (2%)
    pallas_call x1, Pallas kernels, final(): pl.pallas_call(k, out_shape=tuple(outs), in_specs=[ANY] * 6 + [V] * 8, ou...  158 us
    pallas_call x1, Pallas kernels, entry(): pl.pallas_call(functools.partial(entry_kernel, nd, ns, nw), out_shape=tup...  71.8 us
    pallas_call x1, Pallas kernels, attn_bwd(): pl.pallas_call(functools.partial(bwd_kernel, T=T, nh=nh), out_shape=jax.S...  68.1 us
    pallas_call x1, Pallas kernels, mid(): pl.pallas_call(functools.partial(mid_kernel, R=R), out_shape=(S((F, D), b...  42.7 us
    pallas_call x1, Pallas kernels, attn_fwd(): pl.pallas_call(functools.partial(fwd_kernel, T=T, nh=nh), out_shape=(jax....  40 us
    all_to_all x1, waiting for transfers between devices, body(): lax.all_to_all(packed, 'head', split_axis=0, concat_axis=0, tiled=True)  32.8 us
    all_to_all x1, waiting for transfers between devices, body(): lax.all_to_all(datt.reshape(F, nd, W).transpose(1, 0, 2), 'head', split_a...  13.9 us
    all_to_all x1, waiting for transfers between devices, back(): lax.all_to_all(a.reshape(nd, F, -1), 'head', split_axis=0, concat_axis=0,...  11.3 us
  transfers between devices with their start and end apart: 4, of which 3 were waited for; matrix products, arithmetic and copies ran while one was open for 3% of the time, Pallas kernels for 23%

profile of v3, /device:TPU:0, one launch (start us, length us, event | category | flops | bytes accessed | tf_op | source)
XLA Modules:
  0.0 524.3 jit_solution(16518142962664031039)
XLA Ops:
  7.3 1.4 reshape.356
  9.4 1.0 copy.124
  10.5 1.6 pad_maximum_fusion
  12.9 71.8 %entry.1 = (bf16[2,2,4,2,32,3072]{5,4,3,2,1,0:T(8,128)(2,1)S(1)}, bf16[32,16,512]{2,1,0:T(8,128)(2,1)S(1)}, s32[4,8,512]{2,1,0:T(8,128)S(1)}, f32[16,768]{1,0:T(8,128)S(1)}, bf16[64,128]{1,0:T(8,128)(2,1)S(1)}) custom-call(bf16[32,3072]{1,0:T(8,128)(2,1)S(1)} %reshape.347.refs_0_, bf16[16,512]{1,0:T(8,128)(2,1)S(1)} %scatter.16.refs_1_, ...), custom_call_target="tpu_custom_call" | custom-call | tf_op jit(solution)/shard_map/entry/pallas_call | solution.py:564
  84.8 2.6 copy-done
  89.9 1.8 negate_select_fusion
  92.4 10.6 %qkv_proj.1 = (bf16[512,1024]{1,0:T(8,128)(2,1)}, bf16[4,512,768]{2,1,0:T(8,128)(2,1)}) custom-call(bf16[512,1024]{1,0:T(8,128)(2,1)} %bitcast.93, s32[512,1]{1,0:T(8,128)} %copy.121.seg_ref.refs_8_, f32[2,6144]{1,0:T(2,128)} %broadcast_add_fusion.emb_ref.refs_9_, bf16[1024,3072]{1,0:T(8,128)(2,1)} %bitcast.80, f32[1,3072]{1,0:T(1,128)} %reshape.352.b_ref, ...), custom_call_target="tpu_custom_call" | custom-call | flops 3221225472 | bytes 14680064 | tf_op jit(solution)/shard_map/qkv_proj/pallas_call | solution.py:249
  103.0 3.7 all-to-all-start
  108.3 2.7 select_convert_fusion
  111.1 32.8 %all-to-all-done = bf16[4,512,768]{2,1,0:T(8,128)(2,1)S(1)} async-done(((bf16[4,512,768]{2,1,0:T(8,128)(2,1)}), bf16[4,512,768]{2,1,0:T(8,128)(2,1)S(1)}, u32[]{:S(2)}, u32[]{:S(2)}) %all-to-all-start) | async-done | bytes 3145760 | tf_op jit(solution)/shard_map/all_to_all | solution.py:832
  143.9 1.8 copy-done.3
  145.6 40.0 %attn_fwd.1 = (bf16[2048,256]{1,0:T(8,128)(2,1)}, f32[2048,128]{1,0:T(8,128)}) custom-call(s32[8]{0:T(128)} %get-tuple-element.115.lo_ref, s32[8]{0:T(128)} %broadcast_add_fusion.2.hi_ref, bf16[2048,768]{1,0:T(8,128)(2,1)} %bitcast.82, bf16[2048,128]{1,0:T(8,128)(2,1)} %get-tuple-element.133.auxq_ref, bf16[2048,128]{1,0:T(8,128)(2,1)} %get-tuple-element.132.auxk_ref), custom_call_target="tpu_custom_call" | custom-call | tf_op jit(solution)/shard_map/attn_fwd/pallas_call | solution.py:93
  185.6 4.0 all-to-all-start.1
  192.7 11.3 %all-to-all-done.1 = bf16[4,512,256]{2,1,0:T(8,128)(2,1)S(1)} async-done(((bf16[4,512,256]{2,1,0:T(8,128)(2,1)}), bf16[4,512,256]{2,1,0:T(8,128)(2,1)S(1)}, u32[]{:S(2)}, u32[]{:S(2)}) %all-to-all-start.1) | async-done | bytes 1048608 | tf_op jit(solution)/shard_map/all_to_all | solution.py:838
  204.0 1.1 copy.138
  205.2 42.7 %mid.1 = (bf16[512,1024]{1,0:T(8,128)(2,1)}, f32[512,1024]{1,0:T(8,128)}, bf16[512,1024]{1,0:T(8,128)(2,1)}, bf16[1024,5120]{1,0:T(8,128)(2,1)}, f32[8,2048]{1,0:T(8,128)}, /*index=5*/f32[8,4096]{1,0:T(8,128)}) custom-call(bf16[512,1024]{1,0:T(8,128)(2,1)} %bitcast.94, bf16[512,1024]{1,0:T(8,128)(2,1)} %bitcast.97, bf16[512,1024]{1,0:T(8,128)(2,1)} %bitcast.132, ...), custom_call_target="tpu_custom_call" | custom-call | flops 16106127360 | bytes 31457280 | tf_op jit(solution)/shard_map/mid/pallas_call | solution.py:323
  247.9 2.3 copy.151
  250.2 3.7 all-to-all-start.2
  254.4 13.9 %all-to-all-done.2 = bf16[4,512,256]{2,1,0:T(8,128)(2,1)S(1)} async-done(((bf16[4,512,256]{2,1,0:T(8,128)(2,1)}), bf16[4,512,256]{2,1,0:T(8,128)(2,1)S(1)}, u32[]{:S(2)}, u32[]{:S(2)}) %all-to-all-start.2) | async-done | bytes 1048608 | tf_op jit(solution)/shard_map/all_to_all | solution.py:841
  268.3 1.0 copy-done.4
  269.3 68.1 %attn_bwd.1 = bf16[2048,768]{1,0:T(8,128)(2,1)} custom-call(s32[8]{0:T(128)} %get-tuple-element.114.lo_ref, s32[8]{0:T(128)} %broadcast_add_fusion.1.hi_ref, bf16[2048,768]{1,0:T(8,128)(2,1)} %bitcast.83, bf16[2048,256]{1,0:T(8,128)(2,1)} %get-tuple-element.88.o_ref, bf16[2048,256]{1,0:T(8,128)(2,1)} %bitcast.89, f32[2048,128]{1,0:T(8,128)} %get-tuple-element.91.lse_ref, ...), custom_call_target="tpu_custom_call" | custom-call | tf_op jit(solution)/shard_map/attn_bwd/pallas_call | solution.py:177
  337.4 157.8 %final.1 = (f32[512,1024]{1,0:T(8,128)}, f32[32,5120]{1,0:T(8,128)}, f32[32,3072]{1,0:T(8,128)}, f32[32,8,256]{2,1,0:T(8,128)}, f32[32,6144]{1,0:T(8,128)}, /*index=5*/f32[8,768]{1,0:T(8,128)}, f32[32,16,128]{2,1,0:T(8,128)}) custom-call(bf16[4,512,768]{2,1,0:T(8,128)(2,1)} %bitcast.84, bf16[2,2,4,2,32,5120]{5,4,3,2,1,0:T(8,128)(2,1)} %bitcast.85, ...), custom_call_target="tpu_custom_call" | custom-call | tf_op jit(solution)/shard_map/final/pallas_call | solution.py:795
  495.2 1.1 fusion.8
  496.3 1.6 slice.132
  497.9 1.5 slice_reduce_fusion
  500.2 1.4 fusion.9
  502.8 2.1 reshape.373
  505.2 0.9 reshape.371
  508.1 1.1 reduce_sum.9
  510.7 1.3 dynamic_slice.17
  511.9 1.3 dynamic_slice.19
  515.0 1.3 copy.163
  (107 shorter events, 18.2 us)
Async XLA Ops:
  7.2 5.0 copy-start.8
  7.2 5.4 %copy-start.17 = (bf16[192]{0:T(256)(128)(2,1)S(1)}, bf16[192]{0:T(256)(128)(2,1)}, u32[]{:S(2)}) copy-start(bf16[192]{0:T(256)(128)(2,1)} %param.30) | copy-start | bytes 1156
  7.2 5.4 %copy-start.13 = (bf16[96]{0:T(256)(128)(2,1)S(1)}, bf16[96]{0:T(256)(128)(2,1)}, u32[]{:S(2)}) copy-start(bf16[96]{0:T(256)(128)(2,1)} %param.32) | copy-start | bytes 580
  7.2 5.4 %copy-start.14 = (bf16[32]{0:T(256)(128)(2,1)S(1)}, bf16[32]{0:T(256)(128)(2,1)}, u32[]{:S(2)}) copy-start(bf16[32]{0:T(256)(128)(2,1)} %param.34) | copy-start | bytes 196
  7.2 5.4 %copy-start.15 = (bf16[64]{0:T(256)(128)(2,1)S(1)}, bf16[64]{0:T(256)(128)(2,1)}, u32[]{:S(2)}) copy-start(bf16[64]{0:T(256)(128)(2,1)} %param.36) | copy-start | bytes 388
  7.2 5.4 %copy-start.16 = (bf16[32]{0:T(256)(128)(2,1)S(1)}, bf16[32]{0:T(256)(128)(2,1)}, u32[]{:S(2)}) copy-start(bf16[32]{0:T(256)(128)(2,1)} %param.38) | copy-start | bytes 196
  7.2 5.5 %copy-start.10 = (s32[1,512]{1,0:T(1,128)S(1)}, s32[1,512]{1,0:T(1,128)}, u32[]{:S(2)}) copy-start(s32[1,512]{1,0:T(1,128)} %param.26) | copy-start | bytes 6148
  7.3 5.6 %copy-start.11 = (s32[1,512]{1,0:T(1,128)S(1)}, s32[1,512]{1,0:T(1,128)}, u32[]{:S(2)}) copy-start(s32[1,512]{1,0:T(1,128)} %param.27) | copy-start | bytes 6148
  7.3 5.6 %copy-start.9 = (bf16[1,2,1024]{2,1,0:T(2,128)(2,1)S(1)}, bf16[1,2,1024]{2,1,0:T(2,128)(2,1)}, u32[]{:S(2)}) copy-start(bf16[1,2,1024]{2,1,0:T(2,128)(2,1)} %param.25) | copy-start | bytes 12292
  7.3 5.6 %copy-start.1 = (bf16[32,6144]{1,0:T(8,128)(2,1)S(1)}, bf16[32,6144]{1,0:T(8,128)(2,1)}, u32[]{:S(2)}) copy-start(bf16[32,6144]{1,0:T(8,128)(2,1)} %refs_13_.1) | copy-start | bytes 1179652
  7.3 197.9 %all-gather.2.cloned.1.call-start = ((), (), s32[]{:S(2)}) async-start(), calls=%async_computation.3 | async-start | bytes 10813440 | tf_op jit(solution)/shard_map/all_gather | solution.py:819
  8.8 80.3 %copy-start.12 = (s32[1,512]{1,0:T(1,128)S(1)}, s32[1,512]{1,0:T(1,128)}, u32[]{:S(2)}) copy-start(s32[1,512]{1,0:T(1,128)} %param.28) | copy-start | bytes 6148
  84.8 2.6 copy-start
  87.4 0.6 copy-start.2
  103.0 40.8 %all-to-all-start = ((bf16[4,512,768]{2,1,0:T(8,128)(2,1)}), bf16[4,512,768]{2,1,0:T(8,128)(2,1)S(1)}, u32[]{:S(2)}, u32[]{:S(2)}) async-start(bf16[4,512,768]{2,1,0:T(8,128)(2,1)} %get-tuple-element.87), calls=%async_computation | async-start | bytes 6291456 | tf_op jit(solution)/shard_map/all_to_all | solution.py:832
  143.9 1.8 copy-start.3
  185.6 18.5 %all-to-all-start.1 = ((bf16[4,512,256]{2,1,0:T(8,128)(2,1)}), bf16[4,512,256]{2,1,0:T(8,128)(2,1)S(1)}, u32[]{:S(2)}, u32[]{:S(2)}) async-start(bf16[4,512,256]{2,1,0:T(8,128)(2,1)} %bitcast.88), calls=%async_computation.1 | async-start | bytes 2097152 | tf_op jit(solution)/shard_map/all_to_all | solution.py:838
  250.2 18.1 %all-to-all-start.2 = ((bf16[4,512,256]{2,1,0:T(8,128)(2,1)}), bf16[4,512,256]{2,1,0:T(8,128)(2,1)S(1)}, u32[]{:S(2)}, u32[]{:S(2)}) async-start(bf16[4,512,256]{2,1,0:T(8,128)(2,1)} %bitcast.70), calls=%async_computation.2 | async-start | bytes 2097152 | tf_op jit(solution)/shard_map/all_to_all | solution.py:841
  268.3 1.0 copy-start.4
  495.2 9.7 %copy-start.7 = (f32[32,3072]{1,0:T(8,128)S(1)}, f32[32,3072]{1,0:T(8,128)}, u32[]{:S(2)}) copy-start(f32[32,3072]{1,0:T(8,128)} %get-tuple-element.102) | copy-start | bytes 1179652
  504.8 10.2 %copy-start.5 = (f32[512,1024]{1,0:T(8,128)S(1)}, f32[512,1024]{1,0:T(8,128)}, u32[]{:S(2)}) copy-start(f32[512,1024]{1,0:T(8,128)} %get-tuple-element.98) | copy-start | bytes 6291460
  506.2 10.1 %copy-start.6 = (f32[32,6144]{1,0:T(8,128)S(1)}, f32[32,6144]{1,0:T(8,128)}, u32[]{:S(2)}) copy-start(f32[32,6144]{1,0:T(8,128)} %get-tuple-element.156) | copy-start | bytes 2359300
Sparse Core Ops, SparseCore 0:
  12.3 112.7 all-gather.1

commit v4 on v3

--- a/solution.py
+++ b/solution.py
@@ -253,7 +253,7 @@
         cost_estimate=pl.CostEstimate(flops=2*F*D*3*D,bytes_accessed=14*2**20,transcendentals=0))(x,seg,emb,w,b,cos,sin)
 
 def mid_kernel(x_ref,a_ref,c_ref,seg_ref,msk_ref,emb_ref,w_ref,bo_ref,bu_ref,bd_ref,
-               out_ref,dm_ref,da_ref,gw_ref,gb_ref,ge_ref,
+               out_ref,dm_ref,da_ref,gu_ref,gw_ref,gb_ref,ge_ref,
                wo_ref,wu_ref,wd_ref,n2s,acts,dhs,dfs,dps,dgelu,sem,*,R):
     F,D=x_ref.shape; H=bu_ref.shape[1]; CH=512
     loads=[pltpu.make_async_copy(w_ref.at[:,pl.ds(o,n)],r,sem.at[i]) for i,(o,n,r) in enumerate(((2*H,D,wo_ref),(0,H,wu_ref),(H,H,wd_ref)))]
@@ -311,18 +311,18 @@
     @pl.loop(0,D//256)
     def _(i):
         c=pl.ds(pl.multiple_of(i*256,256),256)
-        gw_ref[c,2*H:2*H+D]=dot(a_ref[:,c],dps[...],TN).astype(bf)
-        gw_ref[c,0:H]=dot(n2s[:,c],dhs[...],TN).astype(bf)
+        gw_ref[c,H:H+D]=dot(a_ref[:,c],dps[...],TN).astype(bf)
+        gu_ref[c,:]=dot(n2s[:,c],dhs[...],TN).astype(bf)
         for t in range(H//D):
             e=pl.ds(pl.multiple_of(t*D+i*256,256),256)
-            gw_ref[c,H+t*D:H+(t+1)*D]=dot(acts[:,e],dfs[...],TN).astype(bf)
+            gw_ref[c,t*D:(t+1)*D]=dot(acts[:,e],dfs[...],TN).astype(bf)
 
 def mid(x,a,c,seg,msk,emb,w,bo,bu,bd,R=128):
     F,D=x.shape; H=bu.shape[1]
     S=jax.ShapeDtypeStruct; M=pltpu.VMEM
     return pl.pallas_call(functools.partial(mid_kernel,R=R),
-        out_shape=(S((F,D),bf),S((F,D),f32),S((F,D),bf),S((D,2*H+D),bf),S((8,H),f32),S((8,4*D),f32)),
-        in_specs=[V]*6+[ANY]+[V]*3,out_specs=(V,)*6,
+        out_shape=(S((F,D),bf),S((F,D),f32),S((F,D),bf),S((D,H),bf),S((D,H+D),bf),S((8,H),f32),S((8,4*D),f32)),
+        in_specs=[V]*6+[ANY]+[V]*3,out_specs=(V,)*7,
         scratch_shapes=[M((D,D),bf),M((D,H),bf),M((D,H),bf),M((F,D),bf),M((F,H),bf),M((F,H),bf),M((F,D),bf),M((F,D),bf),M((R,H),f32),pltpu.SemaphoreType.DMA((3,))],
         compiler_params=pltpu.CompilerParams(vmem_limit_bytes=62*2**20),name="mid",
         cost_estimate=pl.CostEstimate(flops=6*F*D*(D+2*H),bytes_accessed=30*2**20,transcendentals=F*H))(x,a,c,seg,msk,emb,w,bo,bu,bd)
@@ -565,6 +565,8 @@
         in_specs=[ANY]*(nw+1)+[V,ANY,V],out_specs=tuple([ANY]*(nw+2)+[V,V]),scratch_shapes=scr,
         compiler_params=pltpu.CompilerParams(collective_id=0,has_side_effects=True,vmem_limit_bytes=40*2**20),name="entry")(*shards,bias,time,ids,wada)
 
+ORD_X=-1
+QW=512
 class Reduce:
     def __init__(self,p,parts,scr,own=None,src=None,col=0):
         self.p,self.parts,self.src=p,parts,src
@@ -650,18 +652,16 @@
     def finish(self):
         for c in self.sent: c.wait_send()
 
-def everyone(p,f):
-    @pl.loop(0,p.nd)
-    def _(dh):
-        @pl.loop(0,p.ns)
-        def _(d):
-            @pl.when(dh+d>0)
-            def _(): f(dh,d,(lax.rem(p.h+dh,p.nd),lax.rem(p.s+d,p.ns)))
-
-def make_remote(src,dst,ss,rs,dev):
-    return pltpu.make_async_remote_copy(src_ref=src,dst_ref=dst,send_sem=ss,recv_sem=rs,device_id=dev,device_id_type=pl.DeviceIdType.MESH)
-
-REST=(lambda w:((0,w,"yzx"),)); QKV=(lambda w:((0,w//2,"yxz"),(w//2,w,"xyz")))
+def greet(p):
+    b=pltpu.get_barrier_semaphore()
+    for d in range(1,p.nd): pl.semaphore_signal(b,inc=1,device_id=(lax.rem(p.h+d,p.nd),p.s),device_id_type=pl.DeviceIdType.MESH)
+    for d in range(1,p.ns): pl.semaphore_signal(b,inc=1,device_id=(p.h,lax.rem(p.s+d,p.ns)),device_id_type=pl.DeviceIdType.MESH)
+    pl.semaphore_wait(b,p.nd+p.ns-2)
+
+def along_head(p,f): return [f(d,lax.rem(p.h+d,p.nd),(lax.rem(p.h+d,p.nd),p.s)) for d in range(1,p.nd)]
+def along_seq(p,f): return [f(d,lax.rem(p.s+d,p.ns),(p.h,lax.rem(p.s+d,p.ns))) for d in range(1,p.ns)]
+
+REST=(lambda w,j:((0,w,"xyz"),) if j==ORD_X else ((0,w,"yzx"),)); QKV=(lambda w:((0,w//2,"yxz"),(w//2,w,"xyz")))
 
 def final_kernel(nd,ns,R,refs,scr):
     (g_ref,rest_ref,x_hbm,n1_hbm,dm_hbm,wq_hbm,cos_ref,sin_ref,seg_ref,emb_ref,gbm_ref,gem_ref,act,wada)=refs[:14]
@@ -671,90 +671,100 @@
     pools=scr[26:]
     p=Place(nd,ns); me=p.h*ns+p.s
     F,D=x_ref.shape; W=D//nd; E=D*6//8; K=wada.shape[0]; H=gbm_ref.shape[1]; NR=F//R
-    nr=(2*H+D)//D
-    greet_all(p)
+    nr=H//D; nq=3*D//QW
+    greet(p)
     loads=[pltpu.make_async_copy(a,b,ld.at[i]) for i,(a,b) in enumerate(((x_hbm,x_ref),(wq_hbm,w_ref),(dm_hbm,dm_ref),(n1_hbm,n1_ref)))]
     sends=[]; own=[]
+    def chunk(i):
+        r=pl.ds(i*R,R)
+        sends.append([remote(g_ref.at[lax.rem(p.h+d,nd),r],g.at[p.h,r],gs.at[i,d],gr.at[i,d],(lax.rem(p.h+d,nd),p.s)) for d in range(1,nd)])
     for i in range(NR):
         r=pl.ds(i*R,R)
-        sends.append([remote(g_ref.at[lax.rem(p.h+d,nd),r],g.at[p.h,r],gs.at[i,d],gr.at[i,d],(lax.rem(p.h+d,nd),p.s)) for d in range(1,nd)])
         c=pltpu.make_async_copy(g_ref.at[p.h,r],g.at[p.h,r],gl.at[i]); c.start(); own.append(c)
+    for i in range(min(2,NR)): chunk(i)
     for l in loads: l.start()
     it=iter(pools)
     take=lambda n: [next(it) for _ in range(n)]
     rest=[]
     for j in range(nr):
-        rest.append(Reduce(p,REST(D),take(len(Reduce.scratch(nd,ns,K,D,bf,REST(D),False))),src=rest_ref,col=j*D))
+        rest.append(Reduce(p,REST(D,j),take(len(Reduce.scratch(nd,ns,K,D,bf,REST(D,j),False))),src=rest_ref,col=j*D))
         rest[-1].start()
-    qkv=[Reduce(p,QKV(D),take(len(Reduce.scratch(nd,ns,K,D,bf,QKV(D),True))),own=gw.at[j]) for j in range(3)]
+    qkv=[Reduce(p,QKV(QW),take(len(Reduce.scratch(nd,ns,K,QW,bf,QKV(QW),True))),own=gw.at[j]) for j in range(nq)]
     bias=Reduce(p,QKV(256),take(len(Reduce.scratch(nd,ns,8,256,f32,QKV(256),True))),own=bsc)
     gbv[...]=jnp.zeros_like(gbv); gev[...]=jnp.zeros_like(gev); bsc[...]=jnp.zeros_like(bsc)
-    for a in rest: a.step()
+    for a in rest[:2]: a.step()
     for l in loads: l.wait()
-    def tile(i):
+    def turn(i):
         for c in sends[i]: c.wait_recv()
         own[i].wait()
+        if i+2<NR: chunk(i+2)
         r=slice(i*R,(i+1)*R)
-        seg=seg_ref[r,:]
         cos=jnp.concatenate([cos_ref[r,:]]*(W//128),1); sin=jnp.concatenate([sin_ref[r,:]]*(W//128),1)
-        dn=jnp.zeros((R,D),f32)
-        for d in range(nd):
+        @pl.loop(0,nd)
+        def _(d):
             for j in range(3):
-                c=(d*3+j)*W
+                c=pl.ds(pl.multiple_of((d*3+j)*W,W),W)
                 v=g[d,r,j*W:(j+1)*W]
                 if j<2:
                     v=v.astype(f32)
                     v=(v*cos-partner(v)*sin).astype(bf)
-                dps[r,c:c+W]=v
-                gbv[0:1,c:c+W]+=jnp.sum(v.astype(f32),0,keepdims=True)
-        for j in range(3*D//512):
-            dn+=dot(dps[r,j*512:(j+1)*512],w_ref[:,j*512:(j+1)*512],NT)
-        n,rs=moments(x_ref[r,:].astype(f32))
-        for k,x in ((0,dn),(1,dn*n)):
-            a,b=sums(x,seg)
-            gev[0:1,k*D:(k+1)*D]+=a; gev[1:2,k*D:(k+1)*D]+=b
-        dn=dn*(1.0+pick(seg,emb_ref,1,D))
-        gf_ref[r,:]=dm_ref[r,:]+(dn-jnp.mean(dn,-1,keepdims=True)-n*jnp.mean(dn*n,-1,keepdims=True))*rs
+                dps[r,c]=v
+                gbv[0:1,c]+=jnp.sum(v.astype(f32),0,keepdims=True)
+    def norm(lo,hi):
+        @pl.loop(lo,hi)
+        def _(i):
+            r=pl.ds(pl.multiple_of(i*R,R),R)
+            seg=seg_ref[r,:]
+            dn=jnp.zeros((R,D),f32)
+            for j in range(3*D//512):
+                dn+=dot(dps[r,j*512:(j+1)*512],w_ref[:,j*512:(j+1)*512],NT)
+            n,rs=moments(x_ref[r,:].astype(f32))
+            for k,x in ((0,dn),(1,dn*n)):
+                a,b=sums(x,seg)
+                gev[0:1,k*D:(k+1)*D]+=a; gev[1:2,k*D:(k+1)*D]+=b
+            dn=dn*(1.0+pick(seg,emb_ref,1,D))
+            gf_ref[r,:]=dm_ref[r,:]+(dn-jnp.mean(dn,-1,keepdims=True)-n*jnp.mean(dn*n,-1,keepdims=True))*rs
     def weight(j):
         B=D//nd
         for h in range(nd):
-            v=dot(n1_ref[:,h*B:(h+1)*B],dps[:,j*D:(j+1)*D],TN).astype(bf)
-            gw[j,h//2,h%2]=v.reshape(p.Z,p.Y,K,D)
+            v=dot(n1_ref[:,h*B:(h+1)*B],dps[:,j*QW:(j+1)*QW],TN).astype(bf)
+            gw[j,h//2,h%2]=v.reshape(p.Z,p.Y,K,QW)
         qkv[j].start()
-    todo=[a.step for a in rest]+[a.step for a in rest]
-    per=-(-len(todo)//NR)
+    steps=[a.step for _ in range(2) for a in rest]
     for i in range(NR):
-        tile(i)
-        if i<NR-1:
-            for f in todo[i*per:(i+1)*per]: f()
-    gev[0:2,2*D:]=gem_ref[0:2,:]
-    for j in range(8):
-        for t in range(2): hsum[p.h,2*j+t:2*j+t+1,:]=gev[t:t+1,j*E:(j+1)*E]
-    hc=[remote(hsum.at[p.h],hsum.at[p.h],hs.at[d],hr.at[d],(lax.rem(p.h+d,nd),p.s)) for d in range(1,nd)]
+        turn(i)
+        if i:
+            for f in steps[(i-1)*len(steps)//(NR-1):i*len(steps)//(NR-1)]: f()
+    for j in range(nq):
+        weight(j)
+        if j: qkv[j-1].step()
     vec=jnp.concatenate([gbv[0:1,:],gbm_ref[0:1,0:D],gbm_ref[1:2,:],gbm_ref[2:3,0:D]],1)
     for q in range(vec.shape[1]//256):
         h,s=divmod(q,ns)
         bsc[h//2,h%2,s//p.Y,s%p.Y,0:1,:]=vec[:,q*256:(q+1)*256]
     bias.start()
-    weight(0)
-    weight(1)
-    qkv[0].step(); bias.step()
-    weight(2)
-    qkv[1].step(); qkv[2].step()
-    for f in todo[(NR-1)*per:]: f()
+    qkv[nq-1].step()
+    norm(0,NR//2)
     bias.step()
+    qkv[0].step()
+    qkv[1].step()
+    norm(NR//2,NR)
+    gev[0:2,2*D:]=gem_ref[0:2,:]
+    for j in range(8):
+        for t in range(2): hsum[p.h,2*j+t:2*j+t+1,:]=gev[t:t+1,j*E:(j+1)*E]
+    hc=[remote(hsum.at[p.h],hsum.at[p.h],hs.at[d],hr.at[d],(lax.rem(p.h+d,nd),p.s)) for d in range(1,nd)]
+    qkv[0].step(); qkv[2].step(); qkv[1].step(); bias.step()
     for c in hc: c.wait()
     tot=hsum[0]
     for i in range(1,nd): tot=tot+hsum[i]
     demb[p.s]=tot.astype(bf)
     qc=[remote(demb.at[p.s],demb.at[p.s],qs.at[d],qr.at[d],(p.h,lax.rem(p.s+d,ns))) for d in range(1,ns)]
-    qkv[0].step(); bias.step()
-    qkv[1].step()
-    qkv[2].step()
+    qkv[3].step(); qkv[2].step(); bias.step()
     for j,a in enumerate(rest): a.last(rest_out,j*D)
     bias.last(bout)
-    everyone(p,lambda dh,d,dev: remote(bout,bias_all.at[me],bs.at[dh,d],br.at[dh,d],dev))
-    bias_all[me]=bout[...]
+    bias_all[p.h,p.s]=bout[...]
+    bc=along_head(p,lambda d,h,dev: remote(bout,bias_all.at[p.h,p.s],bs.at[0,d],br.at[0,d],dev))
+    qkv[4].step(); qkv[3].step()
     for c in qc: c.wait()
     Q=ns*16
     flat=demb[...].reshape(Q,E)
@@ -768,28 +778,33 @@
         gada[:,j*E:(j+1)*E]=dot(m,flat,TN)[:K,:]
         tot=jnp.where(rk==j,dot(flat,wada[:,j*E:(j+1)*E],NT),tot)
     dscr[...]=jnp.concatenate([tot,jnp.zeros((Q,128-K),f32)],1).reshape(ns,16,128)
-    dact[me]=dscr[p.s]
-    everyone(p,lambda dh,d,dev: remote(dscr.at[dev[1]],dact.at[me],ds_.at[dh,d],dr.at[dh,d],dev))
+    dact[p.h,p.s]=dscr[p.s]
+    dc=along_seq(p,lambda d,s,dev: remote(dscr.at[s],dact.at[p.h,p.s],ds_.at[0,d],dr.at[0,d],dev))
+    for c in bc: c.wait()
+    bc=along_seq(p,lambda d,s,dev: remote(bias_all.at[:,p.s],bias_all.at[:,p.s],bs.at[1,d],br.at[1,d],dev))
     r8=lax.broadcasted_iota(jnp.int32,(8,Q),0); c8=lax.broadcasted_iota(jnp.int32,(8,Q),1)
     gbada[...]=dot(jnp.where(c8%16//2==r8,1.0,0.0).astype(bf),flat)
-    for a in qkv: a.step()
-    for j in range(3): qkv[j].last(qkv_out,j*D)
+    qkv[5].step(); qkv[4].step()
+    for c in dc: c.wait()
+    dc=along_head(p,lambda d,h,dev: remote(dact.at[p.h],dact.at[p.h],ds_.at[1,d],dr.at[1,d],dev))
+    for j in range(nq-1): qkv[j].last(qkv_out,j*QW)
+    qkv[5].step()
+    qkv[nq-1].last(qkv_out,(nq-1)*QW)
     for a in rest+qkv+[bias]: a.finish()
     for i in range(NR):
         for c in sends[i]: c.wait_send()
-    everyone(p,lambda dh,d,dev: make_remote(bout,bias_all.at[me],bs.at[dh,d],br.at[dh,d],dev).wait())
-    everyone(p,lambda dh,d,dev: make_remote(dscr.at[dev[1]],dact.at[me],ds_.at[dh,d],dr.at[dh,d],dev).wait())
+    for c in bc+dc: c.wait()
 
 def final(nd,ns,dqkv,rest,x,n1,dm,wq,cos,sin,seg,emb,gb,ge,act,wada,R=128):
     F,D=x.shape; K,E6=wada.shape; E=E6//8; H=gb.shape[1]; N=nd*ns; W=D//nd; NR=F//R
     X,Y,Z=sizes(nd,ns)
     S=jax.ShapeDtypeStruct; M=pltpu.VMEM; A=pltpu.SemaphoreType.DMA
-    outs=[S((F,D),f32),S((K,2*H+D),f32),S((K,3*D),f32),S((N,8,256),f32),S((K,E6),f32),S((8,E),f32),S((N,16,128),f32)]
-    scr=[M((nd,F,3*W),bf),M((F,D),bf),M((F,D),bf),M((F,D),f32),M((D,3*D),bf),M((F,3*D),bf),M((3,X,2,Z,Y,K,D),bf),M((8,3*D),f32),M((8,E6),f32),
+    outs=[S((F,D),f32),S((K,H),f32),S((K,3*D),f32),S((nd,ns,8,256),f32),S((K,E6),f32),S((8,E),f32),S((nd,ns,16,128),f32)]
+    scr=[M((nd,F,3*W),bf),M((F,D),bf),M((F,D),bf),M((F,D),f32),M((D,3*D),bf),M((F,3*D),bf),M((3*D//QW,X,2,Z,Y,K,QW),bf),M((8,3*D),f32),M((8,E6),f32),
          M((X,2,Z,Y,8,256),f32),M((8,256),f32),M((nd,16,E),f32),M((ns,16,E),bf),M((ns,16,128),f32),
-         A((NR,nd)),A((NR,nd)),A((NR,)),A((4,)),A((nd,)),A((nd,)),A((ns,)),A((ns,)),A((nd,ns)),A((nd,ns)),A((nd,ns)),A((nd,ns))]
-    for _ in range((2*H+D)//D): scr+=Reduce.scratch(nd,ns,K,D,bf,REST(D),False)
-    for _ in range(3): scr+=Reduce.scratch(nd,ns,K,D,bf,QKV(D),True)
+         A((NR,nd)),A((NR,nd)),A((NR,)),A((4,)),A((nd,)),A((nd,)),A((ns,)),A((ns,)),A((2,max(nd,ns))),A((2,max(nd,ns))),A((2,max(nd,ns))),A((2,max(nd,ns)))]
+    for j in range(H//D): scr+=Reduce.scratch(nd,ns,K,D,bf,REST(D,j),False)
+    for _ in range(3*D//QW): scr+=Reduce.scratch(nd,ns,K,QW,bf,QKV(QW),True)
     scr+=Reduce.scratch(nd,ns,8,256,f32,QKV(256),True)
     def k(*refs): final_kernel(nd,ns,R,refs[:14+len(outs)],refs[14+len(outs):])
     return pl.pallas_call(k,out_shape=tuple(outs),in_specs=[ANY]*6+[V]*8,out_specs=(V,)*len(outs),scratch_shapes=scr,
@@ -830,29 +845,30 @@
     segc=segment_ids[0][:,None]; mskc=frame_mask[0].astype(f32)[:,None]
     normed,packed=qkv_proj(x,segc,emb,wq,bq,cos,sin,nd)
     qkv=lax.all_to_all(packed,"head",split_axis=0,concat_axis=0,tiled=True).reshape(nd*F,3*W)
-    T=256
+    T=512
     qlo,qhi,klo,khi=tables(seg_row,msk_row,T)
     aq,ak=aux(seg_row,msk_row)
     o,lse=attn_fwd(qkv,qlo,qhi,aq,ak,T)
     def back(a):
         return lax.all_to_all(a.reshape(nd,F,-1),"head",split_axis=0,concat_axis=0,tiled=True)
     att=back(o).transpose(1,0,2).reshape(F,D)
-    out,dmid,datt,grest,gb,ge=mid(x,att,cot,segc,mskc,emb,rest_all,bo,bu,bd)
+    out,dmid,datt,gup,gdo,gb,ge=mid(x,att,cot,segc,mskc,emb,rest_all,bo,bu,bd)
+    gdo=lax.psum_scatter(gdo,HS,scatter_dimension=0,tiled=True).astype(f32)
     do=lax.all_to_all(datt.reshape(F,nd,W).transpose(1,0,2),"head",split_axis=0,concat_axis=0,tiled=True).reshape(nd*F,W)
     dqkv=attn_bwd(qkv,o,do,lse,klo,khi,aq,ak,T)
-    gx,grest,gqkv,gbias,gada,gbada,dact=final(nd,ns,dqkv.reshape(nd,F,3*W),grest.reshape(X,2,Z,Y,K,2*H+D),x,normed,dmid,wq,cos,sin,segc,emb,gb,ge,act,w_ada)
-    dact=dact[:,:,:K].reshape(N,8,2,K).sum(1).transpose(1,0,2).reshape(2,D)
+    gx,gup,gqkv,gbias,gada,gbada,dact=final(nd,ns,dqkv.reshape(nd,F,3*W),gup.reshape(X,2,Z,Y,K,H),x,normed,dmid,wq,cos,sin,segc,emb,gb,ge,act,w_ada)
+    dact=dact[:,:,:,:K].reshape(N,8,2,K).sum(1).transpose(1,0,2).reshape(2,D)
     _,pull=jax.vjp(jax.nn.silu,time_embed[0].astype(f32))
     gtime=pull(dact)[0][None]
     gbada=lax.dynamic_slice_in_dim(gbada.reshape(-1),dev*E,E,0)
-    gbias=gbias[:,0,:].reshape(-1)
+    gbias=gbias[:,:,0,:].reshape(-1)
     gbs=[]; at=0
     for k,order in ((3*D,restore),(D,None),(H,unhide),(D,None)):
         v=gbias[at:at+k]; at+=k
         if order: v=order(v[None])[0]
         gbs.append(lax.dynamic_slice_in_dim(v,dev*(k//N),k//N,0))
-    gdown=grest[:,H:2*H].reshape(K,nt,D).transpose(1,0,2).reshape(nt*K,D)
-    return (out[None],gx[None],gtime,gada,gbada,restore(gqkv),gbs[0],grest[:,2*H:],gbs[1],unhide(grest[:,:H]),gbs[2],gdown,gbs[3])
+    gdown=gdo[:,:H].reshape(K,nt,D).transpose(1,0,2).reshape(nt*K,D)
+    return (out[None],gx[None],gtime,gada,gbada,restore(gqkv),gbs[0],gdo[:,H:],gbs[1],unhide(gup),gbs[2],gdown,gbs[3])
 
 
 def solution(mesh):

time: 532 us -> 476 us (0.89)
  Pallas kernels: 391 us -> 340 us
    pallas_call x1, Pallas kernels: 158 us -> 119 us  [final(): pl.pallas_call(k, out_shape=tuple(outs), in_specs=[ANY] * 6 + [V] * 8, ou...]
    pallas_call x1, Pallas kernels: 68.1 us -> 61.4 us  [attn_bwd(): pl.pallas_call(functools.partial(bwd_kernel, T=T, nh=nh), out_shape=jax.S...]
  transfers between devices with their start and end apart: 4 -> 5, of which waited for: 3 -> 3; matrix products, arithmetic and copies ran while one was open for 3% -> 6% of each run, Pallas kernels for 23% -> 64%
where the time goes in v4:
time: 476 us; the launch traced here: 469 us
  Pallas kernels  340 us (71%)
  waiting for transfers between devices  57.7 us (12%)
  local copies, waits for them, and re-layouts  34.4 us (7%)
  between operations  15 us (3%)
  starting transfers between devices  11.2 us (2%)
  other arithmetic  9.84 us (2%)
    pallas_call x1, Pallas kernels, final(): pl.pallas_call(k, out_shape=tuple(outs), in_specs=[ANY] * 6 + [V] * 8, ou...  119 us
    pallas_call x1, Pallas kernels, entry(): pl.pallas_call(functools.partial(entry_kernel, nd, ns, nw), out_shape=tup...  71.8 us
    pallas_call x1, Pallas kernels, attn_bwd(): pl.pallas_call(functools.partial(bwd_kernel, T=T, nh=nh), out_shape=jax.S...  61.4 us
    pallas_call x1, Pallas kernels, mid(): pl.pallas_call(functools.partial(mid_kernel, R=R), out_shape=(S((F, D), b...  42.7 us
    pallas_call x1, Pallas kernels, attn_fwd(): pl.pallas_call(functools.partial(fwd_kernel, T=T, nh=nh), out_shape=(jax....  35 us
    all_to_all x1, waiting for transfers between devices, body(): lax.all_to_all(packed, 'head', split_axis=0, concat_axis=0, tiled=True)  32.7 us
    all_to_all x1, waiting for transfers between devices, body(): lax.all_to_all(datt.reshape(F, nd, W).transpose(1, 0, 2), 'head', split_a...  13.9 us
    all_to_all x1, waiting for transfers between devices, back(): lax.all_to_all(a.reshape(nd, F, -1), 'head', split_axis=0, concat_axis=0,...  11.1 us
  transfers between devices with their start and end apart: 5, of which 3 were waited for; matrix products, arithmetic and copies ran while one was open for 6% of the time, Pallas kernels for 64%

profile of v4, /device:TPU:0, one launch (start us, length us, event | category | flops | bytes accessed | tf_op | source)
XLA Modules:
  0.0 468.6 jit_solution(912639370829175510)
XLA Ops:
  7.3 1.4 reshape.354
  9.4 1.0 copy.124
  10.5 1.6 pad_maximum_fusion
  12.9 71.8 %entry.1 = (bf16[2,2,4,2,32,3072]{5,4,3,2,1,0:T(8,128)(2,1)S(1)}, bf16[32,16,512]{2,1,0:T(8,128)(2,1)S(1)}, s32[4,8,512]{2,1,0:T(8,128)S(1)}, f32[16,768]{1,0:T(8,128)S(1)}, bf16[64,128]{1,0:T(8,128)(2,1)S(1)}) custom-call(bf16[32,3072]{1,0:T(8,128)(2,1)S(1)} %reshape.345.refs_0_, bf16[16,512]{1,0:T(8,128)(2,1)S(1)} %scatter.16.refs_1_, ...), custom_call_target="tpu_custom_call" | custom-call | tf_op jit(solution)/shard_map/entry/pallas_call | solution.py:564
  84.8 2.6 copy-done
  89.9 1.8 negate_select_fusion
  92.4 10.6 %qkv_proj.1 = (bf16[512,1024]{1,0:T(8,128)(2,1)}, bf16[4,512,768]{2,1,0:T(8,128)(2,1)}) custom-call(bf16[512,1024]{1,0:T(8,128)(2,1)} %bitcast.91, s32[512,1]{1,0:T(8,128)} %copy.121.seg_ref.refs_8_, f32[2,6144]{1,0:T(2,128)} %broadcast_add_fusion.emb_ref.refs_9_, bf16[1024,3072]{1,0:T(8,128)(2,1)} %bitcast.78, f32[1,3072]{1,0:T(1,128)} %reshape.350.b_ref, ...), custom_call_target="tpu_custom_call" | custom-call | flops 3221225472 | bytes 14680064 | tf_op jit(solution)/shard_map/qkv_proj/pallas_call | solution.py:249
  103.0 3.7 all-to-all-start
  108.4 2.8 select_convert_fusion
  111.2 32.7 %all-to-all-done = bf16[4,512,768]{2,1,0:T(8,128)(2,1)S(1)} async-done(((bf16[4,512,768]{2,1,0:T(8,128)(2,1)}), bf16[4,512,768]{2,1,0:T(8,128)(2,1)S(1)}, u32[]{:S(2)}, u32[]{:S(2)}) %all-to-all-start) | async-done | bytes 3145760 | tf_op jit(solution)/shard_map/all_to_all | solution.py:847
  143.8 1.8 copy-done.3
  145.6 35.0 %attn_fwd.1 = (bf16[2048,256]{1,0:T(8,128)(2,1)}, f32[2048,128]{1,0:T(8,128)}) custom-call(s32[4]{0:T(128)} %get-tuple-element.114.lo_ref, s32[4]{0:T(128)} %broadcast_add_fusion.2.hi_ref, bf16[2048,768]{1,0:T(8,128)(2,1)} %bitcast.80, bf16[2048,128]{1,0:T(8,128)(2,1)} %get-tuple-element.131.auxq_ref, bf16[2048,128]{1,0:T(8,128)(2,1)} %get-tuple-element.130.auxk_ref), custom_call_target="tpu_custom_call" | custom-call | tf_op jit(solution)/shard_map/attn_fwd/pallas_call | solution.py:93
  180.6 3.5 all-to-all-start.1
  187.4 11.1 %all-to-all-done.1 = bf16[4,512,256]{2,1,0:T(8,128)(2,1)S(1)} async-done(((bf16[4,512,256]{2,1,0:T(8,128)(2,1)}), bf16[4,512,256]{2,1,0:T(8,128)(2,1)S(1)}, u32[]{:S(2)}, u32[]{:S(2)}) %all-to-all-start.1) | async-done | bytes 1048608 | tf_op jit(solution)/shard_map/all_to_all | solution.py:853
  198.6 1.1 copy.138
  199.7 42.7 %mid.1 = (bf16[512,1024]{1,0:T(8,128)(2,1)}, f32[512,1024]{1,0:T(8,128)}, bf16[512,1024]{1,0:T(8,128)(2,1)}, bf16[1024,2048]{1,0:T(8,128)(2,1)}, bf16[1024,3072]...) custom-call(bf16[512,1024]{1,0:T(8,128)(2,1)} %bitcast.92, bf16[512,1024]{1,0:T(8,128)(2,1)} %bitcast.96, ...), custom_call_target="tpu_custom_call" | custom-call | flops 16106127360 | bytes 31457280 | tf_op jit(solution)/shard_map/mid/pallas_call | solution.py:323
  242.5 1.2 copy-done.6
  243.6 1.0 copy.151
  244.7 3.7 all-to-all-start.2
  248.9 13.9 %all-to-all-done.2 = bf16[4,512,256]{2,1,0:T(8,128)(2,1)S(1)} async-done(((bf16[4,512,256]{2,1,0:T(8,128)(2,1)}), bf16[4,512,256]{2,1,0:T(8,128)(2,1)S(1)}, u32[]{:S(2)}, u32[]{:S(2)}) %all-to-all-start.2) | async-done | bytes 1048608 | tf_op jit(solution)/shard_map/all_to_all | solution.py:857
  262.8 1.0 copy-done.4
  263.8 61.4 %attn_bwd.1 = bf16[2048,768]{1,0:T(8,128)(2,1)} custom-call(s32[4]{0:T(128)} %get-tuple-element.113.lo_ref, s32[4]{0:T(128)} %broadcast_add_fusion.1.hi_ref, bf16[2048,768]{1,0:T(8,128)(2,1)} %bitcast.81, bf16[2048,256]{1,0:T(8,128)(2,1)} %get-tuple-element.89.o_ref, bf16[2048,256]{1,0:T(8,128)(2,1)} %bitcast.87, f32[2048,128]{1,0:T(8,128)} %get-tuple-element.92.lse_ref, ...), custom_call_target="tpu_custom_call" | custom-call | tf_op jit(solution)/shard_map/attn_bwd/pallas_call | solution.py:177
  325.3 118.8 %final.1 = (f32[512,1024]{1,0:T(8,128)}, f32[32,2048]{1,0:T(8,128)}, f32[32,3072]{1,0:T(8,128)}, f32[4,8,8,256]{3,2,1,0:T(8,128)}, f32[32,6144]{1,0:T(8,128)}, /...) custom-call(bf16[4,512,768]{2,1,0:T(8,128)(2,1)} %bitcast.82, bf16[2,2,4,2,32,2048]{5,4,3,2,1,0:T(8,128)(2,1)} %bitcast.85, ...), custom_call_target="tpu_custom_call" | custom-call | tf_op jit(solution)/shard_map/final/pallas_call | solution.py:810
  444.1 1.3 reshape.370
  446.3 2.1 reshape.371
  448.8 0.9 reshape.369
  449.7 1.0 slice.120
  450.8 0.9 slice_reduce_fusion
  455.7 0.9 slice.135
  457.6 1.5 slice.133
  459.1 1.3 copy.163
  460.4 0.9 copy.164
  (114 shorter events, 16.3 us)
Async XLA Ops:
  7.2 5.0 %copy-start.10 = (bf16[32,3072]{1,0:T(8,128)(2,1)S(1)}, bf16[32,3072]{1,0:T(8,128)(2,1)}, u32[]{:S(2)}) copy-start(bf16[32,3072]{1,0:T(8,128)(2,1)} %param.31) | copy-start | bytes 589828
  7.2 5.4 %copy-start.20 = (bf16[192]{0:T(256)(128)(2,1)S(1)}, bf16[192]{0:T(256)(128)(2,1)}, u32[]{:S(2)}) copy-start(bf16[192]{0:T(256)(128)(2,1)} %param.30) | copy-start | bytes 1156
  7.2 5.4 %copy-start.16 = (bf16[96]{0:T(256)(128)(2,1)S(1)}, bf16[96]{0:T(256)(128)(2,1)}, u32[]{:S(2)}) copy-start(bf16[96]{0:T(256)(128)(2,1)} %param.32) | copy-start | bytes 580
  7.2 5.4 %copy-start.17 = (bf16[32]{0:T(256)(128)(2,1)S(1)}, bf16[32]{0:T(256)(128)(2,1)}, u32[]{:S(2)}) copy-start(bf16[32]{0:T(256)(128)(2,1)} %param.34) | copy-start | bytes 196
  7.2 5.4 %copy-start.18 = (bf16[64]{0:T(256)(128)(2,1)S(1)}, bf16[64]{0:T(256)(128)(2,1)}, u32[]{:S(2)}) copy-start(bf16[64]{0:T(256)(128)(2,1)} %param.36) | copy-start | bytes 388
  7.2 5.4 %copy-start.19 = (bf16[32]{0:T(256)(128)(2,1)S(1)}, bf16[32]{0:T(256)(128)(2,1)}, u32[]{:S(2)}) copy-start(bf16[32]{0:T(256)(128)(2,1)} %param.38) | copy-start | bytes 196
  7.2 5.5 %copy-start.13 = (s32[1,512]{1,0:T(1,128)S(1)}, s32[1,512]{1,0:T(1,128)}, u32[]{:S(2)}) copy-start(s32[1,512]{1,0:T(1,128)} %param.26) | copy-start | bytes 6148
  7.3 5.6 %copy-start.14 = (s32[1,512]{1,0:T(1,128)S(1)}, s32[1,512]{1,0:T(1,128)}, u32[]{:S(2)}) copy-start(s32[1,512]{1,0:T(1,128)} %param.27) | copy-start | bytes 6148
  7.3 5.6 %copy-start.12 = (bf16[1,2,1024]{2,1,0:T(2,128)(2,1)S(1)}, bf16[1,2,1024]{2,1,0:T(2,128)(2,1)}, u32[]{:S(2)}) copy-start(bf16[1,2,1024]{2,1,0:T(2,128)(2,1)} %param.25) | copy-start | bytes 12292
  7.3 5.6 %copy-start.1 = (bf16[32,6144]{1,0:T(8,128)(2,1)S(1)}, bf16[32,6144]{1,0:T(8,128)(2,1)}, u32[]{:S(2)}) copy-start(bf16[32,6144]{1,0:T(8,128)(2,1)} %refs_13_.1) | copy-start | bytes 1179652
  7.3 192.4 %all-gather.2.cloned.1.call-start = ((), (), s32[]{:S(2)}) async-start(), calls=%async_computation.4 | async-start | bytes 10813440 | tf_op jit(solution)/shard_map/all_gather | solution.py:834
  8.8 80.2 %copy-start.15 = (s32[1,512]{1,0:T(1,128)S(1)}, s32[1,512]{1,0:T(1,128)}, u32[]{:S(2)}) copy-start(s32[1,512]{1,0:T(1,128)} %param.28) | copy-start | bytes 6148
  84.8 2.6 copy-start
  87.4 0.6 copy-start.2
  103.0 40.9 %all-to-all-start = ((bf16[4,512,768]{2,1,0:T(8,128)(2,1)}), bf16[4,512,768]{2,1,0:T(8,128)(2,1)S(1)}, u32[]{:S(2)}, u32[]{:S(2)}) async-start(bf16[4,512,768]{2,1,0:T(8,128)(2,1)} %get-tuple-element.88), calls=%async_computation | async-start | bytes 6291456 | tf_op jit(solution)/shard_map/all_to_all | solution.py:847
  143.8 1.8 copy-start.3
  180.6 18.0 %all-to-all-start.1 = ((bf16[4,512,256]{2,1,0:T(8,128)(2,1)}), bf16[4,512,256]{2,1,0:T(8,128)(2,1)S(1)}, u32[]{:S(2)}, u32[]{:S(2)}) async-start(bf16[4,512,256]{2,1,0:T(8,128)(2,1)} %bitcast.86), calls=%async_computation.1 | async-start | bytes 2097152 | tf_op jit(solution)/shard_map/all_to_all | solution.py:853
  184.1 271.5 %reduce-scatter.2.cloned.1.call-start = ((), (), s32[]{:S(2)}) async-start(), calls=%async_computation.5 | async-start | bytes 6488064 | tf_op jit(solution)/shard_map/reduce_scatter | solution.py:856
  242.4 1.2 copy-start.6
  244.7 18.1 %all-to-all-start.2 = ((bf16[4,512,256]{2,1,0:T(8,128)(2,1)}), bf16[4,512,256]{2,1,0:T(8,128)(2,1)S(1)}, u32[]{:S(2)}, u32[]{:S(2)}) async-start(bf16[4,512,256]{2,1,0:T(8,128)(2,1)} %bitcast.68), calls=%async_computation.2 | async-start | bytes 2097152 | tf_op jit(solution)/shard_map/all_to_all | solution.py:857
  262.8 1.0 copy-start.4
  444.1 4.3 copy-start.8
  445.5 6.4 %copy-start.9 = (f32[4,8,16,128]{3,2,1,0:T(8,128)S(1)}, f32[4,8,16,128]{3,2,1,0:T(8,128)}, u32[]{:S(2)}) copy-start(f32[4,8,16,128]{3,2,1,0:T(8,128)} %get-tuple-element.100) | copy-start | bytes 786436
  445.5 7.8 %copy-start.11 = (f32[8,768]{1,0:T(8,128)S(1)}, f32[8,768]{1,0:T(8,128)}, u32[]{:S(2)}) copy-start(f32[8,768]{1,0:T(8,128)} %get-tuple-element.102) | copy-start | bytes 73732
  448.4 10.7 %copy-start.5 = (f32[512,1024]{1,0:T(8,128)S(1)}, f32[512,1024]{1,0:T(8,128)}, u32[]{:S(2)}) copy-start(f32[512,1024]{1,0:T(8,128)} %get-tuple-element.99) | copy-start | bytes 6291460
  452.0 8.5 %copy-start.7 = (f32[32,6144]{1,0:T(8,128)S(1)}, f32[32,6144]{1,0:T(8,128)}, u32[]{:S(2)}) copy-start(f32[32,6144]{1,0:T(8,128)} %get-tuple-element.154) | copy-start | bytes 2359300
Sparse Core Ops, SparseCore 0:
  12.3 112.7 all-gather.1
  242.6 121.1 reduce-scatter.1

commit v5 on v4

--- a/solution.py
+++ b/solution.py
@@ -3,6 +3,7 @@
 
 import jax
 import jax.numpy as jnp
+import numpy as np
 from jax import lax
 from jax.experimental import pallas as pl
 from jax.experimental.pallas import tpu as pltpu
@@ -26,40 +27,30 @@
 LOG2E=math.log2(math.e)
 NEG=-1e30
 
-def fwd_kernel(lo_ref,hi_ref,qkv_ref,auxq_ref,auxk_ref,o_ref,lse_ref,k2,vx,q2,s_scr,m_scr,acc,*,T,nh):
+def only(x,h):
+    lane=lax.broadcasted_iota(jnp.int32,x.shape,1)
+    return jnp.where((lane<HD) if h%2==0 else (lane>=HD),x,jnp.zeros_like(x))
+
+def fwd_kernel(lo_ref,hi_ref,qkv_ref,auxq_ref,auxk_ref,o_ref,lse_ref,qs,s_scr,m_scr,acc,*,T,nh):
     qt=pl.program_id(0)
     W=nh*HD
-    L=qkv_ref.shape[0]
-    nk=L//T
     lane=lax.broadcasted_iota(jnp.int32,(T,128),1)
-    @pl.when(qt==0)
-    def _():
-        @pl.loop(0,nk)
-        def _(t):
-            r=pl.ds(pl.multiple_of(t*T,T),T)
-            for h in range(nh):
-                k=qkv_ref[r,W+h*HD:W+(h+1)*HD]
-                k2[h,t]=jnp.concatenate([k,k],axis=1)
-                v=qkv_ref[r,2*W+h*HD:2*W+(h+1)*HD]
-                one=jnp.where(lax.broadcasted_iota(jnp.int32,(T,HD),1)==0,1.0,0.0).astype(bf)
-                vx[h,t]=jnp.concatenate([v,one],axis=1)
     lo=lo_ref[qt]; hi=hi_ref[qt]
-    r=pl.ds(pl.multiple_of(qt*T,T),T)
+    rq=pl.ds(pl.multiple_of(qt*T,T),T)
+    def key(kt,h): return qkv_ref[pl.ds(pl.multiple_of(kt*T,T),T),W+h//2*128:W+(h//2+1)*128]
+    def value(kt,h): return qkv_ref[pl.ds(pl.multiple_of(kt*T,T),T),2*W+h//2*128:2*W+(h//2+1)*128]
     for h in range(nh):
-        q=qkv_ref[r,h*HD:(h+1)*HD].astype(f32)*(HD**-0.5*LOG2E)
-        qh=q.astype(bf)
-        ql=(q-qh.astype(f32)).astype(bf)
-        q2[h]=jnp.concatenate([qh,ql],axis=1)
-    auxq=auxq_ref[r,:]
+        qs[h]=only(qkv_ref[rq,h//2*128:(h//2+1)*128],h)*jnp.asarray(HD**-0.5,bf)
+    auxq=auxq_ref[rq,:]
     eye=lax.broadcasted_iota(jnp.int32,(T,T),0)==lax.broadcasted_iota(jnp.int32,(T,T),1)
     def mx(s):
         m=s[:,:128]
         for j in range(1,T//128): m=jnp.maximum(m,s[:,j*128:(j+1)*128])
         return m
-    ak=auxk_ref[r,:]
+    ak=auxk_ref[rq,:]
     for h in range(nh):
-        raw=dot(q2[h],k2[h,qt],NT)
-        s=dot(jnp.concatenate([q2[h],auxq],axis=1),jnp.concatenate([k2[h,qt],ak],axis=1),NT)
+        raw=dot(qs[h],key(qt,h),NT)
+        s=dot(jnp.concatenate([qs[h],auxq],axis=1),jnp.concatenate([key(qt,h),ak],axis=1),NT)
         s=jnp.where(eye,raw,s)
         s_scr[h,qt]=s
         m_scr[h]=mx(s)
@@ -68,24 +59,27 @@
         kt=jnp.where(t>=qt,t+1,t)
         ak=auxk_ref[pl.ds(pl.multiple_of(kt*T,T),T),:]
         for h in range(nh):
-            s=dot(jnp.concatenate([q2[h],auxq],axis=1),jnp.concatenate([k2[h,kt],ak],axis=1),NT)
+            s=dot(jnp.concatenate([qs[h],auxq],axis=1),jnp.concatenate([key(kt,h),ak],axis=1),NT)
             s_scr[h,kt]=s
             m_scr[h]=jnp.maximum(m_scr[h],mx(s))
     for h in range(nh):
         m_scr[h]=jnp.broadcast_to(jnp.max(m_scr[h],axis=1,keepdims=True),(T,128))
-        acc[h]=jnp.zeros((T,128),f32)
+        acc[h]=jnp.zeros((T,256),f32)
+    ones=jnp.ones((T,128),bf)
     @pl.loop(lo,hi)
     def _(kt):
         for h in range(nh):
             s=s_scr[h,kt]; m=m_scr[h]
-            p=jnp.exp2(s-jnp.concatenate([m]*(T//128),axis=1)).astype(bf)
-            acc[h]+=dot(p,vx[h,kt])
+            p=jnp.exp2((s-jnp.concatenate([m]*(T//128),axis=1))*LOG2E).astype(bf)
+            acc[h]+=dot(p,jnp.concatenate([value(kt,h),ones],axis=1))
     lse=jnp.zeros((T,128),f32)
-    for h in range(nh):
-        a=acc[h]
-        l=a[:,HD:HD+1]
-        o_ref[:,h*HD:(h+1)*HD]=(a[:,:HD]/l).astype(bf)
-        lse=jnp.where(lane==h,m_scr[h]+jnp.log2(l),lse)
+    for g in range(nh//2):
+        o=[]
+        for h in (2*g,2*g+1):
+            l=acc[h,:,128:]
+            o.append(acc[h,:,:128]/l)
+            lse=jnp.where(lane==h,m_scr[h]+jnp.log(l),lse)
+        o_ref[:,g*128:(g+1)*128]=jnp.where(lane<HD,o[0],o[1]).astype(bf)
     lse_ref[...]=lse
 
 def attn_fwd(qkv,lo,hi,auxq,auxk,T):
@@ -96,19 +90,18 @@
         grid_spec=pltpu.PrefetchScalarGridSpec(num_scalar_prefetch=2,grid=(nk,),
             in_specs=[pl.BlockSpec((L,W3),lambda i,*_:(0,0)),pl.BlockSpec((L,128),lambda i,*_:(0,0)),pl.BlockSpec((L,128),lambda i,*_:(0,0))],
             out_specs=[pl.BlockSpec((T,W),lambda i,*_:(i,0)),pl.BlockSpec((T,128),lambda i,*_:(i,0))],
-            scratch_shapes=[pltpu.VMEM((nh,nk,T,128),bf),pltpu.VMEM((nh,nk,T,128),bf),pltpu.VMEM((nh,T,128),bf),
-                pltpu.VMEM((nh,nk,T,T),f32),pltpu.VMEM((nh,T,128),f32),pltpu.VMEM((nh,T,128),f32)]),
+            scratch_shapes=[pltpu.VMEM((nh,T,128),bf),pltpu.VMEM((nh,nk,T,T),f32),pltpu.VMEM((nh,T,128),f32),pltpu.VMEM((nh,T,256),f32)]),
         compiler_params=pltpu.CompilerParams(vmem_limit_bytes=60*2**20),
         name="attn_fwd",
     )(lo,hi,qkv,auxq,auxk)
 
-def bwd_kernel(lo_ref,hi_ref,qkv_ref,o_ref,do_ref,lse_ref,auxq_ref,auxk_ref,dqkv_ref,q2,qa,k2,dox,vx,kT,dqT,dk,dv,*,T,nh):
+def bwd_kernel(lo_ref,hi_ref,qkv_ref,o_ref,do_ref,lse_ref,auxq_ref,auxk_ref,dqkv_ref,qs,qa,dos,dd,kT,dqT,dk,dv,*,T,nh):
     kt=pl.program_id(0)
     W=nh*HD
     L=qkv_ref.shape[0]
     nk=L//T
     lane=lax.broadcasted_iota(jnp.int32,(T,128),1)
-    lane64=lax.broadcasted_iota(jnp.int32,(T,HD),1)
+    def pair(ref,t,h,at=0): return ref[pl.ds(pl.multiple_of(t*T,T),T),at+h//2*128:at+(h//2+1)*128]
     @pl.when(kt==0)
     def _():
         dqT[...]=jnp.zeros_like(dqT)
@@ -119,43 +112,33 @@
             aq=auxq_ref[r,:].astype(f32)
             kT[t]=qkv_ref[r,W:2*W].T
             for h in range(nh):
-                q=qkv_ref[r,h*HD:(h+1)*HD].astype(f32)*(HD**-0.5*LOG2E)
-                qh=q.astype(bf)
-                ql=(q-qh.astype(f32)).astype(bf)
-                q2[h,t]=jnp.concatenate([qh,ql],axis=1)
-                k=qkv_ref[r,W+h*HD:W+(h+1)*HD]
-                k2[h,t]=jnp.concatenate([k,k],axis=1)
-                v=qkv_ref[r,2*W+h*HD:2*W+(h+1)*HD]
-                vx[h,t]=jnp.concatenate([v,jnp.where(lane64<2,1.0,0.0).astype(bf)],axis=1)
+                qs[h,t]=only(pair(qkv_ref,t,h),h)*jnp.asarray(HD**-0.5,bf)
                 nl=-lse[:,h:h+1]
                 l1=nl.astype(bf).astype(f32); l2=(nl-l1).astype(bf).astype(f32); l3=nl-l1-l2
                 qa[h,t]=jnp.where(lane==0,l1,jnp.where(lane==1,l2,jnp.where(lane==2,l3,aq))).astype(bf)
-                do=do_ref[r,h*HD:(h+1)*HD]
-                nd=-jnp.sum(do.astype(f32)*o_ref[r,h*HD:(h+1)*HD].astype(f32),axis=1,keepdims=True)
+                do=only(pair(do_ref,t,h),h)
+                dos[h,t]=do
+                nd=-jnp.sum(do.astype(f32)*pair(o_ref,t,h).astype(f32),axis=1,keepdims=True)
                 d1=nd.astype(bf).astype(f32); d2=nd-d1
-                dox[h,t]=jnp.concatenate([do,jnp.where(lane64==0,d1,jnp.where(lane64==1,d2,0.0)).astype(bf)],axis=1)
+                dd[h,t]=jnp.where(lane==0,d1,jnp.where(lane==1,d2,0.0)).astype(bf)
     r=pl.ds(pl.multiple_of(kt*T,T),T)
     ak=auxk_ref[r,:]
+    av=jnp.where(lane<2,1.0,0.0).astype(bf)
     lo=lo_ref[kt]; hi=hi_ref[kt]
     def tile(qt,diag):
-        rq=pl.ds(pl.multiple_of(qt*T,T),T)
         for h in range(nh):
-            kx=jnp.concatenate([k2[h,kt],ak],axis=1)
-            s=dot(kx,jnp.concatenate([q2[h,qt],qa[h,qt]],axis=1),NT)
+            kx=jnp.concatenate([pair(qkv_ref,kt,h,W),ak],axis=1)
+            s=dot(kx,jnp.concatenate([qs[h,qt],qa[h,qt]],axis=1),NT)
             if diag:
                 eye=lax.broadcasted_iota(jnp.int32,(T,T),0)==lax.broadcasted_iota(jnp.int32,(T,T),1)
                 qr=jnp.where(lane<3,qa[h,qt].astype(f32),0.0).astype(bf)
-                raw=dot(kx,jnp.concatenate([q2[h,qt],qr],axis=1),NT)
+                raw=dot(kx,jnp.concatenate([qs[h,qt],qr],axis=1),NT)
                 s=jnp.where(eye,raw,s)
-            p=jnp.exp2(s)
-            dp=dot(vx[h,kt],dox[h,qt],NT)
+            p=jnp.exp2(s*LOG2E)
+            dp=dot(jnp.concatenate([pair(qkv_ref,kt,h,2*W),av],axis=1),jnp.concatenate([dos[h,qt],dd[h,qt]],axis=1),NT)
             ds=(p*dp).astype(bf)
-            pb=p.astype(bf)
-            g=h//2
-            rv=dot(pb,do_ref[rq,g*128:(g+1)*128])
-            rk=dot(ds,qkv_ref[rq,g*128:(g+1)*128])
-            dv[h]+=rv
-            dk[h]+=rk
+            dv[h]+=dot(p.astype(bf),pair(do_ref,qt,h))
+            dk[h]+=dot(ds,pair(qkv_ref,qt,h))
             dqT[qt,h*HD:(h+1)*HD,:]+=dot(kT[kt,h*HD:(h+1)*HD,:],ds)
     dk[...]=jnp.zeros_like(dk); dv[...]=jnp.zeros_like(dv)
     tile(kt,True)
@@ -180,7 +163,7 @@
         grid_spec=pltpu.PrefetchScalarGridSpec(num_scalar_prefetch=2,grid=(nk,),
             in_specs=[full(W3),full(W),full(W),full(128),full(128),full(128)],
             out_specs=full(W3),
-            scratch_shapes=[pltpu.VMEM((nh,nk,T,128),bf)]*5+[pltpu.VMEM((nk,W,T),bf),pltpu.VMEM((nk,W,T),f32),
+            scratch_shapes=[pltpu.VMEM((nh,nk,T,128),bf)]*4+[pltpu.VMEM((nk,W,T),bf),pltpu.VMEM((nk,W,T),f32),
                 pltpu.VMEM((nh,T,128),f32),pltpu.VMEM((nh,T,128),f32)]),
         compiler_params=pltpu.CompilerParams(vmem_limit_bytes=60*2**20),
         name="attn_bwd",
@@ -252,122 +235,6 @@
         compiler_params=pltpu.CompilerParams(vmem_limit_bytes=60*2**20),name="qkv_proj",
         cost_estimate=pl.CostEstimate(flops=2*F*D*3*D,bytes_accessed=14*2**20,transcendentals=0))(x,seg,emb,w,b,cos,sin)
 
-def mid_kernel(x_ref,a_ref,c_ref,seg_ref,msk_ref,emb_ref,w_ref,bo_ref,bu_ref,bd_ref,
-               out_ref,dm_ref,da_ref,gu_ref,gw_ref,gb_ref,ge_ref,
-               wo_ref,wu_ref,wd_ref,n2s,acts,dhs,dfs,dps,dgelu,sem,*,R):
-    F,D=x_ref.shape; H=bu_ref.shape[1]; CH=512
-    loads=[pltpu.make_async_copy(w_ref.at[:,pl.ds(o,n)],r,sem.at[i]) for i,(o,n,r) in enumerate(((2*H,D,wo_ref),(0,H,wu_ref),(H,H,wd_ref)))]
-    for l in loads: l.start()
-    gb_ref[...]=jnp.zeros_like(gb_ref); ge_ref[...]=jnp.zeros_like(ge_ref)
-    for l in loads: l.wait()
-    def down(j):
-        t,o=divmod(j*CH,D)
-        return slice(o,o+CH),slice(t*D,(t+1)*D)
-    @pl.loop(0,F//R)
-    def _(i):
-        r=pl.ds(pl.multiple_of(i*R,R),R)
-        seg=seg_ref[r,:]; msk=msk_ref[r,:]
-        def acc(k,x):
-            a,b=sums(x,seg)
-            ge_ref[0:1,k*D:(k+1)*D]+=a; ge_ref[1:2,k*D:(k+1)*D]+=b
-        branch=(dot(a_ref[r,:],wo_ref[...])+bo_ref[0:1,:])*msk
-        g1=pick(seg,emb_ref,2,D)
-        middle=x_ref[r,:].astype(f32)+g1*branch
-        n,rs=moments(middle)
-        sc2=1.0+pick(seg,emb_ref,4,D)
-        n2=(n*sc2+pick(seg,emb_ref,3,D)).astype(bf)
-        n2s[r,:]=n2
-        feed=jnp.broadcast_to(bd_ref[0:1,:],(R,D))
-        for j in range(H//CH):
-            c=slice(j*CH,(j+1)*CH)
-            h=dot(n2,wu_ref[:,c])+bu_ref[0:1,c]
-            a,g=gelu_both(h)
-            a=a.astype(bf)
-            acts[r,c]=a; dgelu[:,c]=g
-            feed+=dot(a,wd_ref[down(j)])
-        up=c_ref[r,:].astype(f32)
-        g2=pick(seg,emb_ref,5,D)
-        out_ref[r,:]=(middle+g2*feed).astype(bf)
-        df=(up*g2).astype(bf)
-        dfs[r,:]=df
-        acc(3,up*feed)
-        gb_ref[2:3,0:D]+=jnp.sum(df.astype(f32),0,keepdims=True)
-        dn=jnp.zeros((R,D),f32)
-        for j in range(H//CH):
-            c=slice(j*CH,(j+1)*CH)
-            dh=(dot(df,wd_ref[down(j)],NT)*dgelu[:,c]).astype(bf)
-            dhs[r,c]=dh
-            gb_ref[1:2,c]+=jnp.sum(dh.astype(f32),0,keepdims=True)
-            dn+=dot(dh,wu_ref[:,c],NT)
-        acc(1,dn); acc(2,dn*n)
-        dn=dn*sc2
-        dmid=up+(dn-jnp.mean(dn,-1,keepdims=True)-n*jnp.mean(dn*n,-1,keepdims=True))*rs
-        dm_ref[r,:]=dmid
-        acc(0,dmid*branch)
-        dp=(dmid*g1*msk).astype(bf)
-        dps[r,:]=dp
-        gb_ref[0:1,0:D]+=jnp.sum(dp.astype(f32),0,keepdims=True)
-        da_ref[r,:]=dot(dp,wo_ref[...],NT).astype(bf)
-    @pl.loop(0,D//256)
-    def _(i):
-        c=pl.ds(pl.multiple_of(i*256,256),256)
-        gw_ref[c,H:H+D]=dot(a_ref[:,c],dps[...],TN).astype(bf)
-        gu_ref[c,:]=dot(n2s[:,c],dhs[...],TN).astype(bf)
-        for t in range(H//D):
-            e=pl.ds(pl.multiple_of(t*D+i*256,256),256)
-            gw_ref[c,t*D:(t+1)*D]=dot(acts[:,e],dfs[...],TN).astype(bf)
-
-def mid(x,a,c,seg,msk,emb,w,bo,bu,bd,R=128):
-    F,D=x.shape; H=bu.shape[1]
-    S=jax.ShapeDtypeStruct; M=pltpu.VMEM
-    return pl.pallas_call(functools.partial(mid_kernel,R=R),
-        out_shape=(S((F,D),bf),S((F,D),f32),S((F,D),bf),S((D,H),bf),S((D,H+D),bf),S((8,H),f32),S((8,4*D),f32)),
-        in_specs=[V]*6+[ANY]+[V]*3,out_specs=(V,)*7,
-        scratch_shapes=[M((D,D),bf),M((D,H),bf),M((D,H),bf),M((F,D),bf),M((F,H),bf),M((F,H),bf),M((F,D),bf),M((F,D),bf),M((R,H),f32),pltpu.SemaphoreType.DMA((3,))],
-        compiler_params=pltpu.CompilerParams(vmem_limit_bytes=62*2**20),name="mid",
-        cost_estimate=pl.CostEstimate(flops=6*F*D*(D+2*H),bytes_accessed=30*2**20,transcendentals=F*H))(x,a,c,seg,msk,emb,w,bo,bu,bd)
-
-def tail_kernel(x_ref,n1_ref,dm_ref,g_ref,seg_ref,emb_ref,w_ref,cos_ref,sin_ref,gf_ref,gw_ref,gb_ref,ge_ref,dps,*,R,nd,W):
-    F,D=x_ref.shape
-    gb_ref[...]=jnp.zeros_like(gb_ref); ge_ref[...]=jnp.zeros_like(ge_ref)
-    @pl.loop(0,F//R)
-    def _(i):
-        r=pl.ds(pl.multiple_of(i*R,R),R)
-        seg=seg_ref[r,:]
-        cos=jnp.concatenate([cos_ref[r,:]]*(W//128),1); sin=jnp.concatenate([sin_ref[r,:]]*(W//128),1)
-        dn=jnp.zeros((R,D),f32)
-        for d in range(nd):
-            for j in range(3):
-                c=(d*3+j)*W
-                v=g_ref[d,r,j*W:(j+1)*W]
-                if j<2:
-                    v=v.astype(f32)
-                    v=(v*cos-partner(v)*sin).astype(bf)
-                dps[r,c:c+W]=v
-                gb_ref[0:1,c:c+W]+=jnp.sum(v.astype(f32),0,keepdims=True)
-        for j in range(3*D//512):
-            dn+=dot(dps[r,j*512:(j+1)*512],w_ref[:,j*512:(j+1)*512],NT)
-        n,rs=moments(x_ref[r,:].astype(f32))
-        for k,x in ((0,dn),(1,dn*n)):
-            a,b=sums(x,seg)
-            ge_ref[0:1,k*D:(k+1)*D]+=a; ge_ref[1:2,k*D:(k+1)*D]+=b
-        dn=dn*(1.0+pick(seg,emb_ref,1,D))
-        gf_ref[r,:]=dm_ref[r,:]+(dn-jnp.mean(dn,-1,keepdims=True)-n*jnp.mean(dn*n,-1,keepdims=True))*rs
-    @pl.loop(0,D//256)
-    def _(i):
-        c=pl.ds(pl.multiple_of(i*256,256),256)
-        for j in range(3):
-            gw_ref[c,j*D:(j+1)*D]=dot(n1_ref[:,c],dps[:,j*D:(j+1)*D],TN).astype(bf)
-
-def tail(x,n1,dm,g,seg,emb,w,cos,sin,R=128):
-    F,D=x.shape; nd=g.shape[0]; W=D//nd
-    S=jax.ShapeDtypeStruct
-    return pl.pallas_call(functools.partial(tail_kernel,R=R,nd=nd,W=W),
-        out_shape=(S((F,D),f32),S((D,3*D),bf),S((8,3*D),f32),S((8,2*D),f32)),
-        in_specs=[V]*9,out_specs=(V,)*4,
-        scratch_shapes=[pltpu.VMEM((F,3*D),bf)],
-        compiler_params=pltpu.CompilerParams(vmem_limit_bytes=60*2**20),name="tail",
-        cost_estimate=pl.CostEstimate(flops=4*F*D*3*D,bytes_accessed=20*2**20,transcendentals=0))(x,n1,dm,g,seg,emb,w,cos,sin)
 
 def sizes(nd,ns):
     Y=2**((ns.bit_length()-1)//2)
@@ -564,6 +431,107 @@
     return pl.pallas_call(functools.partial(entry_kernel,nd,ns,nw),out_shape=tuple(outs),
         in_specs=[ANY]*(nw+1)+[V,ANY,V],out_specs=tuple([ANY]*(nw+2)+[V,V]),scratch_shapes=scr,
         compiler_params=pltpu.CompilerParams(collective_id=0,has_side_effects=True,vmem_limit_bytes=40*2**20),name="entry")(*shards,bias,time,ids,wada)
+
+def make_remote(src,dst,ss,rs,dev):
+    return pltpu.make_async_remote_copy(src_ref=src,dst_ref=dst,send_sem=ss,recv_sem=rs,device_id=dev,device_id_type=pl.DeviceIdType.MESH)
+
+def mid_kernel(o_ref,x_ref,c_ref,seg_ref,msk_ref,emb_ref,w_ref,bo_ref,bu_ref,bd_ref,
+               out_ref,dm_ref,do_ref,gu_ref,gw_ref,gb_ref,ge_ref,
+               wo_ref,wu_ref,wd_ref,n2s,acts,dhs,dfs,dps,dgelu,a_ref,da_ref,sem,s1,s2,s3,t1,t2,t3,*,R,nd,ns):
+    F,D=x_ref.shape; H=bu_ref.shape[1]; CH=512
+    loads=[pltpu.make_async_copy(w_ref.at[:,pl.ds(o,n)],r,sem.at[i]) for i,(o,n,r) in enumerate(((2*H,D,wo_ref),(0,H,wu_ref),(H,H,wd_ref)))]
+    p=Place(nd,ns); W=D//nd; NR=F//R
+    b=pltpu.get_barrier_semaphore()
+    for d in range(1,nd): pl.semaphore_signal(b,inc=1,device_id=(lax.rem(p.h+d,nd),p.s),device_id_type=pl.DeviceIdType.MESH)
+    pl.semaphore_wait(b,nd-1)
+    def rows(i): return pl.ds(pl.multiple_of(i*R,R),R)
+    def cols(h): return pl.ds(pl.multiple_of(h*W,W),W)
+    def arrive(i):
+        return [make_remote(o_ref.at[lax.rem(p.h+d,nd),rows(i)],a_ref.at[rows(i),cols(p.h)],s1.at[i,d],s2.at[i,d],(lax.rem(p.h+d,nd),p.s)) for d in range(1,nd)]
+    def kept(i): return pltpu.make_async_copy(o_ref.at[p.h,rows(i)],a_ref.at[rows(i),cols(p.h)],s3.at[i])
+    def leave(i):
+        return [make_remote(da_ref.at[rows(i),cols(lax.rem(p.h+d,nd))],do_ref.at[p.h,rows(i)],t1.at[i,d],t2.at[i,d],(lax.rem(p.h+d,nd),p.s)) for d in range(1,nd)]
+    def stays(i): return pltpu.make_async_copy(da_ref.at[rows(i),cols(p.h)],do_ref.at[p.h,rows(i)],t3.at[i])
+    for c in arrive(0)+[kept(0)]: c.start()
+    for l in loads: l.start()
+    gb_ref[...]=jnp.zeros_like(gb_ref); ge_ref[...]=jnp.zeros_like(ge_ref)
+    for l in loads: l.wait()
+    def down(j):
+        t,o=divmod(j*CH,D)
+        return slice(o,o+CH),slice(t*D,(t+1)*D)
+    @pl.loop(0,F//R)
+    def _(i):
+        r=rows(i)
+        for c in arrive(i): c.wait_recv()
+        kept(i).wait()
+        @pl.when(i+1<NR)
+        def _():
+            for c in arrive(i+1)+[kept(i+1)]: c.start()
+        seg=seg_ref[r,:]; msk=msk_ref[r,:]
+        def acc(k,x):
+            a,b=sums(x,seg)
+            ge_ref[0:1,k*D:(k+1)*D]+=a; ge_ref[1:2,k*D:(k+1)*D]+=b
+        branch=(dot(a_ref[r,:],wo_ref[...])+bo_ref[0:1,:])*msk
+        g1=pick(seg,emb_ref,2,D)
+        middle=x_ref[r,:].astype(f32)+g1*branch
+        n,rs=moments(middle)
+        sc2=1.0+pick(seg,emb_ref,4,D)
+        n2=(n*sc2+pick(seg,emb_ref,3,D)).astype(bf)
+        n2s[r,:]=n2
+        feed=jnp.broadcast_to(bd_ref[0:1,:],(R,D))
+        for j in range(H//CH):
+            c=slice(j*CH,(j+1)*CH)
+            h=dot(n2,wu_ref[:,c])+bu_ref[0:1,c]
+            a,g=gelu_both(h)
+            a=a.astype(bf)
+            acts[r,c]=a; dgelu[:,c]=g
+            feed+=dot(a,wd_ref[down(j)])
+        up=c_ref[r,:].astype(f32)
+        g2=pick(seg,emb_ref,5,D)
+        out_ref[r,:]=(middle+g2*feed).astype(bf)
+        df=(up*g2).astype(bf)
+        dfs[r,:]=df
+        acc(3,up*feed)
+        gb_ref[2:3,0:D]+=jnp.sum(df.astype(f32),0,keepdims=True)
+        dn=jnp.zeros((R,D),f32)
+        for j in range(H//CH):
+            c=slice(j*CH,(j+1)*CH)
+            dh=(dot(df,wd_ref[down(j)],NT)*dgelu[:,c]).astype(bf)
+            dhs[r,c]=dh
+            gb_ref[1:2,c]+=jnp.sum(dh.astype(f32),0,keepdims=True)
+            dn+=dot(dh,wu_ref[:,c],NT)
+        acc(1,dn); acc(2,dn*n)
+        dn=dn*sc2
+        dmid=up+(dn-jnp.mean(dn,-1,keepdims=True)-n*jnp.mean(dn*n,-1,keepdims=True))*rs
+        dm_ref[r,:]=dmid
+        acc(0,dmid*branch)
+        dp=(dmid*g1*msk).astype(bf)
+        dps[r,:]=dp
+        gb_ref[0:1,0:D]+=jnp.sum(dp.astype(f32),0,keepdims=True)
+        da_ref[r,:]=dot(dp,wo_ref[...],NT).astype(bf)
+        for c in leave(i)+[stays(i)]: c.start()
+    @pl.loop(0,D//256)
+    def _(i):
+        c=pl.ds(pl.multiple_of(i*256,256),256)
+        gw_ref[c,H:H+D]=dot(a_ref[:,c],dps[...],TN).astype(bf)
+        gu_ref[c,:]=dot(n2s[:,c],dhs[...],TN).astype(bf)
+        for t in range(H//D):
+            e=pl.ds(pl.multiple_of(t*D+i*256,256),256)
+            gw_ref[c,t*D:(t+1)*D]=dot(acts[:,e],dfs[...],TN).astype(bf)
+    for i in range(NR):
+        for c in arrive(i): c.wait_send()
+        for c in leave(i)+[stays(i)]: c.wait()
+
+def mid(nd,ns,o,x,c,seg,msk,emb,w,bo,bu,bd,R=256):
+    F,D=x.shape; H=bu.shape[1]; NR=F//R; A=pltpu.SemaphoreType.DMA
+    S=jax.ShapeDtypeStruct; M=pltpu.VMEM
+    return pl.pallas_call(functools.partial(mid_kernel,R=R,nd=nd,ns=ns),
+        out_shape=(S((F,D),bf),S((F,D),f32),S((nd,F,D//nd),bf),S((D,H),bf),S((D,H+D),bf),S((8,H),f32),S((8,4*D),f32)),
+        in_specs=[ANY]+[V]*5+[ANY]+[V]*3,out_specs=(V,V,ANY)+(V,)*4,
+        scratch_shapes=[M((D,D),bf),M((D,H),bf),M((D,H),bf),M((F,D),bf),M((F,H),bf),M((F,H),bf),M((F,D),bf),M((F,D),bf),M((R,H),f32),M((F,D),bf),M((F,D),bf),A((3,)),A((NR,nd)),A((NR,nd)),A((NR,)),A((NR,nd)),A((NR,nd)),A((NR,))],
+        compiler_params=pltpu.CompilerParams(collective_id=2,has_side_effects=True,vmem_limit_bytes=62*2**20),name="mid",
+        cost_estimate=pl.CostEstimate(flops=6*F*D*(D+2*H),bytes_accessed=30*2**20,transcendentals=F*H))(o,x,c,seg,msk,emb,w,bo,bu,bd)
+
 
 ORD_X=-1
 QW=512
@@ -849,12 +817,9 @@
     qlo,qhi,klo,khi=tables(seg_row,msk_row,T)
     aq,ak=aux(seg_row,msk_row)
     o,lse=attn_fwd(qkv,qlo,qhi,aq,ak,T)
-    def back(a):
-        return lax.all_to_all(a.reshape(nd,F,-1),"head",split_axis=0,concat_axis=0,tiled=True)
-    att=back(o).transpose(1,0,2).reshape(F,D)
-    out,dmid,datt,gup,gdo,gb,ge=mid(x,att,cot,segc,mskc,emb,rest_all,bo,bu,bd)
+    out,dmid,do,gup,gdo,gb,ge=mid(nd,ns,o.reshape(nd,F,W),x,cot,segc,mskc,emb,rest_all,bo,bu,bd)
+    do=do.reshape(nd*F,W)
     gdo=lax.psum_scatter(gdo,HS,scatter_dimension=0,tiled=True).astype(f32)
-    do=lax.all_to_all(datt.reshape(F,nd,W).transpose(1,0,2),"head",split_axis=0,concat_axis=0,tiled=True).reshape(nd*F,W)
     dqkv=attn_bwd(qkv,o,do,lse,klo,khi,aq,ak,T)
     gx,gup,gqkv,gbias,gada,gbada,dact=final(nd,ns,dqkv.reshape(nd,F,3*W),gup.reshape(X,2,Z,Y,K,H),x,normed,dmid,wq,cos,sin,segc,emb,gb,ge,act,w_ada)
     dact=dact[:,:,:,:K].reshape(N,8,2,K).sum(1).transpose(1,0,2).reshape(2,D)

time: 476 us -> 429 us (0.901); the launches traced: 469 us -> 426 us
  waiting for transfers between devices: 57.7 us -> 29.5 us
  starting transfers between devices: 11.2 us -> 3.78 us
    all_to_all x2 -> x0, waiting for transfers between devices: 25 us -> none  [the longest x1 13.9 us: body(): lax.all_to_all(datt.reshape(F, nd, W).transpose(1, 0, 2), 'head', split_a...]
    all_to_all x2 -> x0, starting transfers between devices: 7.24 us -> none  [the longest x1 3.73 us: body(): lax.all_to_all(datt.reshape(F, nd, W).transpose(1, 0, 2), 'head', split_a...]
    pallas_call x1, Pallas kernels: 119 us -> 124 us  [final(): pl.pallas_call(k, out_shape=tuple(outs), in_specs=[ANY] * 6 + [V] * 8, ou...]
    pallas_call x1, Pallas kernels: 42.7 us -> 37.4 us  [mid(): pl.pallas_call(functools.partial(mid_kernel, R=R, nd=nd, ns=ns), out_shap...]
    unnamed x48 -> x45, local copies, waits for them, and re-layouts: 9.5 us -> 9.61 us
  transfers between devices with their start and end apart: 5 -> 3, of which waited for: 3 -> 1; matrix products, arithmetic and copies ran while one was open for 6% -> 6% of each run, Pallas kernels for 64% -> 70%
where the time goes in v5:
time: 429 us; the launch traced here: 426 us
  Pallas kernels  336 us (78%)
  local copies, waits for them, and re-layouts  32.3 us (8%)
  waiting for transfers between devices  29.5 us (7%)
  between operations  14.7 us (3%)
  other arithmetic  9.98 us (2%)
    pallas_call x1, Pallas kernels, final(): pl.pallas_call(k, out_shape=tuple(outs), in_specs=[ANY] * 6 + [V] * 8, ou...  124 us
    pallas_call x1, Pallas kernels, entry(): pl.pallas_call(functools.partial(entry_kernel, nd, ns, nw), out_shape=tup...  71.8 us
    pallas_call x1, Pallas kernels, attn_bwd(): pl.pallas_call(functools.partial(bwd_kernel, T=T, nh=nh), out_shape=jax.S...  59.5 us
    pallas_call x1, Pallas kernels, mid(): pl.pallas_call(functools.partial(mid_kernel, R=R, nd=nd, ns=ns), out_shap...  37.4 us
    pallas_call x1, Pallas kernels, attn_fwd(): pl.pallas_call(functools.partial(fwd_kernel, T=T, nh=nh), out_shape=(jax....  32.7 us
    all_to_all x1, waiting for transfers between devices, body(): lax.all_to_all(packed, 'head', split_axis=0, concat_axis=0, tiled=True)  29.4 us
    pallas_call x1, Pallas kernels, qkv_proj(): pl.pallas_call(functools.partial(qkv_kernel, R=R, nd=nd, W=W), out_shape=...  10.6 us
    unnamed x45, local copies, waits for them, and re-layouts  9.61 us
  transfers between devices with their start and end apart: 3, of which 1 were waited for; matrix products, arithmetic and copies ran while one was open for 6% of the time, Pallas kernels for 70%

profile of v5, /device:TPU:0, one launch (start us, length us, event | category | flops | bytes accessed | tf_op | source)
XLA Modules:
  0.0 426.5 jit_solution(12568265087746622843)
XLA Ops:
  7.3 1.4 reshape.347
  9.4 1.0 copy.113
  10.5 1.6 pad_maximum_fusion
  12.9 71.8 %entry.1 = (bf16[2,2,4,2,32,3072]{5,4,3,2,1,0:T(8,128)(2,1)S(1)}, bf16[32,16,512]{2,1,0:T(8,128)(2,1)S(1)}, s32[4,8,512]{2,1,0:T(8,128)S(1)}, f32[16,768]{1,0:T(8,128)S(1)}, bf16[64,128]{1,0:T(8,128)(2,1)S(1)}) custom-call(bf16[32,3072]{1,0:T(8,128)(2,1)S(1)} %reshape.339.refs_0_, bf16[16,512]{1,0:T(8,128)(2,1)S(1)} %scatter.16.refs_1_, ...), custom_call_target="tpu_custom_call" | custom-call | tf_op jit(solution)/shard_map/entry/pallas_call | solution.py:431
  84.8 2.6 copy-done
  89.0 0.9 copy.111.seg_ref.refs_8_
  89.9 1.8 negate_select_fusion
  92.4 10.6 %qkv_proj.1 = (bf16[512,1024]{1,0:T(8,128)(2,1)}, bf16[4,512,768]{2,1,0:T(8,128)(2,1)}) custom-call(bf16[512,1024]{1,0:T(8,128)(2,1)} %bitcast.78, s32[512,1]{1,0:T(8,128)} %copy.111.seg_ref.refs_8_, f32[2,6144]{1,0:T(2,128)} %broadcast_add_fusion.emb_ref.refs_9_, bf16[1024,3072]{1,0:T(8,128)(2,1)} %bitcast.68, f32[1,3072]{1,0:T(1,128)} %reshape.344.b_ref, ...), custom_call_target="tpu_custom_call" | custom-call | flops 3221225472 | bytes 14680064 | tf_op jit(solution)/shard_map/qkv_proj/pallas_call | solution.py:232
  103.0 3.7 all-to-all-start
  106.8 0.7 reshape.351.bo_ref
  107.5 0.7 reshape.353.bd_ref
  108.3 0.7 reshape.352.bu_ref
  109.0 0.9 copy.116.msk_ref
  111.5 2.9 select_convert_fusion
  114.4 29.4 %all-to-all-done = bf16[4,512,768]{2,1,0:T(8,128)(2,1)S(1)} async-done(((bf16[4,512,768]{2,1,0:T(8,128)(2,1)}), bf16[4,512,768]{2,1,0:T(8,128)(2,1)S(1)}, u32[]{:S(2)}, u32[]{:S(2)}) %all-to-all-start) | async-done | bytes 3145760 | tf_op jit(solution)/shard_map/all_to_all | solution.py:815
  143.8 1.8 copy-done.3
  145.6 32.7 %attn_fwd.1 = (bf16[2048,256]{1,0:T(8,128)(2,1)}, f32[2048,128]{1,0:T(8,128)}) custom-call(s32[4]{0:T(128)} %get-tuple-element.114.lo_ref, s32[4]{0:T(128)} %broadcast_add_fusion.2.hi_ref, bf16[2048,768]{1,0:T(8,128)(2,1)} %bitcast.70, bf16[2048,128]{1,0:T(8,128)(2,1)} %get-tuple-element.131.auxq_ref, bf16[2048,128]{1,0:T(8,128)(2,1)} %get-tuple-element.130.auxk_ref), custom_call_target="tpu_custom_call" | custom-call | tf_op jit(solution)/shard_map/attn_fwd/pallas_call | solution.py:87
  178.3 37.4 %mid.1 = (bf16[512,1024]{1,0:T(8,128)(2,1)}, f32[512,1024]{1,0:T(8,128)}, bf16[4,512,256]{2,1,0:T(8,128)(2,1)}, bf16[1024,2048]{1,0:T(8,128)(2,1)}, bf16[1024,30...) custom-call(bf16[4,512,256]{2,1,0:T(8,128)(2,1)} %bitcast.84, bf16[512,1024]{1,0:T(8,128)(2,1)} %bitcast.79, ...), custom_call_target="tpu_custom_call" | custom-call | flops 16106127360 | bytes 31457280 | tf_op jit(solution)/shard_map/mid/pallas_call | solution.py:528
  216.2 59.5 %attn_bwd.1 = bf16[2048,768]{1,0:T(8,128)(2,1)} custom-call(s32[4]{0:T(128)} %get-tuple-element.113.lo_ref, s32[4]{0:T(128)} %broadcast_add_fusion.1.hi_ref, bf16[2048,768]{1,0:T(8,128)(2,1)} %bitcast.71, bf16[2048,256]{1,0:T(8,128)(2,1)} %get-tuple-element.89.o_ref, bf16[2048,256]{1,0:T(8,128)(2,1)} %bitcast.85, f32[2048,128]{1,0:T(8,128)} %get-tuple-element.92.lse_ref, ...), custom_call_target="tpu_custom_call" | custom-call | tf_op jit(solution)/shard_map/attn_bwd/pallas_call | solution.py:160
  275.6 124.3 %final.1 = (f32[512,1024]{1,0:T(8,128)}, f32[32,2048]{1,0:T(8,128)}, f32[32,3072]{1,0:T(8,128)}, f32[4,8,8,256]{3,2,1,0:T(8,128)}, f32[32,6144]{1,0:T(8,128)}, /...) custom-call(bf16[4,512,768]{2,1,0:T(8,128)(2,1)} %bitcast.72, bf16[2,2,4,2,32,2048]{5,4,3,2,1,0:T(8,128)(2,1)} %bitcast.74, ...), custom_call_target="tpu_custom_call" | custom-call | tf_op jit(solution)/shard_map/final/pallas_call | solution.py:778
  399.9 1.3 reshape.362
  401.3 0.8 copy.121
  402.1 2.1 reshape.363
  404.6 0.9 reshape.361
  405.5 1.0 slice.120
  406.6 0.9 slice_reduce_fusion
  411.5 0.9 slice.135
  412.6 0.8 copy.123
  413.4 1.5 slice.133
  414.9 2.3 copy.148
  417.3 1.3 copy.149
  418.6 0.9 copy.150
  (105 shorter events, 10.8 us)
Async XLA Ops:
  7.2 5.0 %copy-start.8 = (bf16[32,3072]{1,0:T(8,128)(2,1)S(1)}, bf16[32,3072]{1,0:T(8,128)(2,1)}, u32[]{:S(2)}) copy-start(bf16[32,3072]{1,0:T(8,128)(2,1)} %param.31) | copy-start | bytes 589828
  7.2 5.4 %copy-start.18 = (bf16[192]{0:T(256)(128)(2,1)S(1)}, bf16[192]{0:T(256)(128)(2,1)}, u32[]{:S(2)}) copy-start(bf16[192]{0:T(256)(128)(2,1)} %param.30) | copy-start | bytes 1156
  7.2 5.4 %copy-start.14 = (bf16[96]{0:T(256)(128)(2,1)S(1)}, bf16[96]{0:T(256)(128)(2,1)}, u32[]{:S(2)}) copy-start(bf16[96]{0:T(256)(128)(2,1)} %param.32) | copy-start | bytes 580
  7.2 5.4 %copy-start.15 = (bf16[32]{0:T(256)(128)(2,1)S(1)}, bf16[32]{0:T(256)(128)(2,1)}, u32[]{:S(2)}) copy-start(bf16[32]{0:T(256)(128)(2,1)} %param.34) | copy-start | bytes 196
  7.2 5.4 %copy-start.16 = (bf16[64]{0:T(256)(128)(2,1)S(1)}, bf16[64]{0:T(256)(128)(2,1)}, u32[]{:S(2)}) copy-start(bf16[64]{0:T(256)(128)(2,1)} %param.36) | copy-start | bytes 388
  7.2 5.4 %copy-start.17 = (bf16[32]{0:T(256)(128)(2,1)S(1)}, bf16[32]{0:T(256)(128)(2,1)}, u32[]{:S(2)}) copy-start(bf16[32]{0:T(256)(128)(2,1)} %param.38) | copy-start | bytes 196
  7.2 5.5 %copy-start.11 = (s32[1,512]{1,0:T(1,128)S(1)}, s32[1,512]{1,0:T(1,128)}, u32[]{:S(2)}) copy-start(s32[1,512]{1,0:T(1,128)} %param.26) | copy-start | bytes 6148
  7.3 5.6 %copy-start.12 = (s32[1,512]{1,0:T(1,128)S(1)}, s32[1,512]{1,0:T(1,128)}, u32[]{:S(2)}) copy-start(s32[1,512]{1,0:T(1,128)} %param.27) | copy-start | bytes 6148
  7.3 5.6 %copy-start.10 = (bf16[1,2,1024]{2,1,0:T(2,128)(2,1)S(1)}, bf16[1,2,1024]{2,1,0:T(2,128)(2,1)}, u32[]{:S(2)}) copy-start(bf16[1,2,1024]{2,1,0:T(2,128)(2,1)} %param.25) | copy-start | bytes 12292
  7.3 5.6 %copy-start.1 = (bf16[32,6144]{1,0:T(8,128)(2,1)S(1)}, bf16[32,6144]{1,0:T(8,128)(2,1)}, u32[]{:S(2)}) copy-start(bf16[32,6144]{1,0:T(8,128)(2,1)} %refs_13_.1) | copy-start | bytes 1179652
  7.3 171.0 %all-gather.2.cloned.1.call-start = ((), (), s32[]{:S(2)}) async-start(), calls=%async_computation.2 | async-start | bytes 10813440 | tf_op jit(solution)/shard_map/all_gather | solution.py:802
  8.8 80.2 %copy-start.13 = (s32[1,512]{1,0:T(1,128)S(1)}, s32[1,512]{1,0:T(1,128)}, u32[]{:S(2)}) copy-start(s32[1,512]{1,0:T(1,128)} %param.28) | copy-start | bytes 6148
  84.8 2.6 copy-start
  87.4 0.6 copy-start.2
  103.0 40.8 %all-to-all-start = ((bf16[4,512,768]{2,1,0:T(8,128)(2,1)}), bf16[4,512,768]{2,1,0:T(8,128)(2,1)S(1)}, u32[]{:S(2)}, u32[]{:S(2)}) async-start(bf16[4,512,768]{2,1,0:T(8,128)(2,1)} %get-tuple-element.88), calls=%async_computation | async-start | bytes 6291456 | tf_op jit(solution)/shard_map/all_to_all | solution.py:815
  106.7 304.8 %reduce-scatter.2.cloned.1.call-start = ((), (), s32[]{:S(2)}) async-start(), calls=%async_computation.3 | async-start | bytes 6488064 | tf_op jit(solution)/shard_map/reduce_scatter | solution.py:822
  143.8 1.8 copy-start.3
  399.9 4.3 %copy-start.6 = (f32[32,3072]{1,0:T(8,128)S(1)}, f32[32,3072]{1,0:T(8,128)}, u32[]{:S(2)}) copy-start(f32[32,3072]{1,0:T(8,128)} %get-tuple-element.103) | copy-start | bytes 1179652
  401.3 6.4 %copy-start.7 = (f32[4,8,16,128]{3,2,1,0:T(8,128)S(1)}, f32[4,8,16,128]{3,2,1,0:T(8,128)}, u32[]{:S(2)}) copy-start(f32[4,8,16,128]{3,2,1,0:T(8,128)} %get-tuple-element.100) | copy-start | bytes 786436
  401.3 7.8 %copy-start.9 = (f32[8,768]{1,0:T(8,128)S(1)}, f32[8,768]{1,0:T(8,128)}, u32[]{:S(2)}) copy-start(f32[8,768]{1,0:T(8,128)} %get-tuple-element.102) | copy-start | bytes 73732
  404.5 12.8 %copy-start.4 = (f32[512,1024]{1,0:T(8,128)S(1)}, f32[512,1024]{1,0:T(8,128)}, u32[]{:S(2)}) copy-start(f32[512,1024]{1,0:T(8,128)} %get-tuple-element.99) | copy-start | bytes 6291460
  414.9 3.7 copy-start.5
Sparse Core Ops, SparseCore 0:
  12.3 112.7 all-gather.1
  215.8 128.6 reduce-scatter.1

commit v6 on v5

--- a/solution.py
+++ b/solution.py
@@ -92,7 +92,7 @@
             out_specs=[pl.BlockSpec((T,W),lambda i,*_:(i,0)),pl.BlockSpec((T,128),lambda i,*_:(i,0))],
             scratch_shapes=[pltpu.VMEM((nh,T,128),bf),pltpu.VMEM((nh,nk,T,T),f32),pltpu.VMEM((nh,T,128),f32),pltpu.VMEM((nh,T,256),f32)]),
         compiler_params=pltpu.CompilerParams(vmem_limit_bytes=60*2**20),
-        name="attn_fwd",
+        name="attn_fwd",cost_estimate=pl.CostEstimate(flops=16*nh*L*L*HD,bytes_accessed=4*2**20,transcendentals=nh*L*L),
     )(lo,hi,qkv,auxq,auxk)
 
 def bwd_kernel(lo_ref,hi_ref,qkv_ref,o_ref,do_ref,lse_ref,auxq_ref,auxk_ref,dqkv_ref,qs,qa,dos,dd,kT,dqT,dk,dv,*,T,nh):
@@ -166,7 +166,7 @@
             scratch_shapes=[pltpu.VMEM((nh,nk,T,128),bf)]*4+[pltpu.VMEM((nk,W,T),bf),pltpu.VMEM((nk,W,T),f32),
                 pltpu.VMEM((nh,T,128),f32),pltpu.VMEM((nh,T,128),f32)]),
         compiler_params=pltpu.CompilerParams(vmem_limit_bytes=60*2**20),
-        name="attn_bwd",
+        name="attn_bwd",cost_estimate=pl.CostEstimate(flops=40*nh*L*L*HD,bytes_accessed=8*2**20,transcendentals=nh*L*L),
     )(lo,hi,qkv,o,do,lse,auxq,auxk)
 
 def tables(seg,mask,T):
@@ -210,29 +210,33 @@
     h=0.5*(1.0+t)
     return v*h, h+0.5*v*(1.0-t*t)*(c*(1.0+3*0.044715*v2))
 
-def qkv_kernel(x_ref,seg_ref,emb_ref,w_ref,b_ref,cos_ref,sin_ref,n_ref,p_ref,*,R,nd,W):
+def qkv_kernel(x_ref,seg_ref,emb_ref,w_ref,b_ref,cos_ref,sin_ref,n_ref,*p_refs,R,nd):
     F,D=x_ref.shape
     @pl.loop(0,F//R)
     def _(i):
         r=pl.ds(pl.multiple_of(i*R,R),R)
         seg=seg_ref[r,:]
         n,_=moments(x_ref[r,:].astype(f32))
-        y=(n*(1.0+pick(seg,emb_ref,1,D))+pick(seg,emb_ref,0,D)).astype(bf)
-        n_ref[r,:]=y
-        cos=jnp.concatenate([cos_ref[r,:]]*(W//128),1); sin=jnp.concatenate([sin_ref[r,:]]*(W//128),1)
-        for d in range(nd):
-            for j in range(3):
-                c=(d*3+j)*W
-                v=dot(y,w_ref[:,c:c+W])+b_ref[0:1,c:c+W]
-                if j<2: v=v*cos+partner(v)*sin
-                p_ref[d,r,j*W:(j+1)*W]=v.astype(bf)
-
-def qkv_proj(x,seg,emb,w,b,cos,sin,nd,R=128):
-    F,D=x.shape; W=D//nd
-    return pl.pallas_call(functools.partial(qkv_kernel,R=R,nd=nd,W=W),
-        out_shape=(jax.ShapeDtypeStruct((F,D),bf),jax.ShapeDtypeStruct((nd,F,3*W),bf)),
-        in_specs=[V]*7,out_specs=(V,V),
-        compiler_params=pltpu.CompilerParams(vmem_limit_bytes=60*2**20),name="qkv_proj",
+        n_ref[r,:]=(n*(1.0+pick(seg,emb_ref,1,D))+pick(seg,emb_ref,0,D)).astype(bf)
+    for q,p_ref in enumerate(p_refs):
+        @pl.loop(0,F//R)
+        def _(i):
+            r=pl.ds(pl.multiple_of(i*R,R),R)
+            cos=cos_ref[r,:]; sin=sin_ref[r,:]
+            for d in range(0,nd,2):
+                c=(q*nd+d)*384
+                v=dot(n_ref[r,:],w_ref[:,c:c+768])+b_ref[0:1,c:c+768]
+                for k in range(6):
+                    a=v[:,k*128:(k+1)*128]
+                    if k%3<2: a=a*cos+partner(a)*sin
+                    p_ref[d+k//3,r,k%3*128:(k%3+1)*128]=a.astype(bf)
+
+def qkv_proj(x,seg,emb,w,b,cos,sin,nd,R=256):
+    F,D=x.shape; PP=D//nd//128
+    return pl.pallas_call(functools.partial(qkv_kernel,R=R,nd=nd),
+        out_shape=(jax.ShapeDtypeStruct((F,D),bf),)+(jax.ShapeDtypeStruct((nd,F,384),bf),)*PP,
+        in_specs=[V]*7,out_specs=(V,)*(1+PP),
+        compiler_params=pltpu.CompilerParams(vmem_limit_bytes=40*2**20),name="qkv_proj",
         cost_estimate=pl.CostEstimate(flops=2*F*D*3*D,bytes_accessed=14*2**20,transcendentals=0))(x,seg,emb,w,b,cos,sin)
 
 
@@ -264,16 +268,14 @@
     cp.start()
     return cp
 
-def greet_all(p):
+def greet(p):
     b=pltpu.get_barrier_semaphore()
-    @pl.loop(0,p.nd)
-    def _(dh):
-        @pl.loop(0,p.ns)
-        def _(ds):
-            @pl.when(dh+ds>0)
-            def _():
-                pl.semaphore_signal(b,inc=1,device_id=(lax.rem(p.h+dh,p.nd),lax.rem(p.s+ds,p.ns)),device_id_type=pl.DeviceIdType.MESH)
-    pl.semaphore_wait(b,p.nd*p.ns-1)
+    for d in range(1,p.nd): pl.semaphore_signal(b,inc=1,device_id=(lax.rem(p.h+d,p.nd),p.s),device_id_type=pl.DeviceIdType.MESH)
+    for d in range(1,p.ns): pl.semaphore_signal(b,inc=1,device_id=(p.h,lax.rem(p.s+d,p.ns)),device_id_type=pl.DeviceIdType.MESH)
+    pl.semaphore_wait(b,p.nd+p.ns-2)
+
+def along_head(p,f): return [f(d,lax.rem(p.h+d,p.nd),(lax.rem(p.h+d,p.nd),p.s)) for d in range(1,p.nd)]
+def along_seq(p,f): return [f(d,lax.rem(p.s+d,p.ns),(p.h,lax.rem(p.s+d,p.ns))) for d in range(1,p.ns)]
 
 class Gather:
     @staticmethod
@@ -356,7 +358,7 @@
     time_all,part,r1,r2,bs,br,isd,ir,ts,tr,e1s,e1r,e2s,e2r=refs[2*nw+8:2*nw+22]
     gs=refs[2*nw+22:]
     p=Place(nd,ns); n=len(Gather.sems(nd,ns))
-    greet_all(p)
+    greet(p)
     tail=[]
     first=[]
     for ds in range(1,ns):
@@ -366,14 +368,8 @@
     me=p.h*ns+p.s
     for dh in range(1,nd):
         tail.append(remote(ids,ids_all.at[p.h],isd.at[dh],ir.at[dh],(lax.rem(p.h+dh,nd),p.s)))
-    @pl.loop(0,nd)
-    def _(dh):
-        @pl.loop(0,ns)
-        def _(ds):
-            @pl.when(dh+ds>0)
-            def _():
-                remote(bias,bias_all.at[me],bs.at[dh,ds],br.at[dh,ds],(lax.rem(p.h+dh,nd),lax.rem(p.s+ds,ns)))
-    l1=pltpu.make_async_copy(bias,bias_all.at[me],bs.at[0,0]); l1.start()
+    bc=along_head(p,lambda d,h,dev: remote(bias,bias_all.at[p.h,p.s],bs.at[0,d],br.at[0,d],dev))
+    l1=pltpu.make_async_copy(bias,bias_all.at[p.h,p.s],bs.at[0,0]); l1.start()
     l2=pltpu.make_async_copy(ids,ids_all.at[p.h],isd.at[0]); l2.start()
     time_all[p.s]=time[...]
     for cp in first: cp.wait()
@@ -390,6 +386,9 @@
         for s in range(ns):
             part[s,2*j:2*j+2,:]=pj[8*s:8*s+2,:]
     one=[remote(part.at[lax.rem(p.s+ds,ns)],r1.at[ds],e1s.at[ds],e1r.at[ds],(p.h,lax.rem(p.s+ds,ns))) for ds in range(1,ns)]
+    l1.wait()
+    for cp in bc: cp.wait()
+    tail+=along_seq(p,lambda d,s,dev: remote(bias_all.at[:,p.s],bias_all.at[:,p.s],bs.at[1,d],br.at[1,d],dev))
     order=[0]+near_first(p.Z)
     for a in g:
         for i,dz in enumerate(order):
@@ -410,23 +409,16 @@
     emb[...]=tot
     for a in g: a.finish()
     for cp in tail: cp.wait()
-    l1.wait(); l2.wait()
-    @pl.loop(0,nd)
-    def _(dh):
-        @pl.loop(0,ns)
-        def _(ds):
-            @pl.when(dh+ds>0)
-            def _():
-                pltpu.make_async_remote_copy(src_ref=bias,dst_ref=bias_all.at[me],send_sem=bs.at[dh,ds],recv_sem=br.at[dh,ds],device_id=(lax.rem(p.h+dh,nd),lax.rem(p.s+ds,ns)),device_id_type=pl.DeviceIdType.MESH).wait()
+    l2.wait()
 
 def entry(nd,ns,shards,bias,time,ids,wada):
     X,Y,Z=sizes(nd,ns)
     S=jax.ShapeDtypeStruct
     D=pltpu.SemaphoreType.DMA
     nw=len(shards); E=wada.shape[1]//8
-    outs=[S((X,2,Z,Y)+a.shape,a.dtype) for a in shards]+[S((nd*ns,)+bias.shape,bias.dtype),S((nd,)+ids.shape,ids.dtype),S((16,E),f32),S((ns*8,128),bf)]
+    outs=[S((X,2,Z,Y)+a.shape,a.dtype) for a in shards]+[S((nd,ns)+bias.shape,bias.dtype),S((nd,)+ids.shape,ids.dtype),S((16,E),f32),S((ns*8,128),bf)]
     scr=[pltpu.VMEM((ns,8,time.shape[1]),f32),pltpu.VMEM((ns,16,E),f32),pltpu.VMEM((ns,16,E),f32),pltpu.VMEM((nd,16,E),f32),
-         D((nd,ns)),D((nd,ns)),D((nd,)),D((nd,)),D((ns,)),D((ns,)),D((ns,)),D((ns,)),D((nd,)),D((nd,))]
+         D((2,max(nd,ns))),D((2,max(nd,ns))),D((nd,)),D((nd,)),D((ns,)),D((ns,)),D((ns,)),D((ns,)),D((nd,)),D((nd,))]
     for _ in shards: scr+=Gather.sems(nd,ns)
     return pl.pallas_call(functools.partial(entry_kernel,nd,ns,nw),out_shape=tuple(outs),
         in_specs=[ANY]*(nw+1)+[V,ANY,V],out_specs=tuple([ANY]*(nw+2)+[V,V]),scratch_shapes=scr,
@@ -435,8 +427,11 @@
 def make_remote(src,dst,ss,rs,dev):
     return pltpu.make_async_remote_copy(src_ref=src,dst_ref=dst,send_sem=ss,recv_sem=rs,device_id=dev,device_id_type=pl.DeviceIdType.MESH)
 
-def mid_kernel(o_ref,x_ref,c_ref,seg_ref,msk_ref,emb_ref,w_ref,bo_ref,bu_ref,bd_ref,
-               out_ref,dm_ref,do_ref,gu_ref,gw_ref,gb_ref,ge_ref,
+def mid_kernel(PP,*refs,R,nd,ns):
+    mid_body(refs[:PP],refs[PP+9:2*PP+9],*refs[PP:PP+9],*refs[2*PP+9:],R=R,nd=nd,ns=ns)
+
+def mid_body(o_refs,do_refs,x_ref,c_ref,seg_ref,msk_ref,emb_ref,w_ref,bo_ref,bu_ref,bd_ref,
+               out_ref,dm_ref,gu_ref,gw_ref,gb_ref,ge_ref,
                wo_ref,wu_ref,wd_ref,n2s,acts,dhs,dfs,dps,dgelu,a_ref,da_ref,sem,s1,s2,s3,t1,t2,t3,*,R,nd,ns):
     F,D=x_ref.shape; H=bu_ref.shape[1]; CH=512
     loads=[pltpu.make_async_copy(w_ref.at[:,pl.ds(o,n)],r,sem.at[i]) for i,(o,n,r) in enumerate(((2*H,D,wo_ref),(0,H,wu_ref),(H,H,wd_ref)))]
@@ -445,14 +440,14 @@
     for d in range(1,nd): pl.semaphore_signal(b,inc=1,device_id=(lax.rem(p.h+d,nd),p.s),device_id_type=pl.DeviceIdType.MESH)
     pl.semaphore_wait(b,nd-1)
     def rows(i): return pl.ds(pl.multiple_of(i*R,R),R)
-    def cols(h): return pl.ds(pl.multiple_of(h*W,W),W)
+    def cols(h,q): return pl.ds(pl.multiple_of(h*W+q*128,128),128)
     def arrive(i):
-        return [make_remote(o_ref.at[lax.rem(p.h+d,nd),rows(i)],a_ref.at[rows(i),cols(p.h)],s1.at[i,d],s2.at[i,d],(lax.rem(p.h+d,nd),p.s)) for d in range(1,nd)]
-    def kept(i): return pltpu.make_async_copy(o_ref.at[p.h,rows(i)],a_ref.at[rows(i),cols(p.h)],s3.at[i])
+        return [make_remote(o.at[lax.rem(p.h+d,nd),rows(i)],a_ref.at[rows(i),cols(p.h,q)],s1.at[i,d,q],s2.at[i,d,q],(lax.rem(p.h+d,nd),p.s)) for d in range(1,nd) for q,o in enumerate(o_refs)]
+    def kept(i): return [pltpu.make_async_copy(o.at[p.h,rows(i)],a_ref.at[rows(i),cols(p.h,q)],s3.at[i,q]) for q,o in enumerate(o_refs)]
     def leave(i):
-        return [make_remote(da_ref.at[rows(i),cols(lax.rem(p.h+d,nd))],do_ref.at[p.h,rows(i)],t1.at[i,d],t2.at[i,d],(lax.rem(p.h+d,nd),p.s)) for d in range(1,nd)]
-    def stays(i): return pltpu.make_async_copy(da_ref.at[rows(i),cols(p.h)],do_ref.at[p.h,rows(i)],t3.at[i])
-    for c in arrive(0)+[kept(0)]: c.start()
+        return [make_remote(da_ref.at[rows(i),cols(lax.rem(p.h+d,nd),q)],o.at[p.h,rows(i)],t1.at[i,d,q],t2.at[i,d,q],(lax.rem(p.h+d,nd),p.s)) for q,o in enumerate(do_refs) for d in range(1,nd)]
+    def stays(i): return [pltpu.make_async_copy(da_ref.at[rows(i),cols(p.h,q)],o.at[p.h,rows(i)],t3.at[i,q]) for q,o in enumerate(do_refs)]
+    for c in arrive(0)+kept(0): c.start()
     for l in loads: l.start()
     gb_ref[...]=jnp.zeros_like(gb_ref); ge_ref[...]=jnp.zeros_like(ge_ref)
     for l in loads: l.wait()
@@ -463,10 +458,10 @@
     def _(i):
         r=rows(i)
         for c in arrive(i): c.wait_recv()
-        kept(i).wait()
+        for c in kept(i): c.wait()
         @pl.when(i+1<NR)
         def _():
-            for c in arrive(i+1)+[kept(i+1)]: c.start()
+            for c in arrive(i+1)+kept(i+1): c.start()
         seg=seg_ref[r,:]; msk=msk_ref[r,:]
         def acc(k,x):
             a,b=sums(x,seg)
@@ -509,7 +504,7 @@
         dps[r,:]=dp
         gb_ref[0:1,0:D]+=jnp.sum(dp.astype(f32),0,keepdims=True)
         da_ref[r,:]=dot(dp,wo_ref[...],NT).astype(bf)
-        for c in leave(i)+[stays(i)]: c.start()
+        for c in leave(i)+stays(i): c.start()
     @pl.loop(0,D//256)
     def _(i):
         c=pl.ds(pl.multiple_of(i*256,256),256)
@@ -520,17 +515,17 @@
             gw_ref[c,t*D:(t+1)*D]=dot(acts[:,e],dfs[...],TN).astype(bf)
     for i in range(NR):
         for c in arrive(i): c.wait_send()
-        for c in leave(i)+[stays(i)]: c.wait()
-
-def mid(nd,ns,o,x,c,seg,msk,emb,w,bo,bu,bd,R=256):
-    F,D=x.shape; H=bu.shape[1]; NR=F//R; A=pltpu.SemaphoreType.DMA
+        for c in leave(i)+stays(i): c.wait()
+
+def mid(nd,ns,os,x,c,seg,msk,emb,w,bo,bu,bd,R=256):
+    F,D=x.shape; H=bu.shape[1]; NR=F//R; PP=len(os); A=pltpu.SemaphoreType.DMA
     S=jax.ShapeDtypeStruct; M=pltpu.VMEM
-    return pl.pallas_call(functools.partial(mid_kernel,R=R,nd=nd,ns=ns),
-        out_shape=(S((F,D),bf),S((F,D),f32),S((nd,F,D//nd),bf),S((D,H),bf),S((D,H+D),bf),S((8,H),f32),S((8,4*D),f32)),
-        in_specs=[ANY]+[V]*5+[ANY]+[V]*3,out_specs=(V,V,ANY)+(V,)*4,
-        scratch_shapes=[M((D,D),bf),M((D,H),bf),M((D,H),bf),M((F,D),bf),M((F,H),bf),M((F,H),bf),M((F,D),bf),M((F,D),bf),M((R,H),f32),M((F,D),bf),M((F,D),bf),A((3,)),A((NR,nd)),A((NR,nd)),A((NR,)),A((NR,nd)),A((NR,nd)),A((NR,))],
+    return pl.pallas_call(functools.partial(mid_kernel,PP,R=R,nd=nd,ns=ns),
+        out_shape=(S((nd,F,128),bf),)*PP+(S((F,D),bf),S((F,D),f32),S((D,H),bf),S((D,H+D),bf),S((8,H),f32),S((8,4*D),f32)),
+        in_specs=[ANY]*PP+[V]*5+[ANY]+[V]*3,out_specs=(ANY,)*PP+(V,)*6,
+        scratch_shapes=[M((D,D),bf),M((D,H),bf),M((D,H),bf),M((F,D),bf),M((F,H),bf),M((F,H),bf),M((F,D),bf),M((F,D),bf),M((R,H),f32),M((F,D),bf),M((F,D),bf),A((3,)),A((NR,nd,PP)),A((NR,nd,PP)),A((NR,PP)),A((NR,nd,PP)),A((NR,nd,PP)),A((NR,PP))],
         compiler_params=pltpu.CompilerParams(collective_id=2,has_side_effects=True,vmem_limit_bytes=62*2**20),name="mid",
-        cost_estimate=pl.CostEstimate(flops=6*F*D*(D+2*H),bytes_accessed=30*2**20,transcendentals=F*H))(o,x,c,seg,msk,emb,w,bo,bu,bd)
+        cost_estimate=pl.CostEstimate(flops=6*F*D*(D+2*H),bytes_accessed=30*2**20,transcendentals=F*H))(*os,x,c,seg,msk,emb,w,bo,bu,bd)
 
 
 ORD_X=-1
@@ -620,35 +615,28 @@
     def finish(self):
         for c in self.sent: c.wait_send()
 
-def greet(p):
-    b=pltpu.get_barrier_semaphore()
-    for d in range(1,p.nd): pl.semaphore_signal(b,inc=1,device_id=(lax.rem(p.h+d,p.nd),p.s),device_id_type=pl.DeviceIdType.MESH)
-    for d in range(1,p.ns): pl.semaphore_signal(b,inc=1,device_id=(p.h,lax.rem(p.s+d,p.ns)),device_id_type=pl.DeviceIdType.MESH)
-    pl.semaphore_wait(b,p.nd+p.ns-2)
-
-def along_head(p,f): return [f(d,lax.rem(p.h+d,p.nd),(lax.rem(p.h+d,p.nd),p.s)) for d in range(1,p.nd)]
-def along_seq(p,f): return [f(d,lax.rem(p.s+d,p.ns),(p.h,lax.rem(p.s+d,p.ns))) for d in range(1,p.ns)]
-
 REST=(lambda w,j:((0,w,"xyz"),) if j==ORD_X else ((0,w,"yzx"),)); QKV=(lambda w:((0,w//2,"yxz"),(w//2,w,"xyz")))
 
-def final_kernel(nd,ns,R,refs,scr):
+def final_kernel(nd,ns,R,here,refs,scr):
     (g_ref,rest_ref,x_hbm,n1_hbm,dm_hbm,wq_hbm,cos_ref,sin_ref,seg_ref,emb_ref,gbm_ref,gem_ref,act,wada)=refs[:14]
     (gf_ref,rest_out,qkv_out,bias_all,gada,gbada,dact)=refs[14:]
     (g,x_ref,n1_ref,dm_ref,w_ref,dps,gw,gbv,gev,bsc,bout,hsum,demb,dscr)=scr[:14]
-    (gs,gr,gl,ld,hs,hr,qs,qr,ds_,dr,bs,br)=scr[14:26]
-    pools=scr[26:]
+    (gs,gr,gl,gh,ld,hs,hr,qs,qr,ds_,dr,bs,br)=scr[14:27]
+    pools=scr[27:]
     p=Place(nd,ns); me=p.h*ns+p.s
     F,D=x_ref.shape; W=D//nd; E=D*6//8; K=wada.shape[0]; H=gbm_ref.shape[1]; NR=F//R
-    nr=H//D; nq=3*D//QW
+    nr=H//D; nq=3*D//QW; PP=W//128; C=3*D//PP; ne=nq//PP*(PP-1)
+    come=[pltpu.make_async_copy(a,g.at[q],gh.at[q]) for q,a in enumerate(here)]
+    for c in come: c.start()
     greet(p)
     loads=[pltpu.make_async_copy(a,b,ld.at[i]) for i,(a,b) in enumerate(((x_hbm,x_ref),(wq_hbm,w_ref),(dm_hbm,dm_ref),(n1_hbm,n1_ref)))]
     sends=[]; own=[]
     def chunk(i):
         r=pl.ds(i*R,R)
-        sends.append([remote(g_ref.at[lax.rem(p.h+d,nd),r],g.at[p.h,r],gs.at[i,d],gr.at[i,d],(lax.rem(p.h+d,nd),p.s)) for d in range(1,nd)])
+        sends.append([remote(g_ref.at[lax.rem(p.h+d,nd),r],g.at[PP-1,p.h,r],gs.at[i,d],gr.at[i,d],(lax.rem(p.h+d,nd),p.s)) for d in range(1,nd)])
     for i in range(NR):
         r=pl.ds(i*R,R)
-        c=pltpu.make_async_copy(g_ref.at[p.h,r],g.at[p.h,r],gl.at[i]); c.start(); own.append(c)
+        c=pltpu.make_async_copy(g_ref.at[p.h,r],g.at[PP-1,p.h,r],gl.at[i]); c.start(); own.append(c)
     for i in range(min(2,NR)): chunk(i)
     for l in loads: l.start()
     it=iter(pools)
@@ -662,22 +650,24 @@
     gbv[...]=jnp.zeros_like(gbv); gev[...]=jnp.zeros_like(gev); bsc[...]=jnp.zeros_like(bsc)
     for a in rest[:2]: a.step()
     for l in loads: l.wait()
+    def unturn(q,r):
+        cos=cos_ref[r,:]; sin=sin_ref[r,:]
+        @pl.loop(0,nd)
+        def _(d):
+            for j in range(3):
+                c=pl.ds(pl.multiple_of(((q*nd+d)*3+j)*128,128),128)
+                v=g[q,d,r,j*128:(j+1)*128]
+                if j<2:
+                    v=v.astype(f32)
+                    v=(v*cos-partner(v)*sin).astype(bf)
+                dps[r,c]=v
+                gbv[0:1,c]+=jnp.sum(v.astype(f32),0,keepdims=True)
     def turn(i):
         for c in sends[i]: c.wait_recv()
         own[i].wait()
         if i+2<NR: chunk(i+2)
         r=slice(i*R,(i+1)*R)
-        cos=jnp.concatenate([cos_ref[r,:]]*(W//128),1); sin=jnp.concatenate([sin_ref[r,:]]*(W//128),1)
-        @pl.loop(0,nd)
-        def _(d):
-            for j in range(3):
-                c=pl.ds(pl.multiple_of((d*3+j)*W,W),W)
-                v=g[d,r,j*W:(j+1)*W]
-                if j<2:
-                    v=v.astype(f32)
-                    v=(v*cos-partner(v)*sin).astype(bf)
-                dps[r,c]=v
-                gbv[0:1,c]+=jnp.sum(v.astype(f32),0,keepdims=True)
+        unturn(PP-1,r)
     def norm(lo,hi):
         @pl.loop(lo,hi)
         def _(i):
@@ -698,42 +688,53 @@
             v=dot(n1_ref[:,h*B:(h+1)*B],dps[:,j*QW:(j+1)*QW],TN).astype(bf)
             gw[j,h//2,h%2]=v.reshape(p.Z,p.Y,K,QW)
         qkv[j].start()
-    steps=[a.step for _ in range(2) for a in rest]
+    for q,c in enumerate(come):
+        c.wait()
+        @pl.loop(0,NR)
+        def _(i,q=q): unturn(q,pl.ds(pl.multiple_of(i*R,R),R))
+    for j in range(ne):
+        weight(j)
+        if j: qkv[j-1].step()
+    for a in qkv[:ne][-1:]: a.step()
+    steps=[]
+    for k in range(max(ne,nr)): steps+=[a.step for a in qkv[:ne][k:k+1]]+[a.step for a in rest[k:k+1]]
     for i in range(NR):
         turn(i)
-        if i:
-            for f in steps[(i-1)*len(steps)//(NR-1):i*len(steps)//(NR-1)]: f()
-    for j in range(nq):
+        for f in steps[i*len(steps)//NR:(i+1)*len(steps)//NR]: f()
+    for j in range(ne,nq):
         weight(j)
-        if j: qkv[j-1].step()
+        if j>ne: qkv[j-1].step()
+        if j-ne<nr: rest[j-ne].step()
     vec=jnp.concatenate([gbv[0:1,:],gbm_ref[0:1,0:D],gbm_ref[1:2,:],gbm_ref[2:3,0:D]],1)
     for q in range(vec.shape[1]//256):
         h,s=divmod(q,ns)
         bsc[h//2,h%2,s//p.Y,s%p.Y,0:1,:]=vec[:,q*256:(q+1)*256]
     bias.start()
     qkv[nq-1].step()
+    for a in qkv[:ne]: a.step()
     norm(0,NR//2)
     bias.step()
-    qkv[0].step()
-    qkv[1].step()
+    qkv[ne].step()
     norm(NR//2,NR)
     gev[0:2,2*D:]=gem_ref[0:2,:]
     for j in range(8):
         for t in range(2): hsum[p.h,2*j+t:2*j+t+1,:]=gev[t:t+1,j*E:(j+1)*E]
     hc=[remote(hsum.at[p.h],hsum.at[p.h],hs.at[d],hr.at[d],(lax.rem(p.h+d,nd),p.s)) for d in range(1,nd)]
-    qkv[0].step(); qkv[2].step(); qkv[1].step(); bias.step()
+    qkv[ne+1].step(); qkv[ne].step(); bias.step()
     for c in hc: c.wait()
     tot=hsum[0]
     for i in range(1,nd): tot=tot+hsum[i]
     demb[p.s]=tot.astype(bf)
     qc=[remote(demb.at[p.s],demb.at[p.s],qs.at[d],qr.at[d],(p.h,lax.rem(p.s+d,ns))) for d in range(1,ns)]
-    qkv[3].step(); qkv[2].step(); bias.step()
+    qkv[ne+2].step(); qkv[ne+1].step(); bias.step()
+    for j in range(ne+3,nq): qkv[j].step(); qkv[j-1].step()
     for j,a in enumerate(rest): a.last(rest_out,j*D)
     bias.last(bout)
     bias_all[p.h,p.s]=bout[...]
     bc=along_head(p,lambda d,h,dev: remote(bout,bias_all.at[p.h,p.s],bs.at[0,d],br.at[0,d],dev))
-    qkv[4].step(); qkv[3].step()
+    for j in range(ne): qkv[j].last(qkv_out,j*QW)
     for c in qc: c.wait()
+    qkv[nq-1].step()
     Q=ns*16
     flat=demb[...].reshape(Q,E)
     r0=lax.broadcasted_iota(jnp.int32,(Q,ns*8),0); c0=lax.broadcasted_iota(jnp.int32,(Q,ns*8),1)
@@ -752,32 +753,30 @@
     bc=along_seq(p,lambda d,s,dev: remote(bias_all.at[:,p.s],bias_all.at[:,p.s],bs.at[1,d],br.at[1,d],dev))
     r8=lax.broadcasted_iota(jnp.int32,(8,Q),0); c8=lax.broadcasted_iota(jnp.int32,(8,Q),1)
     gbada[...]=dot(jnp.where(c8%16//2==r8,1.0,0.0).astype(bf),flat)
-    qkv[5].step(); qkv[4].step()
     for c in dc: c.wait()
     dc=along_head(p,lambda d,h,dev: remote(dact.at[p.h],dact.at[p.h],ds_.at[1,d],dr.at[1,d],dev))
-    for j in range(nq-1): qkv[j].last(qkv_out,j*QW)
-    qkv[5].step()
-    qkv[nq-1].last(qkv_out,(nq-1)*QW)
+    for j in range(ne,nq): qkv[j].last(qkv_out,j*QW)
     for a in rest+qkv+[bias]: a.finish()
     for i in range(NR):
         for c in sends[i]: c.wait_send()
     for c in bc+dc: c.wait()
 
-def final(nd,ns,dqkv,rest,x,n1,dm,wq,cos,sin,seg,emb,gb,ge,act,wada,R=128):
+def final(nd,ns,here,dqkv,rest,x,n1,dm,wq,cos,sin,seg,emb,gb,ge,act,wada,R=128):
     F,D=x.shape; K,E6=wada.shape; E=E6//8; H=gb.shape[1]; N=nd*ns; W=D//nd; NR=F//R
     X,Y,Z=sizes(nd,ns)
     S=jax.ShapeDtypeStruct; M=pltpu.VMEM; A=pltpu.SemaphoreType.DMA
     outs=[S((F,D),f32),S((K,H),f32),S((K,3*D),f32),S((nd,ns,8,256),f32),S((K,E6),f32),S((8,E),f32),S((nd,ns,16,128),f32)]
-    scr=[M((nd,F,3*W),bf),M((F,D),bf),M((F,D),bf),M((F,D),f32),M((D,3*D),bf),M((F,3*D),bf),M((3*D//QW,X,2,Z,Y,K,QW),bf),M((8,3*D),f32),M((8,E6),f32),
+    scr=[M((W//128,nd,F,384),bf),M((F,D),bf),M((F,D),bf),M((F,D),f32),M((D,3*D),bf),M((F,3*D),bf),M((3*D//QW,X,2,Z,Y,K,QW),bf),M((8,3*D),f32),M((8,E6),f32),
          M((X,2,Z,Y,8,256),f32),M((8,256),f32),M((nd,16,E),f32),M((ns,16,E),bf),M((ns,16,128),f32),
-         A((NR,nd)),A((NR,nd)),A((NR,)),A((4,)),A((nd,)),A((nd,)),A((ns,)),A((ns,)),A((2,max(nd,ns))),A((2,max(nd,ns))),A((2,max(nd,ns))),A((2,max(nd,ns)))]
+         A((NR,nd)),A((NR,nd)),A((NR,)),A((W//128,)),A((4,)),A((nd,)),A((nd,)),A((ns,)),A((ns,)),A((2,max(nd,ns))),A((2,max(nd,ns))),A((2,max(nd,ns))),A((2,max(nd,ns)))]
     for j in range(H//D): scr+=Reduce.scratch(nd,ns,K,D,bf,REST(D,j),False)
     for _ in range(3*D//QW): scr+=Reduce.scratch(nd,ns,K,QW,bf,QKV(QW),True)
     scr+=Reduce.scratch(nd,ns,8,256,f32,QKV(256),True)
-    def k(*refs): final_kernel(nd,ns,R,refs[:14+len(outs)],refs[14+len(outs):])
-    return pl.pallas_call(k,out_shape=tuple(outs),in_specs=[ANY]*6+[V]*8,out_specs=(V,)*len(outs),scratch_shapes=scr,
+    m=len(here)
+    def k(*refs): final_kernel(nd,ns,R,refs[:m],refs[m:m+14+len(outs)],refs[m+14+len(outs):])
+    return pl.pallas_call(k,out_shape=tuple(outs),in_specs=[ANY]*(6+m)+[V]*8,out_specs=(V,)*len(outs),scratch_shapes=scr,
         compiler_params=pltpu.CompilerParams(collective_id=1,has_side_effects=True,vmem_limit_bytes=63*2**20),name="final")(
-        dqkv,rest,x,n1,dm,wq,cos,sin,seg,emb,gb,ge,act,wada)
+        *here,dqkv,rest,x,n1,dm,wq,cos,sin,seg,emb,gb,ge,act,wada)
 
 
 def body(frames,time_embed,segment_ids,frame_mask,positions,w_ada,b_ada,w_qkv,b_qkv,w_out,b_out,w_up,b_up,w_down,b_down,cotangent):
@@ -787,8 +786,9 @@
     W=D//nd
     E=b_ada.shape[0]; E6=w_ada.shape[1]; K=w_ada.shape[0]; H=w_up.shape[1]; nt=H//D
     x=frames[0]; cot=cotangent[0]
-    def reorder(w): return w.reshape(-1,3,nd,W).transpose(0,2,1,3).reshape(-1,3*D)
-    def restore(w): return w.reshape(-1,nd,3,W).transpose(0,2,1,3).reshape(-1,3*D)
+    PP=W//128
+    def reorder(w): return w.reshape(-1,3,nd,PP,128).transpose(0,3,2,1,4).reshape(-1,3*D)
+    def restore(w): return w.reshape(-1,PP,nd,3,128).transpose(0,3,2,1,4).reshape(-1,3*D)
     def hide(w): return w.reshape(-1,N,nt,K).transpose(0,2,1,3).reshape(-1,H)
     def unhide(w): return w.reshape(-1,nt,N,K).transpose(0,2,1,3).reshape(-1,H)
     rest=jnp.concatenate([hide(w_up),w_down.reshape(nt,K,D).transpose(1,0,2).reshape(K,H),w_out],axis=1)
@@ -801,7 +801,7 @@
     wq,bias_all,ids_all,emb,act=entry(nd,ns,[reorder(w_qkv)],bias,time8,ids,w_ada)
     rest_all=lax.all_gather(rest,HS,axis=0,tiled=True)
     wq=wq.reshape(D,3*D)
-    bias_all=bias_all[:,0,:].astype(f32)
+    bias_all=bias_all[:,:,0,:].reshape(N,-1).astype(f32)
     bq,bo,bu,bd,ba=[bias_all[:,ends[i]:ends[i+1]].reshape(1,-1) for i in range(5)]
     bq=reorder(bq); bu=hide(bu)
     emb=emb.reshape(8,2,-1).transpose(1,0,2).reshape(2,E6)+ba
@@ -811,17 +811,22 @@
     angles=positions[0].astype(f32)[:,None]*(10000.0**(-(2.0*pair)/HD))
     cos=jnp.cos(angles); sin=jnp.where(column%2==0,-jnp.sin(angles),jnp.sin(angles))
     segc=segment_ids[0][:,None]; mskc=frame_mask[0].astype(f32)[:,None]
-    normed,packed=qkv_proj(x,segc,emb,wq,bq,cos,sin,nd)
-    qkv=lax.all_to_all(packed,"head",split_axis=0,concat_axis=0,tiled=True).reshape(nd*F,3*W)
+    normed,*packed=qkv_proj(x,segc,emb,wq,bq,cos,sin,nd)
+    def swap(a): return lax.all_to_all(a,"head",split_axis=0,concat_axis=0,tiled=True)
+    qkv=[]
+    for a in packed:
+        if qkv: a,qkv[-1]=lax.optimization_barrier((a,qkv[-1]))
+        qkv.append(swap(a))
+    qkv=[a.reshape(nd*F,384) for a in qkv]
     T=512
     qlo,qhi,klo,khi=tables(seg_row,msk_row,T)
     aq,ak=aux(seg_row,msk_row)
-    o,lse=attn_fwd(qkv,qlo,qhi,aq,ak,T)
-    out,dmid,do,gup,gdo,gb,ge=mid(nd,ns,o.reshape(nd,F,W),x,cot,segc,mskc,emb,rest_all,bo,bu,bd)
-    do=do.reshape(nd*F,W)
+    os=[attn_fwd(a,qlo,qhi,aq,ak,T) for a in qkv]
+    *dos,out,dmid,gup,gdo,gb,ge=mid(nd,ns,[o.reshape(nd,F,128) for o,_ in os],x,cot,segc,mskc,emb,rest_all,bo,bu,bd)
     gdo=lax.psum_scatter(gdo,HS,scatter_dimension=0,tiled=True).astype(f32)
-    dqkv=attn_bwd(qkv,o,do,lse,klo,khi,aq,ak,T)
-    gx,gup,gqkv,gbias,gada,gbada,dact=final(nd,ns,dqkv.reshape(nd,F,3*W),gup.reshape(X,2,Z,Y,K,H),x,normed,dmid,wq,cos,sin,segc,emb,gb,ge,act,w_ada)
+    dqkv=[attn_bwd(a,o,do.reshape(nd*F,128),lse,klo,khi,aq,ak,T).reshape(nd,F,384) for a,(o,lse),do in zip(qkv,os,dos)]
+    gx,gup,gqkv,gbias,gada,gbada,dact=final(nd,ns,[swap(a) for a in dqkv[:-1]],dqkv[-1],gup.reshape(X,2,Z,Y,K,H),x,normed,dmid,
+        wq,cos,sin,segc,emb,gb,ge,act,w_ada)
     dact=dact[:,:,:,:K].reshape(N,8,2,K).sum(1).transpose(1,0,2).reshape(2,D)
     _,pull=jax.vjp(jax.nn.silu,time_embed[0].astype(f32))
     gtime=pull(dact)[0][None]

time: 429 us -> 431 us (level); the launches traced: 426 us -> 424 us
  waiting for transfers between devices: 29.5 us -> 17.7 us
  starting transfers between devices: 3.78 us -> 12.8 us
    all_to_all x1 -> x3, waiting for transfers between devices: 29.4 us -> 17.6 us  [swap(): return lax.all_to_all(a, 'head', split_axis=0, concat_axis=0, tiled=True)]
    pallas_call x3, Pallas kernels: 172 us -> 162 us  [the longest x1 115 us: final(): pl.pallas_call(k, out_shape=tuple(outs), in_specs=[ANY] * (6 + m) + [V] *...]
    all_to_all x1 -> x3, starting transfers between devices: 3.7 us -> 12.3 us  [swap(): return lax.all_to_all(a, 'head', split_axis=0, concat_axis=0, tiled=True)]
    pallas_call x1 -> x2, Pallas kernels: 32.7 us -> 40.9 us  [attn_fwd(): pl.pallas_call(functools.partial(fwd_kernel, T=T, nh=nh), out_shape=(jax....]
    pallas_call x1 -> x2, Pallas kernels: 59.5 us -> 64.7 us  [attn_bwd(): pl.pallas_call(functools.partial(bwd_kernel, T=T, nh=nh), out_shape=jax.S...]
    unnamed x45 -> x64, local copies, waits for them, and re-layouts: 9.61 us -> 12.1 us
  transfers between devices with their start and end apart: 3 -> 5, of which waited for: 1 -> 1; matrix products, arithmetic and copies ran while one was open for 6% -> 5% of each run, Pallas kernels for 70% -> 70%
where the time goes in v6:
time: 431 us; the launch traced here: 424 us
  Pallas kernels  336 us (78%)
  local copies, waits for them, and re-layouts  34.3 us (8%)
  waiting for transfers between devices  17.7 us (4%)
  between operations  14.9 us (3%)
  starting transfers between devices  12.8 us (3%)
  other arithmetic  7.53 us (2%)
    pallas_call x1, Pallas kernels, final(): pl.pallas_call(k, out_shape=tuple(outs), in_specs=[ANY] * (6 + m) + [V] *...  115 us
    pallas_call x1, Pallas kernels, entry(): pl.pallas_call(functools.partial(entry_kernel, nd, ns, nw), out_shape=tup...  68.6 us
    pallas_call x2, Pallas kernels, attn_bwd(): pl.pallas_call(functools.partial(bwd_kernel, T=T, nh=nh), out_shape=jax.S...  64.7 us
    pallas_call x2, Pallas kernels, attn_fwd(): pl.pallas_call(functools.partial(fwd_kernel, T=T, nh=nh), out_shape=(jax....  40.9 us
    pallas_call x1, Pallas kernels, mid(): pl.pallas_call(functools.partial(mid_kernel, PP, R=R, nd=nd, ns=ns), out_...  39.7 us
    all_to_all x3, waiting for transfers between devices, swap(): return lax.all_to_all(a, 'head', split_axis=0, concat_axis=0, tiled=True)  17.6 us
    all_to_all x3, starting transfers between devices, swap(): return lax.all_to_all(a, 'head', split_axis=0, concat_axis=0, tiled=True)  12.3 us
    unnamed x64, local copies, waits for them, and re-layouts  12.1 us
  transfers between devices with their start and end apart: 5, of which 1 were waited for; matrix products, arithmetic and copies ran while one was open for 5% of the time, Pallas kernels for 70%

profile of v6, /device:TPU:0, one launch (start us, length us, event | category | flops | bytes accessed | tf_op | source)
XLA Modules:
  0.0 423.5 jit_solution(4686305276146214971)
XLA Ops:
  7.3 1.4 reshape.361
  11.1 68.6 %entry.1 = (bf16[2,2,4,2,32,3072]{5,4,3,2,1,0:T(8,128)(2,1)S(1)}, bf16[4,8,16,512]{3,2,1,0:T(8,128)(2,1)S(1)}, s32[4,8,512]{2,1,0:T(8,128)S(1)}, f32[16,768]{1,0:T(8,128)S(1)}, bf16[64,128]{1,0:T(8,128)(2,1)S(1)}) custom-call(bf16[32,3072]{1,0:T(8,128)(2,1)S(1)} %reshape.351.refs_0_, bf16[16,512]{1,0:T(8,128)(2,1)S(1)} %scatter.16.refs_1_, ...), custom_call_target="tpu_custom_call" | custom-call | tf_op jit(solution)/shard_map/entry/pallas_call | solution.py:423
  79.8 2.6 copy-done
  83.6 1.0 negate_select_fusion
  84.7 4.2 %copy-done.1 = bf16[2,2,4,2,32,3072]{5,4,3,2,1,0:T(8,128)(2,1)S(1)} copy-done((bf16[2,2,4,2,32,3072]{5,4,3,2,1,0:T(8,128)(2,1)S(1)}, bf16[2,2,4,2,32,3072]{5,4,3,2,1,0:T(8,128)(2,1)}, u32[]{:S(2)}) %copy-start.1) | copy-done | bytes 6291480
  88.9 7.2 %qkv_proj.1 = (bf16[512,1024]{1,0:T(8,128)(2,1)S(1)}, bf16[4,512,384]{2,1,0:T(8,128)(2,1)}, bf16[4,512,384]{2,1,0:T(8,128)(2,1)}) custom-call(bf16[512,1024]{1,0:T(8,128)(2,1)S(1)} %bitcast.71, s32[512,1]{1,0:T(8,128)S(1)} %copy.110.seg_ref.refs_4_.refs_9_, f32[2,6144]{1,0:T(2,128)S(1)} %broadcast_add_fusion.emb_ref.refs_6_.refs_10_, ...), custom_call_target="tpu_custom_call" | custom-call | flops 3221225472 | bytes 14680064 | tf_op jit(solution)/shard_map/qkv_proj/pallas_call | solution.py:236
  96.2 1.0 copy-done.7
  97.2 3.6 all-to-all-start
  103.0 0.9 copy.115.refs_5_
  105.5 17.6 %all-to-all-done = bf16[4,512,384]{2,1,0:T(8,128)(2,1)S(1)} async-done(((bf16[4,512,384]{2,1,0:T(8,128)(2,1)}), bf16[4,512,384]{2,1,0:T(8,128)(2,1)S(1)}, u32[]{:S(2)}, u32[]{:S(2)}) %all-to-all-start) | async-done | bytes 1572896 | tf_op jit(solution)/shard_map/all_to_all | solution.py:815
  123.2 4.4 %all-to-all-start.1 = ((bf16[4,512,384]{2,1,0:T(8,128)(2,1)}), bf16[4,512,384]{2,1,0:T(8,128)(2,1)}, u32[]{:S(2)}, u32[]{:S(2)}) async-start(bf16[4,512,384]{2,1,0:T(8,128)(2,1)} %get-tuple-element.98), calls=%async_computation.1 | async-start | bytes 3145728 | tf_op jit(solution)/shard_map/all_to_all | solution.py:815
  128.1 2.7 select_convert_fusion
  130.8 20.5 %attn_fwd.2 = (bf16[2048,128]{1,0:T(8,128)(2,1)}, f32[2048,128]{1,0:T(8,128)}) custom-call(s32[4]{0:T(128)} %get-tuple-element.126.lo_ref, s32[4]{0:T(128)} %broadcast_add_fusion.2.hi_ref, bf16[2048,384]{1,0:T(8,128)(2,1)} %bitcast.78, bf16[2048,128]{1,0:T(8,128)(2,1)} %get-tuple-element.143.auxq_ref, bf16[2048,128]{1,0:T(8,128)(2,1)} %get-tuple-element.142.auxk_ref), custom_call_target="tpu_custom_call" | custom-call | flops 8589934592 | bytes 4194304 | tf_op jit(solution)/shard_map/attn_fwd/pallas_call | solution.py:87
  151.3 20.4 %attn_fwd.3 = (bf16[2048,128]{1,0:T(8,128)(2,1)}, f32[2048,128]{1,0:T(8,128)}) custom-call(s32[4]{0:T(128)} %get-tuple-element.126.lo_ref, s32[4]{0:T(128)} %broadcast_add_fusion.2.hi_ref, bf16[2048,384]{1,0:T(8,128)(2,1)} %bitcast.19.qkv_ref, bf16[2048,128]{1,0:T(8,128)(2,1)} %get-tuple-element.143.auxq_ref, bf16[2048,128]{1,0:T(8,128)(2,1)} %get-tuple-element.142.auxk_ref), custom_call_target="tpu_custom_call" | custom-call | flops 8589934592 | bytes 4194304 | tf_op jit(solution)/shard_map/attn_fwd/pallas_call | solution.py:87
  171.7 39.7 %mid.1 = (bf16[4,512,128]{2,1,0:T(8,128)(2,1)}, bf16[4,512,128]{2,1,0:T(8,128)(2,1)}, bf16[512,1024]{1,0:T(8,128)(2,1)}, f32[512,1024]{1,0:T(8,128)}, bf16[1024,...) custom-call(bf16[4,512,128]{2,1,0:T(8,128)(2,1)} %bitcast.117, ...), custom_call_target="tpu_custom_call" | custom-call | flops 16106127360 | bytes 31457280 | tf_op jit(solution)/shard_map/mid/pallas_call | solution.py:523
  212.0 32.3 %attn_bwd.2 = bf16[2048,384]{1,0:T(8,128)(2,1)} custom-call(s32[4]{0:T(128)} %get-tuple-element.125.lo_ref, s32[4]{0:T(128)} %broadcast_add_fusion.1.hi_ref, bf16[2048,384]{1,0:T(8,128)(2,1)} %bitcast.79, bf16[2048,128]{1,0:T(8,128)(2,1)} %get-tuple-element.97.o_ref, bf16[2048,128]{1,0:T(8,128)(2,1)} %bitcast.119, f32[2048,128]{1,0:T(8,128)} %get-tuple-element.102.lse_ref, ...), custom_call_target="tpu_custom_call" | custom-call | flops 21474836480 | bytes 8388608 | tf_op jit(solution)/shard_map/attn_bwd/pallas_call | solution.py:160
  244.3 4.3 %all-to-all-start.2 = ((bf16[4,512,384]{2,1,0:T(8,128)(2,1)}), bf16[4,512,384]{2,1,0:T(8,128)(2,1)}, u32[]{:S(2)}, u32[]{:S(2)}) async-start(bf16[4,512,384]{2,1,0:T(8,128)(2,1)} %bitcast.80), calls=%async_computation.2 | async-start | bytes 3145728 | tf_op jit(solution)/shard_map/all_to_all | solution.py:815
  248.7 32.4 %attn_bwd.3 = bf16[2048,384]{1,0:T(8,128)(2,1)} custom-call(s32[4]{0:T(128)} %get-tuple-element.125.lo_ref, s32[4]{0:T(128)} %broadcast_add_fusion.1.hi_ref, bf16[2048,384]{1,0:T(8,128)(2,1)} %bitcast.19.qkv_ref, bf16[2048,128]{1,0:T(8,128)(2,1)} %get-tuple-element.99.o_ref, bf16[2048,128]{1,0:T(8,128)(2,1)} %bitcast.118, ...), custom_call_target="tpu_custom_call" | custom-call | flops 21474836480 | bytes 8388608 | tf_op jit(solution)/shard_map/attn_bwd/pallas_call | solution.py:160
  281.1 115.0 %final.1 = (f32[512,1024]{1,0:T(8,128)}, f32[32,2048]{1,0:T(8,128)}, f32[32,3072]{1,0:T(8,128)}, f32[4,8,8,256]{3,2,1,0:T(8,128)}, f32[32,6144]{1,0:T(8,128)}, /...) custom-call(bf16[4,512,384]{2,1,0:T(8,128)(2,1)} %all-to-all-done.2.refs_0_, bf16[4,512,384]{2,1,0:T(8,128)(2,1)} %bitcast.77, ...), custom_call_target="tpu_custom_call" | custom-call | tf_op jit(solution)/shard_map/final/pallas_call | solution.py:777
  396.1 1.3 reshape.378
  397.4 0.8 copy.120
  398.3 2.1 reshape.379
  400.8 1.1 reshape.377
  401.9 1.0 slice.120
  402.9 0.9 slice_reduce_fusion
  407.8 1.6 slice.135
  409.5 1.2 reshape.380
  410.6 0.8 copy.122
  411.4 1.5 slice.133
  412.9 1.0 copy.142
  413.9 1.3 copy.143
  415.6 0.9 copy.144
  (130 shorter events, 13.3 us)
Async XLA Ops:
  7.2 2.3 copy-start.17
  7.2 2.4 copy-start.18
  7.2 3.2 copy-start.16
  7.2 164.5 %all-gather.2.cloned.1.call-start = ((), (), s32[]{:S(2)}) async-start(), calls=%async_computation.4 | async-start | bytes 10813440 | tf_op jit(solution)/shard_map/all_gather | solution.py:802
  8.7 2.2 copy-start.24
  8.7 2.2 copy-start.25
  8.7 2.2 copy-start.26
  8.7 2.2 copy-start.27
  8.7 2.2 copy-start.28
  8.7 2.3 copy-start.21
  8.7 2.3 copy-start.22
  8.7 2.3 copy-start.20
  8.8 2.4 copy-start.2
  9.6 73.8 %copy-start.23 = (s32[1,512]{1,0:T(1,128)S(1)}, s32[1,512]{1,0:T(1,128)}, u32[]{:S(2)}) copy-start(s32[1,512]{1,0:T(1,128)} %param.28) | copy-start | bytes 6148
  10.4 74.3 %copy-start.6 = (bf16[1,512,1024]{2,1,0:T(8,128)(2,1)S(1)}, bf16[1,512,1024]{2,1,0:T(8,128)(2,1)}, u32[]{:S(2)}) copy-start(bf16[1,512,1024]{2,1,0:T(8,128)(2,1)} %param.24) | copy-start | bytes 3145732
  79.8 2.6 copy-start
  83.6 12.6 %copy-start.3 = (s32[512,1]{1,0:T(8,128)}, s32[512,1]{1,0:T(8,128)S(1)}, u32[]{:S(2)}) copy-start(s32[512,1]{1,0:T(8,128)S(1)} %copy.110.seg_ref.refs_4_.refs_9_) | copy-start | bytes 6148
  84.6 11.6 %copy-start.4 = (f32[512,128]{1,0:T(8,128)}, f32[512,128]{1,0:T(8,128)S(1)}, u32[]{:S(2)}) copy-start(f32[512,128]{1,0:T(8,128)S(1)} %get-tuple-element.140.sin_ref.refs_8_) | copy-start | bytes 786436
  84.6 11.6 %copy-start.5 = (f32[512,128]{1,0:T(8,128)}, f32[512,128]{1,0:T(8,128)S(1)}, u32[]{:S(2)}) copy-start(f32[512,128]{1,0:T(8,128)S(1)} %get-tuple-element.141.cos_ref.refs_7_) | copy-start | bytes 786436
  84.7 11.5 %copy-start.8 = (f32[2,6144]{1,0:T(2,128)}, f32[2,6144]{1,0:T(2,128)S(1)}, u32[]{:S(2)}) copy-start(f32[2,6144]{1,0:T(2,128)S(1)} %broadcast_add_fusion.emb_ref.refs_6_.refs_10_) | copy-start | bytes 147460
  84.7 4.3 %copy-start.1 = (bf16[2,2,4,2,32,3072]{5,4,3,2,1,0:T(8,128)(2,1)S(1)}, bf16[2,2,4,2,32,3072]{5,4,3,2,1,0:T(8,128)(2,1)}, u32[]{:S(2)}) copy-start(bf16[2,2,4,2,32,3072]{5,4,3,2,1,0:T(8,128)(2,1)} %copy-done) | copy-start | bytes 18874372
  97.2 26.0 %all-to-all-start = ((bf16[4,512,384]{2,1,0:T(8,128)(2,1)}), bf16[4,512,384]{2,1,0:T(8,128)(2,1)S(1)}, u32[]{:S(2)}, u32[]{:S(2)}) async-start(bf16[4,512,384]{2,1,0:T(8,128)(2,1)} %get-tuple-element.95), calls=%async_computation | async-start | bytes 3145728 | tf_op jit(solution)/shard_map/all_to_all | solution.py:815
  123.2 7.6 %copy-start.11 = (bf16[4,512,384]{2,1,0:T(8,128)(2,1)}, bf16[4,512,384]{2,1,0:T(8,128)(2,1)S(1)}, u32[]{:S(2)}) copy-start(bf16[4,512,384]{2,1,0:T(8,128)(2,1)S(1)} %all-to-all-done) | copy-start | bytes 4718596
  123.2 28.1 %all-to-all-start.1 = ((bf16[4,512,384]{2,1,0:T(8,128)(2,1)}), bf16[4,512,384]{2,1,0:T(8,128)(2,1)}, u32[]{:S(2)}, u32[]{:S(2)}) async-start(bf16[4,512,384]{2,1,0:T(8,128)(2,1)} %get-tuple-element.98), calls=%async_computation.1 | async-start | bytes 3145728 | tf_op jit(solution)/shard_map/all_to_all | solution.py:815
  127.6 280.3 %reduce-scatter.2.cloned.1.call-start = ((), (), s32[]{:S(2)}) async-start(), calls=%async_computation.5 | async-start | bytes 6488064 | tf_op jit(solution)/shard_map/reduce_scatter | solution.py:826
  244.3 36.8 %all-to-all-start.2 = ((bf16[4,512,384]{2,1,0:T(8,128)(2,1)}), bf16[4,512,384]{2,1,0:T(8,128)(2,1)}, u32[]{:S(2)}, u32[]{:S(2)}) async-start(bf16[4,512,384]{2,1,0:T(8,128)(2,1)} %bitcast.80), calls=%async_computation.2 | async-start | bytes 3145728 | tf_op jit(solution)/shard_map/all_to_all | solution.py:815
  396.1 4.3 %copy-start.14 = (f32[32,3072]{1,0:T(8,128)S(1)}, f32[32,3072]{1,0:T(8,128)}, u32[]{:S(2)}) copy-start(f32[32,3072]{1,0:T(8,128)} %get-tuple-element.115) | copy-start | bytes 1179652
  398.3 5.7 %copy-start.15 = (f32[4,8,16,128]{3,2,1,0:T(8,128)S(1)}, f32[4,8,16,128]{3,2,1,0:T(8,128)}, u32[]{:S(2)}) copy-start(f32[4,8,16,128]{3,2,1,0:T(8,128)} %get-tuple-element.112) | copy-start | bytes 786436
  398.3 7.1 %copy-start.19 = (f32[8,768]{1,0:T(8,128)S(1)}, f32[8,768]{1,0:T(8,128)}, u32[]{:S(2)}) copy-start(f32[8,768]{1,0:T(8,128)} %get-tuple-element.114) | copy-start | bytes 73732
  400.6 12.3 %copy-start.12 = (bf16[512,1024]{1,0:T(8,128)(2,1)S(1)}, bf16[512,1024]{1,0:T(8,128)(2,1)}, u32[]{:S(2)}) copy-start(bf16[512,1024]{1,0:T(8,128)(2,1)} %get-tuple-element.100) | copy-start | bytes 3145732
  404.1 9.8 %copy-start.10 = (f32[512,1024]{1,0:T(8,128)S(1)}, f32[512,1024]{1,0:T(8,128)}, u32[]{:S(2)}) copy-start(f32[512,1024]{1,0:T(8,128)} %get-tuple-element.111) | copy-start | bytes 6291460
  413.9 1.7 copy-start.13
  (2 other events, 1.6 us)
Sparse Core Ops, SparseCore 0:
  11.5 111.6 all-gather.1
  211.6 131.2 reduce-scatter.1

commit v7 on v6

--- a/solution.py
+++ b/solution.py
@@ -603,7 +603,7 @@
                     def _(u): one({left[0]:u})
             go.append(self.send(k,st))
         self.go=go
-    def last(self,out,col=0):
+    def last(self,put):
         p=self.p
         for k,(lo,hi,order) in enumerate(self.parts):
             buf=self.bufs[k][2][0]
@@ -611,16 +611,16 @@
             for d,c in self.go[k]:
                 c.wait_recv()
                 t=t+buf[d-1].astype(f32)
-            out[:,col+lo:col+hi]=t
+            put(lo,t)
     def finish(self):
         for c in self.sent: c.wait_send()
 
-REST=(lambda w,j:((0,w,"xyz"),) if j==ORD_X else ((0,w,"yzx"),)); QKV=(lambda w:((0,w//2,"yxz"),(w//2,w,"xyz")))
+REST=(lambda w,j:((0,w//2,"yxz"),(w//2,w,"xyz"))); QKV=(lambda w:((0,w//2,"yzx"),(w//2,w,"xyz")))
 
 def final_kernel(nd,ns,R,here,refs,scr):
     (g_ref,rest_ref,x_hbm,n1_hbm,dm_hbm,wq_hbm,cos_ref,sin_ref,seg_ref,emb_ref,gbm_ref,gem_ref,act,wada)=refs[:14]
     (gf_ref,rest_out,qkv_out,bias_all,gada,gbada,dact)=refs[14:]
-    (g,x_ref,n1_ref,dm_ref,w_ref,dps,gw,gbv,gev,bsc,bout,hsum,demb,dscr)=scr[:14]
+    (g,x_ref,n1_ref,dm_ref,w_ref,dps,gw,gbv,gev,bsc,bout,hsum,demb,dscr)=scr[:14]; rtmp=scr[-1]; scr=scr[:-1]
     (gs,gr,gl,gh,ld,hs,hr,qs,qr,ds_,dr,bs,br)=scr[14:27]
     pools=scr[27:]
     p=Place(nd,ns); me=p.h*ns+p.s
@@ -728,11 +728,27 @@
     qc=[remote(demb.at[p.s],demb.at[p.s],qs.at[d],qr.at[d],(p.h,lax.rem(p.s+d,ns))) for d in range(1,ns)]
     qkv[ne+2].step(); qkv[ne+1].step(); bias.step()
     for j in range(ne+3,nq): qkv[j].step(); qkv[j-1].step()
-    for j,a in enumerate(rest): a.last(rest_out,j*D)
-    bias.last(bout)
+    for j,a in enumerate(rest):
+        def put(c,t,j=j): rtmp[j,:,c:c+t.shape[1]]=t
+        a.last(put)
+    wide=128*nr
+    r0=lax.broadcasted_iota(jnp.int32,(wide,wide),0); c0=lax.broadcasted_iota(jnp.int32,(wide,wide),1)
+    perm=jnp.where((r0//128==c0//K%nr)&(r0%128//K==c0//(K*nr))&(r0%K==c0%K),1.0,0.0)
+    for b in range(D//128):
+        v=jnp.concatenate([rtmp[j,:,b*128:(b+1)*128] for j in range(nr)],1)
+        rest_out[:,b*wide:(b+1)*wide]=lax.dot_general(v,perm,NN,precision=lax.Precision.HIGHEST,preferred_element_type=f32)
+    def keep(c,t): bout[:,c:c+t.shape[1]]=t
+    bias.last(keep)
+    def home(j):
+        def put(c,t):
+            for k in range(t.shape[1]//128):
+                s=(j*QW+c)//128+k
+                at=(s%3*nd+s//3%nd)*PP+s//3//nd
+                qkv_out[:,at*128:(at+1)*128]=t[:,k*128:(k+1)*128]
+        return put
     bias_all[p.h,p.s]=bout[...]
     bc=along_head(p,lambda d,h,dev: remote(bout,bias_all.at[p.h,p.s],bs.at[0,d],br.at[0,d],dev))
-    for j in range(ne): qkv[j].last(qkv_out,j*QW)
+    for j in range(ne): qkv[j].last(home(j))
     for c in qc: c.wait()
     qkv[nq-1].step()
     Q=ns*16
@@ -755,7 +771,7 @@
     gbada[...]=dot(jnp.where(c8%16//2==r8,1.0,0.0).astype(bf),flat)
     for c in dc: c.wait()
     dc=along_head(p,lambda d,h,dev: remote(dact.at[p.h],dact.at[p.h],ds_.at[1,d],dr.at[1,d],dev))
-    for j in range(ne,nq): qkv[j].last(qkv_out,j*QW)
+    for j in range(ne,nq): qkv[j].last(home(j))
     for a in rest+qkv+[bias]: a.finish()
     for i in range(NR):
         for c in sends[i]: c.wait_send()
@@ -772,6 +788,7 @@
     for j in range(H//D): scr+=Reduce.scratch(nd,ns,K,D,bf,REST(D,j),False)
     for _ in range(3*D//QW): scr+=Reduce.scratch(nd,ns,K,QW,bf,QKV(QW),True)
     scr+=Reduce.scratch(nd,ns,8,256,f32,QKV(256),True)
+    scr+=[M((H//D,K,D),f32)]
     m=len(here)
     def k(*refs): final_kernel(nd,ns,R,refs[:m],refs[m:m+14+len(outs)],refs[m+14+len(outs):])
     return pl.pallas_call(k,out_shape=tuple(outs),in_specs=[ANY]*(6+m)+[V]*8,out_specs=(V,)*len(outs),scratch_shapes=scr,
@@ -838,7 +855,7 @@
         if order: v=order(v[None])[0]
         gbs.append(lax.dynamic_slice_in_dim(v,dev*(k//N),k//N,0))
     gdown=gdo[:,:H].reshape(K,nt,D).transpose(1,0,2).reshape(nt*K,D)
-    return (out[None],gx[None],gtime,gada,gbada,restore(gqkv),gbs[0],gdo[:,H:],gbs[1],unhide(gup),gbs[2],gdown,gbs[3])
+    return (out[None],gx[None],gtime,gada,gbada,gqkv,gbs[0],gdo[:,H:],gbs[1],gup,gbs[2],gdown,gbs[3])
 
 
 def solution(mesh):

time: 431 us -> 420 us (0.974); the launches traced: 424 us -> 418 us
    pallas_call x1, Pallas kernels: 115 us -> 102 us  [final(): pl.pallas_call(k, out_shape=tuple(outs), in_specs=[ANY] * (6 + m) + [V] *...]
    pallas_call x1, Pallas kernels: 39.7 us -> 49.2 us  [mid(): pl.pallas_call(functools.partial(mid_kernel, PP, R=R, nd=nd, ns=ns), out_...]
    reshape x4 -> x0, local copies, waits for them, and re-layouts: 4.74 us -> none  [the longest x2 3.39 us: unhide(): return w.reshape(-1, nt, N, K).transpose(0, 2, 1, 3).reshape(-1, H)]
  transfers between devices with their start and end apart: 5 -> 5, of which waited for: 1 -> 1; matrix products, arithmetic and copies ran while one was open for 5% -> 4% of each run, Pallas kernels for 70% -> 68%
where the time goes in v7:
time: 420 us; the launch traced here: 418 us
  Pallas kernels  333 us (79%)
  local copies, waits for them, and re-layouts  30.8 us (7%)
  waiting for transfers between devices  17.7 us (4%)
  between operations  14.9 us (4%)
  starting transfers between devices  13.3 us (3%)
  other arithmetic  8.48 us (2%)
    pallas_call x1, Pallas kernels, final(): pl.pallas_call(k, out_shape=tuple(outs), in_specs=[ANY] * (6 + m) + [V] *...  102 us
    pallas_call x1, Pallas kernels, entry(): pl.pallas_call(functools.partial(entry_kernel, nd, ns, nw), out_shape=tup...  68.6 us
    pallas_call x2, Pallas kernels, attn_bwd(): pl.pallas_call(functools.partial(bwd_kernel, T=T, nh=nh), out_shape=jax.S...  64.6 us
    pallas_call x1, Pallas kernels, mid(): pl.pallas_call(functools.partial(mid_kernel, PP, R=R, nd=nd, ns=ns), out_...  49.2 us
    pallas_call x2, Pallas kernels, attn_fwd(): pl.pallas_call(functools.partial(fwd_kernel, T=T, nh=nh), out_shape=(jax....  40.9 us
    all_to_all x3, waiting for transfers between devices, swap(): return lax.all_to_all(a, 'head', split_axis=0, concat_axis=0, tiled=True)  17.6 us
    unnamed x64, local copies, waits for them, and re-layouts  13.6 us
    all_to_all x3, starting transfers between devices, swap(): return lax.all_to_all(a, 'head', split_axis=0, concat_axis=0, tiled=True)  13 us
  transfers between devices with their start and end apart: 5, of which 1 were waited for; matrix products, arithmetic and copies ran while one was open for 4% of the time, Pallas kernels for 68%

profile of v7, /device:TPU:0, one launch (start us, length us, event | category | flops | bytes accessed | tf_op | source)
XLA Modules:
  0.0 418.0 jit_solution(6997703312213532799)
XLA Ops:
  7.3 1.4 reshape.349
  9.6 0.7 pad_maximum_fusion
  11.1 68.6 %entry.1 = (bf16[2,2,4,2,32,3072]{5,4,3,2,1,0:T(8,128)(2,1)S(1)}, bf16[4,8,16,512]{3,2,1,0:T(8,128)(2,1)S(1)}, s32[4,8,512]{2,1,0:T(8,128)S(1)}, f32[16,768]{1,0:T(8,128)S(1)}, bf16[64,128]{1,0:T(8,128)(2,1)S(1)}) custom-call(bf16[32,3072]{1,0:T(8,128)(2,1)S(1)} %reshape.339.refs_0_, bf16[16,512]{1,0:T(8,128)(2,1)S(1)} %scatter.16.refs_1_, ...), custom_call_target="tpu_custom_call" | custom-call | tf_op jit(solution)/shard_map/entry/pallas_call | solution.py:423
  79.8 2.6 copy-done
  83.6 1.0 negate_select_fusion
  84.7 4.2 %copy-done.1 = bf16[2,2,4,2,32,3072]{5,4,3,2,1,0:T(8,128)(2,1)S(1)} copy-done((bf16[2,2,4,2,32,3072]{5,4,3,2,1,0:T(8,128)(2,1)S(1)}, bf16[2,2,4,2,32,3072]{5,4,3,2,1,0:T(8,128)(2,1)}, u32[]{:S(2)}) %copy-start.1) | copy-done | bytes 6291480
  88.9 7.3 %qkv_proj.1 = (bf16[512,1024]{1,0:T(8,128)(2,1)S(1)}, bf16[4,512,384]{2,1,0:T(8,128)(2,1)}, bf16[4,512,384]{2,1,0:T(8,128)(2,1)}) custom-call(bf16[512,1024]{1,0:T(8,128)(2,1)S(1)} %bitcast.69, s32[512,1]{1,0:T(8,128)S(1)} %copy.101.seg_ref.refs_4_.refs_9_, f32[2,6144]{1,0:T(2,128)S(1)} %broadcast_add_fusion.emb_ref.refs_6_.refs_10_, ...), custom_call_target="tpu_custom_call" | custom-call | flops 3221225472 | bytes 14680064 | tf_op jit(solution)/shard_map/qkv_proj/pallas_call | solution.py:236
  96.2 1.0 copy-done.7
  97.2 3.6 all-to-all-start
  103.0 0.9 copy.106.refs_5_
  105.5 17.6 %all-to-all-done = bf16[4,512,384]{2,1,0:T(8,128)(2,1)S(1)} async-done(((bf16[4,512,384]{2,1,0:T(8,128)(2,1)}), bf16[4,512,384]{2,1,0:T(8,128)(2,1)S(1)}, u32[]{:S(2)}, u32[]{:S(2)}) %all-to-all-start) | async-done | bytes 1572896 | tf_op jit(solution)/shard_map/all_to_all | solution.py:832
  123.2 4.4 %all-to-all-start.1 = ((bf16[4,512,384]{2,1,0:T(8,128)(2,1)}), bf16[4,512,384]{2,1,0:T(8,128)(2,1)}, u32[]{:S(2)}, u32[]{:S(2)}) async-start(bf16[4,512,384]{2,1,0:T(8,128)(2,1)} %get-tuple-element.98), calls=%async_computation.1 | async-start | bytes 3145728 | tf_op jit(solution)/shard_map/all_to_all | solution.py:832
  127.9 2.7 select_convert_fusion
  130.6 20.5 %attn_fwd.2 = (bf16[2048,128]{1,0:T(8,128)(2,1)}, f32[2048,128]{1,0:T(8,128)}) custom-call(s32[4]{0:T(128)} %get-tuple-element.126.lo_ref, s32[4]{0:T(128)} %broadcast_add_fusion.2.hi_ref, bf16[2048,384]{1,0:T(8,128)(2,1)} %bitcast.74, bf16[2048,128]{1,0:T(8,128)(2,1)} %get-tuple-element.143.auxq_ref, bf16[2048,128]{1,0:T(8,128)(2,1)} %get-tuple-element.142.auxk_ref), custom_call_target="tpu_custom_call" | custom-call | flops 8589934592 | bytes 4194304 | tf_op jit(solution)/shard_map/attn_fwd/pallas_call | solution.py:87
  151.1 20.4 %attn_fwd.3 = (bf16[2048,128]{1,0:T(8,128)(2,1)}, f32[2048,128]{1,0:T(8,128)}) custom-call(s32[4]{0:T(128)} %get-tuple-element.126.lo_ref, s32[4]{0:T(128)} %broadcast_add_fusion.2.hi_ref, bf16[2048,384]{1,0:T(8,128)(2,1)} %bitcast.19.qkv_ref, bf16[2048,128]{1,0:T(8,128)(2,1)} %get-tuple-element.143.auxq_ref, bf16[2048,128]{1,0:T(8,128)(2,1)} %get-tuple-element.142.auxk_ref), custom_call_target="tpu_custom_call" | custom-call | flops 8589934592 | bytes 4194304 | tf_op jit(solution)/shard_map/attn_fwd/pallas_call | solution.py:87
  171.5 49.2 %mid.1 = (bf16[4,512,128]{2,1,0:T(8,128)(2,1)}, bf16[4,512,128]{2,1,0:T(8,128)(2,1)}, bf16[512,1024]{1,0:T(8,128)(2,1)}, f32[512,1024]{1,0:T(8,128)}, bf16[1024,...) custom-call(bf16[4,512,128]{2,1,0:T(8,128)(2,1)} %bitcast.113, ...), custom_call_target="tpu_custom_call" | custom-call | flops 16106127360 | bytes 31457280 | tf_op jit(solution)/shard_map/mid/pallas_call | solution.py:523
  221.3 32.3 %attn_bwd.2 = bf16[2048,384]{1,0:T(8,128)(2,1)} custom-call(s32[4]{0:T(128)} %get-tuple-element.125.lo_ref, s32[4]{0:T(128)} %broadcast_add_fusion.1.hi_ref, bf16[2048,384]{1,0:T(8,128)(2,1)} %bitcast.75, bf16[2048,128]{1,0:T(8,128)(2,1)} %get-tuple-element.97.o_ref, bf16[2048,128]{1,0:T(8,128)(2,1)} %bitcast.115, f32[2048,128]{1,0:T(8,128)} %get-tuple-element.102.lse_ref, ...), custom_call_target="tpu_custom_call" | custom-call | flops 21474836480 | bytes 8388608 | tf_op jit(solution)/shard_map/attn_bwd/pallas_call | solution.py:160
  253.5 5.0 %all-to-all-start.2 = ((bf16[4,512,384]{2,1,0:T(8,128)(2,1)}), bf16[4,512,384]{2,1,0:T(8,128)(2,1)}, u32[]{:S(2)}, u32[]{:S(2)}) async-start(bf16[4,512,384]{2,1,0:T(8,128)(2,1)} %bitcast.76), calls=%async_computation.2 | async-start | bytes 3145728 | tf_op jit(solution)/shard_map/all_to_all | solution.py:832
  258.6 32.3 %attn_bwd.3 = bf16[2048,384]{1,0:T(8,128)(2,1)} custom-call(s32[4]{0:T(128)} %get-tuple-element.125.lo_ref, s32[4]{0:T(128)} %broadcast_add_fusion.1.hi_ref, bf16[2048,384]{1,0:T(8,128)(2,1)} %bitcast.19.qkv_ref, bf16[2048,128]{1,0:T(8,128)(2,1)} %get-tuple-element.99.o_ref, bf16[2048,128]{1,0:T(8,128)(2,1)} %bitcast.114, ...), custom_call_target="tpu_custom_call" | custom-call | flops 21474836480 | bytes 8388608 | tf_op jit(solution)/shard_map/attn_bwd/pallas_call | solution.py:160
  290.9 102.2 %final.1 = (f32[512,1024]{1,0:T(8,128)}, f32[32,2048]{1,0:T(8,128)}, f32[32,3072]{1,0:T(8,128)}, f32[4,8,8,256]{3,2,1,0:T(8,128)}, f32[32,6144]{1,0:T(8,128)}, /...) custom-call(bf16[4,512,384]{2,1,0:T(8,128)(2,1)} %all-to-all-done.2.refs_0_, bf16[4,512,384]{2,1,0:T(8,128)(2,1)} %bitcast.73, ...), custom_call_target="tpu_custom_call" | custom-call | tf_op jit(solution)/shard_map/final/pallas_call | solution.py:794
  393.1 1.1 slice.120
  394.2 0.9 slice_reduce_fusion
  395.3 1.1 reduce_sum.9
  397.6 0.7 reshape.363
  400.8 1.6 slice.135
  402.4 1.2 reshape.364
  403.6 0.8 copy.111
  404.4 1.5 slice.133
  405.9 1.0 copy.133
  406.9 1.3 copy.134
  408.6 0.9 copy.135
  409.4 0.7 copy.136
  (124 shorter events, 12.4 us)
Async XLA Ops:
  7.2 2.3 copy-start.17
  7.2 2.4 copy-start.18
  7.2 3.2 copy-start.16
  7.2 164.3 %all-gather.2.cloned.1.call-start = ((), (), s32[]{:S(2)}) async-start(), calls=%async_computation.4 | async-start | bytes 10813440 | tf_op jit(solution)/shard_map/all_gather | solution.py:819
  8.7 2.2 copy-start.23
  8.7 2.2 copy-start.24
  8.7 2.2 copy-start.25
  8.7 2.2 copy-start.26
  8.7 2.2 copy-start.27
  8.7 2.3 copy-start.20
  8.7 2.3 copy-start.21
  8.7 2.3 copy-start.19
  8.8 2.4 copy-start.2
  9.6 73.8 %copy-start.22 = (s32[1,512]{1,0:T(1,128)S(1)}, s32[1,512]{1,0:T(1,128)}, u32[]{:S(2)}) copy-start(s32[1,512]{1,0:T(1,128)} %param.28) | copy-start | bytes 6148
  10.4 74.3 %copy-start.6 = (bf16[1,512,1024]{2,1,0:T(8,128)(2,1)S(1)}, bf16[1,512,1024]{2,1,0:T(8,128)(2,1)}, u32[]{:S(2)}) copy-start(bf16[1,512,1024]{2,1,0:T(8,128)(2,1)} %param.24) | copy-start | bytes 3145732
  79.8 2.6 copy-start
  83.6 12.6 %copy-start.3 = (s32[512,1]{1,0:T(8,128)}, s32[512,1]{1,0:T(8,128)S(1)}, u32[]{:S(2)}) copy-start(s32[512,1]{1,0:T(8,128)S(1)} %copy.101.seg_ref.refs_4_.refs_9_) | copy-start | bytes 6148
  84.6 11.6 %copy-start.4 = (f32[512,128]{1,0:T(8,128)}, f32[512,128]{1,0:T(8,128)S(1)}, u32[]{:S(2)}) copy-start(f32[512,128]{1,0:T(8,128)S(1)} %get-tuple-element.140.sin_ref.refs_8_) | copy-start | bytes 786436
  84.6 11.6 %copy-start.5 = (f32[512,128]{1,0:T(8,128)}, f32[512,128]{1,0:T(8,128)S(1)}, u32[]{:S(2)}) copy-start(f32[512,128]{1,0:T(8,128)S(1)} %get-tuple-element.141.cos_ref.refs_7_) | copy-start | bytes 786436
  84.7 11.5 %copy-start.8 = (f32[2,6144]{1,0:T(2,128)}, f32[2,6144]{1,0:T(2,128)S(1)}, u32[]{:S(2)}) copy-start(f32[2,6144]{1,0:T(2,128)S(1)} %broadcast_add_fusion.emb_ref.refs_6_.refs_10_) | copy-start | bytes 147460
  84.7 4.3 %copy-start.1 = (bf16[2,2,4,2,32,3072]{5,4,3,2,1,0:T(8,128)(2,1)S(1)}, bf16[2,2,4,2,32,3072]{5,4,3,2,1,0:T(8,128)(2,1)}, u32[]{:S(2)}) copy-start(bf16[2,2,4,2,32,3072]{5,4,3,2,1,0:T(8,128)(2,1)} %copy-done) | copy-start | bytes 18874372
  96.2 1.0 copy-start.7
  97.2 26.0 %all-to-all-start = ((bf16[4,512,384]{2,1,0:T(8,128)(2,1)}), bf16[4,512,384]{2,1,0:T(8,128)(2,1)S(1)}, u32[]{:S(2)}, u32[]{:S(2)}) async-start(bf16[4,512,384]{2,1,0:T(8,128)(2,1)} %get-tuple-element.95), calls=%async_computation | async-start | bytes 3145728 | tf_op jit(solution)/shard_map/all_to_all | solution.py:832
  123.2 7.4 %copy-start.11 = (bf16[4,512,384]{2,1,0:T(8,128)(2,1)}, bf16[4,512,384]{2,1,0:T(8,128)(2,1)S(1)}, u32[]{:S(2)}) copy-start(bf16[4,512,384]{2,1,0:T(8,128)(2,1)S(1)} %all-to-all-done) | copy-start | bytes 4718596
  123.2 27.9 %all-to-all-start.1 = ((bf16[4,512,384]{2,1,0:T(8,128)(2,1)}), bf16[4,512,384]{2,1,0:T(8,128)(2,1)}, u32[]{:S(2)}, u32[]{:S(2)}) async-start(bf16[4,512,384]{2,1,0:T(8,128)(2,1)} %get-tuple-element.98), calls=%async_computation.1 | async-start | bytes 3145728 | tf_op jit(solution)/shard_map/all_to_all | solution.py:832
  127.6 273.3 %reduce-scatter.2.cloned.1.call-start = ((), (), s32[]{:S(2)}) async-start(), calls=%async_computation.5 | async-start | bytes 6488064 | tf_op jit(solution)/shard_map/reduce_scatter | solution.py:843
  253.5 37.3 %all-to-all-start.2 = ((bf16[4,512,384]{2,1,0:T(8,128)(2,1)}), bf16[4,512,384]{2,1,0:T(8,128)(2,1)}, u32[]{:S(2)}, u32[]{:S(2)}) async-start(bf16[4,512,384]{2,1,0:T(8,128)(2,1)} %bitcast.76), calls=%async_computation.2 | async-start | bytes 3145728 | tf_op jit(solution)/shard_map/all_to_all | solution.py:832
  393.1 12.8 %copy-start.12 = (bf16[512,1024]{1,0:T(8,128)(2,1)S(1)}, bf16[512,1024]{1,0:T(8,128)(2,1)}, u32[]{:S(2)}) copy-start(bf16[512,1024]{1,0:T(8,128)(2,1)} %get-tuple-element.100) | copy-start | bytes 3145732
  396.3 10.5 %copy-start.10 = (f32[512,1024]{1,0:T(8,128)S(1)}, f32[512,1024]{1,0:T(8,128)}, u32[]{:S(2)}) copy-start(f32[512,1024]{1,0:T(8,128)} %get-tuple-element.111) | copy-start | bytes 6291460
  406.9 1.7 copy-start.13
  406.9 2.6 copy-start.14
  408.5 1.6 copy-start.15
  (1 other events, 0.6 us)
Sparse Core Ops, SparseCore 0:
  11.5 111.6 all-gather.1
  220.9 126.7 reduce-scatter.1

commit v8 on v7

--- a/solution.py
+++ b/solution.py
@@ -422,7 +422,7 @@
     for _ in shards: scr+=Gather.sems(nd,ns)
     return pl.pallas_call(functools.partial(entry_kernel,nd,ns,nw),out_shape=tuple(outs),
         in_specs=[ANY]*(nw+1)+[V,ANY,V],out_specs=tuple([ANY]*(nw+2)+[V,V]),scratch_shapes=scr,
-        compiler_params=pltpu.CompilerParams(collective_id=0,has_side_effects=True,vmem_limit_bytes=40*2**20),name="entry")(*shards,bias,time,ids,wada)
+        compiler_params=pltpu.CompilerParams(collective_id=0,has_side_effects=True,vmem_limit_bytes=60*2**20),name="entry")(*shards,bias,time,ids,wada)
 
 def make_remote(src,dst,ss,rs,dev):
     return pltpu.make_async_remote_copy(src_ref=src,dst_ref=dst,send_sem=ss,recv_sem=rs,device_id=dev,device_id_type=pl.DeviceIdType.MESH)

time: 420 us -> 424 us (level)
  Pallas kernels: 333 us -> 338 us
    unnamed x64 -> x60, local copies, waits for them, and re-layouts: 13.6 us -> 9.04 us
  transfers between devices with their start and end apart: 5 -> 5, of which waited for: 1 -> 1; matrix products, arithmetic and copies ran while one was open for 4% -> 5% of each run, Pallas kernels for 68% -> 68%
where the time goes in v8:
time: 424 us; the launch traced here: 421 us
  Pallas kernels  338 us (80%)
  local copies, waits for them, and re-layouts  28.4 us (7%)
  waiting for transfers between devices  15.4 us (4%)
  between operations  14.8 us (3%)
  starting transfers between devices  13.1 us (3%)
  other arithmetic  11.8 us (3%)
    pallas_call x1, Pallas kernels, final(): pl.pallas_call(k, out_shape=tuple(outs), in_specs=[ANY] * (6 + m) + [V] *...  104 us
    pallas_call x1, Pallas kernels, entry(): pl.pallas_call(functools.partial(entry_kernel, nd, ns, nw), out_shape=tup...  71.2 us
    pallas_call x2, Pallas kernels, attn_bwd(): pl.pallas_call(functools.partial(bwd_kernel, T=T, nh=nh), out_shape=jax.S...  64.7 us
    pallas_call x1, Pallas kernels, mid(): pl.pallas_call(functools.partial(mid_kernel, PP, R=R, nd=nd, ns=ns), out_...  49.3 us
    pallas_call x2, Pallas kernels, attn_fwd(): pl.pallas_call(functools.partial(fwd_kernel, T=T, nh=nh), out_shape=(jax....  40.9 us
    all_to_all x3, waiting for transfers between devices, swap(): return lax.all_to_all(a, 'head', split_axis=0, concat_axis=0, tiled=True)  15.4 us
    all_to_all x3, starting transfers between devices, swap(): return lax.all_to_all(a, 'head', split_axis=0, concat_axis=0, tiled=True)  12.8 us
    unnamed x60, local copies, waits for them, and re-layouts  9.04 us
  transfers between devices with their start and end apart: 5, of which 1 were waited for; matrix products, arithmetic and copies ran while one was open for 5% of the time, Pallas kernels for 68%

profile of v8, /device:TPU:0, one launch (start us, length us, event | category | flops | bytes accessed | tf_op | source)
XLA Modules:
  0.0 421.3 jit_solution(4091903972572704943)
XLA Ops:
  7.3 1.4 reshape.349
  10.6 0.8 reshape.339.refs_0_
  12.9 71.2 %entry.1 = (bf16[2,2,4,2,32,3072]{5,4,3,2,1,0:T(8,128)(2,1)}, bf16[4,8,16,512]{3,2,1,0:T(8,128)(2,1)}, s32[4,8,512]{2,1,0:T(8,128)}, f32[16,768]{1,0:T(8,128)}, bf16[64,128]{1,0:T(8,128)(2,1)}) custom-call(bf16[32,3072]{1,0:T(8,128)(2,1)} %reshape.339.refs_0_, bf16[16,512]{1,0:T(8,128)(2,1)} %scatter.16.refs_1_, f32[8,1024]{1,0:T(8,128)} %pad_convert_fusion.refs_2_, ...), custom_call_target="tpu_custom_call" | custom-call | tf_op jit(solution)/shard_map/entry/pallas_call | solution.py:423
  84.1 1.0 slice_convert_fusion
  85.3 0.8 reshape.341
  86.5 1.0 negate_select_fusion
  87.6 2.9 copy-done
  90.5 7.3 %qkv_proj.1 = (bf16[512,1024]{1,0:T(8,128)(2,1)S(1)}, bf16[4,512,384]{2,1,0:T(8,128)(2,1)}, bf16[4,512,384]{2,1,0:T(8,128)(2,1)}) custom-call(bf16[512,1024]{1,0:T(8,128)(2,1)S(1)} %bitcast.69, s32[512,1]{1,0:T(8,128)S(1)} %copy.101.seg_ref.refs_4_.refs_9_, f32[2,6144]{1,0:T(2,128)S(1)} %broadcast_add_fusion.emb_ref.refs_6_.refs_10_, ...), custom_call_target="tpu_custom_call" | custom-call | flops 3221225472 | bytes 14680064 | tf_op jit(solution)/shard_map/qkv_proj/pallas_call | solution.py:236
  97.8 1.0 copy-done.5
  98.8 3.6 all-to-all-start
  104.6 0.9 copy.106.refs_5_
  105.4 1.3 fusion.6
  108.0 0.9 compare_select_fusion.1
  108.8 15.4 %all-to-all-done = bf16[4,512,384]{2,1,0:T(8,128)(2,1)S(1)} async-done(((bf16[4,512,384]{2,1,0:T(8,128)(2,1)}), bf16[4,512,384]{2,1,0:T(8,128)(2,1)S(1)}, u32[]{:S(2)}, u32[]{:S(2)}) %all-to-all-start) | async-done | bytes 1572896 | tf_op jit(solution)/shard_map/all_to_all | solution.py:832
  124.3 4.4 %all-to-all-start.1 = ((bf16[4,512,384]{2,1,0:T(8,128)(2,1)}), bf16[4,512,384]{2,1,0:T(8,128)(2,1)}, u32[]{:S(2)}, u32[]{:S(2)}) async-start(bf16[4,512,384]{2,1,0:T(8,128)(2,1)} %get-tuple-element.98), calls=%async_computation.1 | async-start | bytes 3145728 | tf_op jit(solution)/shard_map/all_to_all | solution.py:832
  128.9 2.7 select_convert_fusion
  131.7 20.4 %attn_fwd.2 = (bf16[2048,128]{1,0:T(8,128)(2,1)}, f32[2048,128]{1,0:T(8,128)}) custom-call(s32[4]{0:T(128)} %get-tuple-element.126.lo_ref, s32[4]{0:T(128)} %broadcast_add_fusion.2.hi_ref, bf16[2048,384]{1,0:T(8,128)(2,1)} %bitcast.74, bf16[2048,128]{1,0:T(8,128)(2,1)} %get-tuple-element.143.auxq_ref, bf16[2048,128]{1,0:T(8,128)(2,1)} %get-tuple-element.142.auxk_ref), custom_call_target="tpu_custom_call" | custom-call | flops 8589934592 | bytes 4194304 | tf_op jit(solution)/shard_map/attn_fwd/pallas_call | solution.py:87
  152.1 20.4 %attn_fwd.3 = (bf16[2048,128]{1,0:T(8,128)(2,1)}, f32[2048,128]{1,0:T(8,128)}) custom-call(s32[4]{0:T(128)} %get-tuple-element.126.lo_ref, s32[4]{0:T(128)} %broadcast_add_fusion.2.hi_ref, bf16[2048,384]{1,0:T(8,128)(2,1)} %bitcast.19.qkv_ref, bf16[2048,128]{1,0:T(8,128)(2,1)} %get-tuple-element.143.auxq_ref, bf16[2048,128]{1,0:T(8,128)(2,1)} %get-tuple-element.142.auxk_ref), custom_call_target="tpu_custom_call" | custom-call | flops 8589934592 | bytes 4194304 | tf_op jit(solution)/shard_map/attn_fwd/pallas_call | solution.py:87
  172.6 49.3 %mid.1 = (bf16[4,512,128]{2,1,0:T(8,128)(2,1)}, bf16[4,512,128]{2,1,0:T(8,128)(2,1)}, bf16[512,1024]{1,0:T(8,128)(2,1)}, f32[512,1024]{1,0:T(8,128)}, bf16[1024,...) custom-call(bf16[4,512,128]{2,1,0:T(8,128)(2,1)} %bitcast.113, ...), custom_call_target="tpu_custom_call" | custom-call | flops 16106127360 | bytes 31457280 | tf_op jit(solution)/shard_map/mid/pallas_call | solution.py:523
  222.4 32.3 %attn_bwd.2 = bf16[2048,384]{1,0:T(8,128)(2,1)} custom-call(s32[4]{0:T(128)} %get-tuple-element.125.lo_ref, s32[4]{0:T(128)} %broadcast_add_fusion.1.hi_ref, bf16[2048,384]{1,0:T(8,128)(2,1)} %bitcast.75, bf16[2048,128]{1,0:T(8,128)(2,1)} %get-tuple-element.97.o_ref, bf16[2048,128]{1,0:T(8,128)(2,1)} %bitcast.115, f32[2048,128]{1,0:T(8,128)} %get-tuple-element.102.lse_ref, ...), custom_call_target="tpu_custom_call" | custom-call | flops 21474836480 | bytes 8388608 | tf_op jit(solution)/shard_map/attn_bwd/pallas_call | solution.py:160
  254.7 4.8 %all-to-all-start.2 = ((bf16[4,512,384]{2,1,0:T(8,128)(2,1)}), bf16[4,512,384]{2,1,0:T(8,128)(2,1)}, u32[]{:S(2)}, u32[]{:S(2)}) async-start(bf16[4,512,384]{2,1,0:T(8,128)(2,1)} %bitcast.76), calls=%async_computation.2 | async-start | bytes 3145728 | tf_op jit(solution)/shard_map/all_to_all | solution.py:832
  259.5 32.4 %attn_bwd.3 = bf16[2048,384]{1,0:T(8,128)(2,1)} custom-call(s32[4]{0:T(128)} %get-tuple-element.125.lo_ref, s32[4]{0:T(128)} %broadcast_add_fusion.1.hi_ref, bf16[2048,384]{1,0:T(8,128)(2,1)} %bitcast.19.qkv_ref, bf16[2048,128]{1,0:T(8,128)(2,1)} %get-tuple-element.99.o_ref, bf16[2048,128]{1,0:T(8,128)(2,1)} %bitcast.114, ...), custom_call_target="tpu_custom_call" | custom-call | flops 21474836480 | bytes 8388608 | tf_op jit(solution)/shard_map/attn_bwd/pallas_call | solution.py:160
  291.9 104.5 %final.1 = (f32[512,1024]{1,0:T(8,128)}, f32[32,2048]{1,0:T(8,128)}, f32[32,3072]{1,0:T(8,128)}, f32[4,8,8,256]{3,2,1,0:T(8,128)}, f32[32,6144]{1,0:T(8,128)}, /...) custom-call(bf16[4,512,384]{2,1,0:T(8,128)(2,1)} %all-to-all-done.2.refs_0_, bf16[4,512,384]{2,1,0:T(8,128)(2,1)} %bitcast.73, ...), custom_call_target="tpu_custom_call" | custom-call | tf_op jit(solution)/shard_map/final/pallas_call | solution.py:794
  396.4 1.1 slice.120
  397.5 0.9 slice_reduce_fusion
  398.6 1.1 reduce_sum.9
  404.1 1.6 slice.135
  405.8 1.2 reshape.364
  407.7 1.5 slice.133
  409.2 1.0 copy.133
  410.2 1.3 copy.134
  411.9 0.9 copy.135
  (120 shorter events, 15.4 us)
Async XLA Ops:
  7.2 2.2 copy-start.14
  7.2 2.4 copy-start.15
  7.2 3.2 copy-start.13
  7.2 165.4 %all-gather.2.cloned.1.call-start = ((), (), s32[]{:S(2)}) async-start(), calls=%async_computation.4 | async-start | bytes 10813440 | tf_op jit(solution)/shard_map/all_gather | solution.py:819
  8.7 2.8 copy-start.21
  8.7 2.8 copy-start.22
  8.7 2.8 copy-start.23
  8.7 2.8 copy-start.24
  8.7 2.8 copy-start.25
  8.7 2.9 copy-start.18
  8.7 3.5 copy-start.19
  8.7 3.6 copy-start.17
  9.6 76.7 %copy-start.20 = (s32[1,512]{1,0:T(1,128)S(1)}, s32[1,512]{1,0:T(1,128)}, u32[]{:S(2)}) copy-start(s32[1,512]{1,0:T(1,128)} %param.28) | copy-start | bytes 6148
  10.4 77.2 %copy-start.4 = (bf16[1,512,1024]{2,1,0:T(8,128)(2,1)S(1)}, bf16[1,512,1024]{2,1,0:T(8,128)(2,1)}, u32[]{:S(2)}) copy-start(bf16[1,512,1024]{2,1,0:T(8,128)(2,1)} %param.24) | copy-start | bytes 3145732
  12.3 0.6 copy-start.16
  86.5 11.3 %copy-start.1 = (s32[512,1]{1,0:T(8,128)}, s32[512,1]{1,0:T(8,128)S(1)}, u32[]{:S(2)}) copy-start(s32[512,1]{1,0:T(8,128)S(1)} %copy.101.seg_ref.refs_4_.refs_9_) | copy-start | bytes 6148
  87.5 10.3 %copy-start.2 = (f32[512,128]{1,0:T(8,128)}, f32[512,128]{1,0:T(8,128)S(1)}, u32[]{:S(2)}) copy-start(f32[512,128]{1,0:T(8,128)S(1)} %get-tuple-element.140.sin_ref.refs_8_) | copy-start | bytes 786436
  87.5 10.3 %copy-start.3 = (f32[512,128]{1,0:T(8,128)}, f32[512,128]{1,0:T(8,128)S(1)}, u32[]{:S(2)}) copy-start(f32[512,128]{1,0:T(8,128)S(1)} %get-tuple-element.141.cos_ref.refs_7_) | copy-start | bytes 786436
  87.6 10.2 %copy-start.6 = (f32[2,6144]{1,0:T(2,128)}, f32[2,6144]{1,0:T(2,128)S(1)}, u32[]{:S(2)}) copy-start(f32[2,6144]{1,0:T(2,128)S(1)} %broadcast_add_fusion.emb_ref.refs_6_.refs_10_) | copy-start | bytes 147460
  87.6 2.9 copy-start
  97.8 1.0 copy-start.5
  98.8 25.5 %all-to-all-start = ((bf16[4,512,384]{2,1,0:T(8,128)(2,1)}), bf16[4,512,384]{2,1,0:T(8,128)(2,1)S(1)}, u32[]{:S(2)}, u32[]{:S(2)}) async-start(bf16[4,512,384]{2,1,0:T(8,128)(2,1)} %get-tuple-element.95), calls=%async_computation | async-start | bytes 3145728 | tf_op jit(solution)/shard_map/all_to_all | solution.py:832
  124.3 7.4 %copy-start.8 = (bf16[4,512,384]{2,1,0:T(8,128)(2,1)}, bf16[4,512,384]{2,1,0:T(8,128)(2,1)S(1)}, u32[]{:S(2)}) copy-start(bf16[4,512,384]{2,1,0:T(8,128)(2,1)S(1)} %all-to-all-done) | copy-start | bytes 4718596
  124.3 27.9 %all-to-all-start.1 = ((bf16[4,512,384]{2,1,0:T(8,128)(2,1)}), bf16[4,512,384]{2,1,0:T(8,128)(2,1)}, u32[]{:S(2)}, u32[]{:S(2)}) async-start(bf16[4,512,384]{2,1,0:T(8,128)(2,1)} %get-tuple-element.98), calls=%async_computation.1 | async-start | bytes 3145728 | tf_op jit(solution)/shard_map/all_to_all | solution.py:832
  128.6 275.5 %reduce-scatter.2.cloned.1.call-start = ((), (), s32[]{:S(2)}) async-start(), calls=%async_computation.5 | async-start | bytes 6488064 | tf_op jit(solution)/shard_map/reduce_scatter | solution.py:843
  254.7 37.2 %all-to-all-start.2 = ((bf16[4,512,384]{2,1,0:T(8,128)(2,1)}), bf16[4,512,384]{2,1,0:T(8,128)(2,1)}, u32[]{:S(2)}, u32[]{:S(2)}) async-start(bf16[4,512,384]{2,1,0:T(8,128)(2,1)} %bitcast.76), calls=%async_computation.2 | async-start | bytes 3145728 | tf_op jit(solution)/shard_map/all_to_all | solution.py:832
  396.4 12.8 %copy-start.9 = (bf16[512,1024]{1,0:T(8,128)(2,1)S(1)}, bf16[512,1024]{1,0:T(8,128)(2,1)}, u32[]{:S(2)}) copy-start(bf16[512,1024]{1,0:T(8,128)(2,1)} %get-tuple-element.100) | copy-start | bytes 3145732
  399.7 10.5 %copy-start.7 = (f32[512,1024]{1,0:T(8,128)S(1)}, f32[512,1024]{1,0:T(8,128)}, u32[]{:S(2)}) copy-start(f32[512,1024]{1,0:T(8,128)} %get-tuple-element.111) | copy-start | bytes 6291460
  410.2 1.7 copy-start.10
  410.2 2.6 copy-start.11
  411.9 1.6 copy-start.12
Sparse Core Ops, SparseCore 0:
  11.5 112.1 all-gather.1
  222.0 130.5 reduce-scatter.1
